TPU v7x, 128 devices: a whole 4x4x4 slice. The times are simulated.
128 devices in a mesh: pipe: 4 (over z), width: 32 (over y, x, core).
Axes of the slice: x: 4, y: 4, z: 4, core: 2. Of those that a mesh axis runs over, the one named last changes fastest.
Arguments:
- inputs: bfloat16 [6, 32, 16384], replicated, may hold values from -4 to 4
- in_blocks: bfloat16 [4, 128, 4, 8, 128, 128], P('pipe', 'width'), may hold values from -0.1875 to 0.1875
- rec_blocks: bfloat16 [4, 128, 4, 8, 128, 128], P('pipe', 'width'), may hold values from -0.1875 to 0.1875
- in_cols: int32 [4, 128, 4, 8], P('pipe', 'width'), may hold values from 0 to 127, as said below
- rec_cols: int32 [4, 128, 4, 8], P('pipe', 'width'), may hold values from 0 to 127, as said below
- bias: float32 [4, 4, 16384], P('pipe', None, 'width'), may hold values from -1 to 1
Outputs:
- hidden_seq: bfloat16 [4, 6, 32, 16384], P('pipe', None, None, 'width')
- cells: float32 [4, 32, 16384], P('pipe', None, 'width')
Inputs may be any that keep to these rules, and one draw needn't show every extreme that they name: Each in_cols[l, j, g] holds 8 different hidden block numbers. Each rec_cols[l, j, g] holds 8 different hidden block numbers.
All inputs are finite; a program needn't handle non-finite values.
Results may differ from a plain program's by a relative error of at most 0.0033.
Values may be sent and summed in bfloat16 or wider, within the bound.
No kernel may reach another device: no remote copies, remote signals or barrier semaphores. Data moves between devices by JAX's collectives and lax.ppermute only.
A program may use at most 64 MiB of HBM per device.

v0:
```python
import jax
import jax.numpy as jnp
from jax import lax
from jax.sharding import PartitionSpec as P


def passed_along(block, axis, distance):
    devices = range(lax.axis_size(axis))
    route = [(i - distance, i) for i in devices if i - distance in devices]
    return lax.ppermute(block, axis, route)


def activate(gate_sums, cell_before, local_units):
    row_count = gate_sums.shape[0]
    input_gate = jax.nn.sigmoid(gate_sums[:, :, 0]).reshape(row_count, local_units)
    forget_gate = jax.nn.sigmoid(gate_sums[:, :, 1]).reshape(row_count, local_units)
    cell_input = jnp.tanh(gate_sums[:, :, 2]).reshape(row_count, local_units)
    output_gate = jax.nn.sigmoid(gate_sums[:, :, 3]).reshape(row_count, local_units)
    new_cell = forget_gate * cell_before + input_gate * cell_input
    return (new_cell, (output_gate * jnp.tanh(new_cell)).astype(jnp.bfloat16))


def body(inputs, in_blocks, rec_blocks, in_cols, rec_cols, bias):
    section_count = lax.axis_size("pipe")
    my_section = lax.axis_index("pipe")
    my_column = lax.axis_index("width")
    step_count, row_count, hidden = inputs.shape
    blocks_dev = in_blocks.shape[1]
    kept_blocks = in_blocks.shape[3]
    block_edge = in_blocks.shape[4]
    total_blocks = hidden // block_edge
    local_units = blocks_dev * block_edge
    weights = jnp.concatenate([in_blocks[0], rec_blocks[0]], axis=2)
    block_index = jnp.concatenate([in_cols[0], rec_cols[0] + total_blocks], axis=2).reshape(-1)
    offsets = bias[0].reshape(4, blocks_dev, block_edge).transpose(1, 0, 2)
    micro_count = 1
    part_rows = row_count // micro_count
    item_count = step_count * micro_count
    tick_count = item_count + section_count - 1

    def tick_body(tick_index, carried):
        last_output, history, cell_history, sequence = carried
        position = tick_index - my_section
        is_valid = (position >= 0) & (position < item_count)
        clipped = jnp.clip(position, 0, item_count - 1)
        member = clipped % micro_count
        step_now = clipped // micro_count
        prev_valid = (position >= 1) & (position <= item_count)
        prev_slot = jnp.clip(position - 1, 0, item_count - 1) % micro_count
        gathered = lax.all_gather(last_output, "width", axis=1, tiled=True)
        history = history.at[prev_slot].set(jnp.where(prev_valid, gathered, history[prev_slot]))
        recurrent = history[member]
        row_start = member * part_rows
        fresh_rows = lax.dynamic_slice(
            inputs, (step_now, row_start, jnp.int32(0)), (1, part_rows, hidden)
        )[0]
        lower_rows = passed_along(last_output, "pipe", 1)
        own_slice = lax.dynamic_slice_in_dim(fresh_rows, my_column * local_units, local_units, 1)
        shard_in = jnp.where(my_section == 0, own_slice, lower_rows)
        lower_full = lax.all_gather(shard_in, "width", axis=1, tiled=True)
        stacked = jnp.concatenate([lower_full, recurrent], axis=1).reshape(
            part_rows, 2 * total_blocks, block_edge
        )
        picked = jnp.take(stacked, block_index, axis=1).reshape(
            part_rows, blocks_dev, 4, 2 * kept_blocks, block_edge
        )
        gate_sums = (
            jnp.einsum("rjgka,jgkab->rjgb", picked, weights, preferred_element_type=jnp.float32)
            + offsets
        )
        new_cell, output = activate(gate_sums, cell_history[member], local_units)
        cell_history = cell_history.at[member].set(
            jnp.where(is_valid, new_cell, cell_history[member])
        )
        previous = lax.dynamic_slice(
            sequence, (step_now, row_start, jnp.int32(0)), (1, part_rows, local_units)
        )
        updated = jnp.where(is_valid, output[None], previous)
        sequence = lax.dynamic_update_slice(sequence, updated, (step_now, row_start, jnp.int32(0)))
        return (output, history, cell_history, sequence)

    start_state = (
        jnp.zeros((part_rows, local_units), jnp.bfloat16),
        jnp.zeros((micro_count, part_rows, hidden), jnp.bfloat16),
        jnp.zeros((micro_count, part_rows, local_units), jnp.float32),
        jnp.zeros((step_count, row_count, local_units), jnp.bfloat16),
    )
    last_output, history, cell_history, sequence = lax.fori_loop(
        0, tick_count, tick_body, start_state
    )
    return (sequence[None], cell_history.reshape(row_count, local_units)[None])


def solution(mesh):
    return jax.shard_map(
        body,
        mesh=mesh,
        in_specs=(
            P(),
            P("pipe", "width", None, None, None, None),
            P("pipe", "width", None, None, None, None),
            P("pipe", "width", None, None),
            P("pipe", "width", None, None),
            P("pipe", None, "width"),
        ),
        out_specs=(P("pipe", None, None, "width"), P("pipe", None, "width")),
        check_vma=False,
    )
```

profile of v0, /device:TPU:1, one launch (start us, length us, event | category | flops | bytes accessed | tf_op | source)
XLA Modules:
  0.0 936.7 jit_solution(10159353955262184727)
XLA Ops:
  7.2 7.4 pad_maximum_fusion.1
  14.9 914.2 %while.25 = (s32[]{:T(128)}, bf16[32,512]{1,0:T(8,128)(2,1)S(1)}, bf16[1,32,16384]{2,1,0:T(8,128)(2,1)S(1)}, f32[1,32,512]{2,1,0:T(8,128)S(1)}, bf16[6,32,512]{2...) while((s32[]{:T(128)}, bf16[32,512]{1,0:T(8,128)(2,1)S(1)}, ...), condition=%wide.region_1.2_spmd.clone, body=%wide.region_0.1_spmd.clone.sunk | while | flops 271568128 | bytes 36458376 | solution.py:88
  15.7 4.4 collective-permute-start
  22.9 42.1 %all-gather.3.cloned.1.call-done = bf16[32,16384]{1,0:T(8,128)(2,1)} async-done(((bf16[32,512]{1,0:T(8,128)(2,1)}), bf16[32,16384]{1,0:T(8,128)(2,1)}) %all-gather.3.cloned.1.call-update) | async-done | bytes 1048592 | tf_op jit(solution)/shard_map/while/body/eval_jaxpr/all_gather | solution.py:50
  65.6 44.4 %all-gather.5.cloned.1.call-done = bf16[32,16384]{1,0:T(8,128)(2,1)} async-done(((bf16[32,512]{1,0:T(8,128)(2,1)}), bf16[32,16384]{1,0:T(8,128)(2,1)}) %all-gather.5.cloned.1.call-update) | async-done | bytes 1048592 | tf_op jit(solution)/shard_map/while/body/eval_jaxpr/all_gather | solution.py:60
  115.6 4.3 fusion.46
  121.3 3.2 collective-permute-start
  127.3 39.1 %all-gather.3.cloned.1.call-done = bf16[32,16384]{1,0:T(8,128)(2,1)} async-done(((bf16[32,512]{1,0:T(8,128)(2,1)}), bf16[32,16384]{1,0:T(8,128)(2,1)}) %all-gather.3.cloned.1.call-update) | async-done | bytes 1048592 | tf_op jit(solution)/shard_map/while/body/eval_jaxpr/all_gather | solution.py:50
  168.2 43.1 %all-gather.5.cloned.1.call-done = bf16[32,16384]{1,0:T(8,128)(2,1)} async-done(((bf16[32,512]{1,0:T(8,128)(2,1)}), bf16[32,16384]{1,0:T(8,128)(2,1)}) %all-gather.5.cloned.1.call-update) | async-done | bytes 1048592 | tf_op jit(solution)/shard_map/while/body/eval_jaxpr/all_gather | solution.py:60
  216.8 4.3 fusion.46
  228.4 38.8 %all-gather.3.cloned.1.call-done = bf16[32,16384]{1,0:T(8,128)(2,1)} async-done(((bf16[32,512]{1,0:T(8,128)(2,1)}), bf16[32,16384]{1,0:T(8,128)(2,1)}) %all-gather.3.cloned.1.call-update) | async-done | bytes 1048592 | tf_op jit(solution)/shard_map/while/body/eval_jaxpr/all_gather | solution.py:50
  269.0 43.1 %all-gather.5.cloned.1.call-done = bf16[32,16384]{1,0:T(8,128)(2,1)} async-done(((bf16[32,512]{1,0:T(8,128)(2,1)}), bf16[32,16384]{1,0:T(8,128)(2,1)}) %all-gather.5.cloned.1.call-update) | async-done | bytes 1048592 | tf_op jit(solution)/shard_map/while/body/eval_jaxpr/all_gather | solution.py:60
  317.7 4.3 fusion.46
  323.3 3.2 collective-permute-start
  329.3 39.1 %all-gather.3.cloned.1.call-done = bf16[32,16384]{1,0:T(8,128)(2,1)} async-done(((bf16[32,512]{1,0:T(8,128)(2,1)}), bf16[32,16384]{1,0:T(8,128)(2,1)}) %all-gather.3.cloned.1.call-update) | async-done | bytes 1048592 | tf_op jit(solution)/shard_map/while/body/eval_jaxpr/all_gather | solution.py:50
  370.2 43.2 %all-gather.5.cloned.1.call-done = bf16[32,16384]{1,0:T(8,128)(2,1)} async-done(((bf16[32,512]{1,0:T(8,128)(2,1)}), bf16[32,16384]{1,0:T(8,128)(2,1)}) %all-gather.5.cloned.1.call-update) | async-done | bytes 1048592 | tf_op jit(solution)/shard_map/while/body/eval_jaxpr/all_gather | solution.py:60
  419.0 4.3 fusion.46
  430.6 39.1 %all-gather.3.cloned.1.call-done = bf16[32,16384]{1,0:T(8,128)(2,1)} async-done(((bf16[32,512]{1,0:T(8,128)(2,1)}), bf16[32,16384]{1,0:T(8,128)(2,1)}) %all-gather.3.cloned.1.call-update) | async-done | bytes 1048592 | tf_op jit(solution)/shard_map/while/body/eval_jaxpr/all_gather | solution.py:50
  471.5 43.1 %all-gather.5.cloned.1.call-done = bf16[32,16384]{1,0:T(8,128)(2,1)} async-done(((bf16[32,512]{1,0:T(8,128)(2,1)}), bf16[32,16384]{1,0:T(8,128)(2,1)}) %all-gather.5.cloned.1.call-update) | async-done | bytes 1048592 | tf_op jit(solution)/shard_map/while/body/eval_jaxpr/all_gather | solution.py:60
  520.2 4.3 fusion.46
  531.8 39.1 %all-gather.3.cloned.1.call-done = bf16[32,16384]{1,0:T(8,128)(2,1)} async-done(((bf16[32,512]{1,0:T(8,128)(2,1)}), bf16[32,16384]{1,0:T(8,128)(2,1)}) %all-gather.3.cloned.1.call-update) | async-done | bytes 1048592 | tf_op jit(solution)/shard_map/while/body/eval_jaxpr/all_gather | solution.py:50
  572.7 43.1 %all-gather.5.cloned.1.call-done = bf16[32,16384]{1,0:T(8,128)(2,1)} async-done(((bf16[32,512]{1,0:T(8,128)(2,1)}), bf16[32,16384]{1,0:T(8,128)(2,1)}) %all-gather.5.cloned.1.call-update) | async-done | bytes 1048592 | tf_op jit(solution)/shard_map/while/body/eval_jaxpr/all_gather | solution.py:60
  621.3 4.3 fusion.46
  633.0 39.1 %all-gather.3.cloned.1.call-done = bf16[32,16384]{1,0:T(8,128)(2,1)} async-done(((bf16[32,512]{1,0:T(8,128)(2,1)}), bf16[32,16384]{1,0:T(8,128)(2,1)}) %all-gather.3.cloned.1.call-update) | async-done | bytes 1048592 | tf_op jit(solution)/shard_map/while/body/eval_jaxpr/all_gather | solution.py:50
  673.9 43.1 %all-gather.5.cloned.1.call-done = bf16[32,16384]{1,0:T(8,128)(2,1)} async-done(((bf16[32,512]{1,0:T(8,128)(2,1)}), bf16[32,16384]{1,0:T(8,128)(2,1)}) %all-gather.5.cloned.1.call-update) | async-done | bytes 1048592 | tf_op jit(solution)/shard_map/while/body/eval_jaxpr/all_gather | solution.py:60
  722.5 4.3 fusion.46
  734.1 38.8 %all-gather.3.cloned.1.call-done = bf16[32,16384]{1,0:T(8,128)(2,1)} async-done(((bf16[32,512]{1,0:T(8,128)(2,1)}), bf16[32,16384]{1,0:T(8,128)(2,1)}) %all-gather.3.cloned.1.call-update) | async-done | bytes 1048592 | tf_op jit(solution)/shard_map/while/body/eval_jaxpr/all_gather | solution.py:50
  773.5 44.3 %all-gather.5.cloned.1.call-done = bf16[32,16384]{1,0:T(8,128)(2,1)} async-done(((bf16[32,512]{1,0:T(8,128)(2,1)}), bf16[32,16384]{1,0:T(8,128)(2,1)}) %all-gather.5.cloned.1.call-update) | async-done | bytes 1048592 | tf_op jit(solution)/shard_map/while/body/eval_jaxpr/all_gather | solution.py:60
  823.4 4.3 fusion.46
  835.0 38.8 %all-gather.3.cloned.1.call-done = bf16[32,16384]{1,0:T(8,128)(2,1)} async-done(((bf16[32,512]{1,0:T(8,128)(2,1)}), bf16[32,16384]{1,0:T(8,128)(2,1)}) %all-gather.3.cloned.1.call-update) | async-done | bytes 1048592 | tf_op jit(solution)/shard_map/while/body/eval_jaxpr/all_gather | solution.py:50
  874.4 44.3 %all-gather.5.cloned.1.call-done = bf16[32,16384]{1,0:T(8,128)(2,1)} async-done(((bf16[32,512]{1,0:T(8,128)(2,1)}), bf16[32,16384]{1,0:T(8,128)(2,1)}) %all-gather.5.cloned.1.call-update) | async-done | bytes 1048592 | tf_op jit(solution)/shard_map/while/body/eval_jaxpr/all_gather | solution.py:60
  924.3 4.3 fusion.46
  (257 shorter events, 118.3 us)
Async XLA Ops:
  7.2 7.5 copy-start.4
  7.2 7.5 copy-start.3
  7.2 7.7 copy-start.2
  14.9 50.1 %all-gather.3.cloned.1.call-start = ((), (), s32[]{:S(2)}) async-start(), calls=%async_computation | async-start | bytes 1081344 | tf_op jit(solution)/shard_map/while/body/eval_jaxpr/all_gather | solution.py:50
  15.7 94.4 %all-gather.5.cloned.1.call-start = ((), (), s32[]{:S(2)}) async-start(), calls=%async_computation.1 | async-start | bytes 1081344 | tf_op jit(solution)/shard_map/while/body/eval_jaxpr/all_gather | solution.py:60
  15.7 5.7 collective-permute-start
  120.5 45.9 %all-gather.3.cloned.1.call-start = ((), (), s32[]{:S(2)}) async-start(), calls=%async_computation | async-start | bytes 1081344 | tf_op jit(solution)/shard_map/while/body/eval_jaxpr/all_gather | solution.py:50
  121.2 90.0 %all-gather.5.cloned.1.call-start = ((), (), s32[]{:S(2)}) async-start(), calls=%async_computation.1 | async-start | bytes 1081344 | tf_op jit(solution)/shard_map/while/body/eval_jaxpr/all_gather | solution.py:60
  121.3 4.5 collective-permute-start
  221.7 45.6 %all-gather.3.cloned.1.call-start = ((), (), s32[]{:S(2)}) async-start(), calls=%async_computation | async-start | bytes 1081344 | tf_op jit(solution)/shard_map/while/body/eval_jaxpr/all_gather | solution.py:50
  222.4 89.7 %all-gather.5.cloned.1.call-start = ((), (), s32[]{:S(2)}) async-start(), calls=%async_computation.1 | async-start | bytes 1081344 | tf_op jit(solution)/shard_map/while/body/eval_jaxpr/all_gather | solution.py:60
  222.4 4.5 collective-permute-start
  322.5 45.9 %all-gather.3.cloned.1.call-start = ((), (), s32[]{:S(2)}) async-start(), calls=%async_computation | async-start | bytes 1081344 | tf_op jit(solution)/shard_map/while/body/eval_jaxpr/all_gather | solution.py:50
  323.3 90.2 %all-gather.5.cloned.1.call-start = ((), (), s32[]{:S(2)}) async-start(), calls=%async_computation.1 | async-start | bytes 1081344 | tf_op jit(solution)/shard_map/while/body/eval_jaxpr/all_gather | solution.py:60
  323.3 4.5 collective-permute-start
  423.9 45.9 %all-gather.3.cloned.1.call-start = ((), (), s32[]{:S(2)}) async-start(), calls=%async_computation | async-start | bytes 1081344 | tf_op jit(solution)/shard_map/while/body/eval_jaxpr/all_gather | solution.py:50
  424.6 90.0 %all-gather.5.cloned.1.call-start = ((), (), s32[]{:S(2)}) async-start(), calls=%async_computation.1 | async-start | bytes 1081344 | tf_op jit(solution)/shard_map/while/body/eval_jaxpr/all_gather | solution.py:60
  424.6 4.5 collective-permute-start
  525.0 45.9 %all-gather.3.cloned.1.call-start = ((), (), s32[]{:S(2)}) async-start(), calls=%async_computation | async-start | bytes 1081344 | tf_op jit(solution)/shard_map/while/body/eval_jaxpr/all_gather | solution.py:50
  525.8 90.0 %all-gather.5.cloned.1.call-start = ((), (), s32[]{:S(2)}) async-start(), calls=%async_computation.1 | async-start | bytes 1081344 | tf_op jit(solution)/shard_map/while/body/eval_jaxpr/all_gather | solution.py:60
  525.8 4.5 collective-permute-start
  626.2 45.9 %all-gather.3.cloned.1.call-start = ((), (), s32[]{:S(2)}) async-start(), calls=%async_computation | async-start | bytes 1081344 | tf_op jit(solution)/shard_map/while/body/eval_jaxpr/all_gather | solution.py:50
  627.0 90.0 %all-gather.5.cloned.1.call-start = ((), (), s32[]{:S(2)}) async-start(), calls=%async_computation.1 | async-start | bytes 1081344 | tf_op jit(solution)/shard_map/while/body/eval_jaxpr/all_gather | solution.py:60
  627.0 4.5 collective-permute-start
  727.4 45.6 %all-gather.3.cloned.1.call-start = ((), (), s32[]{:S(2)}) async-start(), calls=%async_computation | async-start | bytes 1081344 | tf_op jit(solution)/shard_map/while/body/eval_jaxpr/all_gather | solution.py:50
  728.1 89.7 %all-gather.5.cloned.1.call-start = ((), (), s32[]{:S(2)}) async-start(), calls=%async_computation.1 | async-start | bytes 1081344 | tf_op jit(solution)/shard_map/while/body/eval_jaxpr/all_gather | solution.py:60
  728.1 4.5 collective-permute-start
  828.3 45.6 %all-gather.3.cloned.1.call-start = ((), (), s32[]{:S(2)}) async-start(), calls=%async_computation | async-start | bytes 1081344 | tf_op jit(solution)/shard_map/while/body/eval_jaxpr/all_gather | solution.py:50
  829.0 89.7 %all-gather.5.cloned.1.call-start = ((), (), s32[]{:S(2)}) async-start(), calls=%async_computation.1 | async-start | bytes 1081344 | tf_op jit(solution)/shard_map/while/body/eval_jaxpr/all_gather | solution.py:60
  829.0 4.5 collective-permute-start
  929.1 0.6 copy-start
  929.1 0.7 copy-start.1
Sparse Core Ops, SparseCore 0:
  18.5 46.4 all-gather.2
  67.8 42.2 all-gather.4
  124.1 42.2 all-gather.2
  169.0 42.2 all-gather.4
  224.9 42.2 all-gather.2
  269.8 42.2 all-gather.4
  326.1 42.2 all-gather.2
  371.2 42.2 all-gather.4
  427.4 42.2 all-gather.2
  472.3 42.2 all-gather.4
  528.6 42.2 all-gather.2
  573.5 42.2 all-gather.4
  629.8 42.2 all-gather.2
  674.7 42.2 all-gather.4
  730.7 42.2 all-gather.2
  775.6 42.2 all-gather.4
  831.5 42.2 all-gather.2
  876.4 42.2 all-gather.4
where the time goes:
time: 938 us; the launch traced here: 937 us
  waiting for transfers between devices  757 us (81%)
  other arithmetic  53.1 us (6%)
  local copies, waits for them, and re-layouts  41.6 us (4%)
  matrix products  39 us (4%)
  starting transfers between devices  30.5 us (3%)
  between operations  14.1 us (2%)
    all_gather x9, waiting for transfers between devices, tick_body(): lower_full = lax.all_gather(shard_in, 'width', axis=1, tiled=True)  391 us
    all_gather x9, waiting for transfers between devices, tick_body(): gathered = lax.all_gather(last_output, 'width', axis=1, tiled=True)  354 us
    dot_general x9, matrix products, tick_body(): jnp.einsum('rjgka,jgkab->rjgb', picked, weights, preferred_element_type=j...  39 us
    ppermute x9, starting transfers between devices, passed_along(): return lax.ppermute(block, axis, route)  29.8 us
    gather x9, local copies, waits for them, and re-layouts, tick_body(): jnp.take(stacked, block_index, axis=1)  23.2 us
  transfers between devices with their start and end apart: 27, of which 27 were waited for; matrix products, arithmetic and copies ran while one was open for 3% of the time, Pallas kernels for 0%

commit v1 on v0

v1 whole, which is shorter than its diff:
```python
import functools

import jax
import jax.numpy as jnp
from jax import lax
from jax.experimental import pallas as pl
from jax.experimental.pallas import tpu as pltpu
from jax.sharding import Mesh
from jax.sharding import PartitionSpec as P

LAG = 2
F32 = jnp.float32
BF16 = jnp.bfloat16
WIDTH = ("y", "x", "core")


def row_sums(index_ref, x_ref, w_ref, row):
    blocks = w_ref.shape[1]
    edge = w_ref.shape[2]
    picked = jnp.concatenate([x_ref[index_ref[row * blocks + k]] for k in range(blocks)], axis=1)
    return jnp.dot(picked, w_ref[row].reshape(blocks * edge, edge), preferred_element_type=F32)


def input_kernel(index_ref, x_ref, w_ref, bias_ref, out_ref):
    for row in range(w_ref.shape[0]):
        out_ref[row] = row_sums(index_ref, x_ref, w_ref, row) + bias_ref[row]


def state_kernel(step_count, index_ref, step_ref, h_ref, w_ref, partial_ref, cell_ref, cell_out, rows_out, send_out):
    step = step_ref[0]
    started = step >= 0
    running = started & (step < step_count)
    edge = h_ref.shape[2]
    for j in range(cell_ref.shape[0]):
        sums = [
            partial_ref[4 * j + g] + row_sums(index_ref, h_ref, w_ref, 4 * j + g) for g in range(4)
        ]
        before = cell_ref[j]
        cell = jax.nn.sigmoid(sums[1]) * before + jax.nn.sigmoid(sums[0]) * jnp.tanh(sums[2])
        output = jax.nn.sigmoid(sums[3]) * jnp.tanh(cell)
        output = jnp.where(started, output, 0.0).astype(BF16)
        cell_out[j] = jnp.where(running, cell, before)
        rows_out[:, j * edge:(j + 1) * edge] = output
        for peer in range(send_out.shape[0]):
            send_out[peer, j] = output


def vmem():
    return pl.BlockSpec(memory_space=pltpu.VMEM)


def smem():
    return pl.BlockSpec(memory_space=pltpu.SMEM)


def input_sums(index, x, w, bias):
    rows = w.shape[0]
    return pl.pallas_call(
        input_kernel,
        out_shape=jax.ShapeDtypeStruct((rows, x.shape[1], x.shape[2]), F32),
        in_specs=[smem(), vmem(), vmem(), vmem()],
        out_specs=vmem(),
        compiler_params=pltpu.CompilerParams(vmem_limit_bytes=24 * 2**20),
        cost_estimate=pl.CostEstimate(flops=2 * w.size * 32, bytes_accessed=2 * w.size, transcendentals=0),
        name="input_sums",
    )(index, x, w, bias)


def state_step(index, step, h, w, partial, cell, step_count, peers):
    per_device, row_count, edge = cell.shape
    return pl.pallas_call(
        functools.partial(state_kernel, step_count),
        out_shape=(
            jax.ShapeDtypeStruct(cell.shape, F32),
            jax.ShapeDtypeStruct((row_count, per_device * edge), BF16),
            jax.ShapeDtypeStruct((peers, per_device, row_count, edge), BF16),
        ),
        in_specs=[smem(), smem(), vmem(), vmem(), vmem(), vmem()],
        out_specs=(vmem(), vmem(), vmem()),
        compiler_params=pltpu.CompilerParams(vmem_limit_bytes=24 * 2**20),
        cost_estimate=pl.CostEstimate(flops=2 * w.size * 32, bytes_accessed=2 * w.size, transcendentals=0),
        name="state_step",
    )(index, step, h, w, partial, cell)


def other_core(x):
    return lax.ppermute(x, "core", [(0, 1), (1, 0)])


def body(inputs, in_blocks, rec_blocks, in_cols, rec_cols, bias):
    layer = lax.axis_index("pipe")
    layers = lax.axis_size("pipe")
    core = lax.axis_index("core")
    chips = lax.axis_size("y") * lax.axis_size("x")
    step_count, row_count, hidden = inputs.shape
    _, per_device, gates, kept, edge, _ = in_blocks.shape
    total = hidden // edge
    half = total // 2
    rows = per_device * gates
    w_in = in_blocks.reshape(rows, kept, edge, edge)
    w_rec = rec_blocks.reshape(rows, kept, edge, edge)

    def place(cols):
        device = cols // per_device
        return ((device % 2) ^ core) * half + (device // 2) * per_device + cols % per_device

    in_flat = in_cols.reshape(-1)
    in_index = jnp.where(layer == 0, in_flat, place(in_flat))
    rec_index = place(rec_cols.reshape(-1))
    offsets = bias[0].reshape(gates, per_device, edge).transpose(1, 0, 2).reshape(rows, 1, edge)
    offsets = jnp.broadcast_to(offsets, (rows, 8, edge))[:, :1]

    tick_count = step_count + LAG * (layers - 1)
    up = [(i, i + 1) for i in range(layers - 1)]
    state = jnp.zeros((total, row_count, edge), BF16)
    cell = jnp.zeros((per_device, row_count, edge), F32)
    arrived = {}
    outputs = []
    for tick in range(tick_count):
        fresh = None
        if tick < step_count:
            fresh = inputs[tick].reshape(row_count, total, edge).transpose(1, 0, 2)
        if tick >= LAG:
            lower = arrived[tick - LAG]
            lower = jnp.concatenate([lower, other_core(lower)], axis=0)
            x = lower if fresh is None else jnp.where(layer == 0, fresh, lower)
        else:
            x = fresh
        partial = input_sums(in_index, x, w_in, offsets)
        step = (tick - LAG * layer).astype(jnp.int32).reshape(1)
        cell, out_rows, send = state_step(rec_index, step, state, w_rec, partial, cell, step_count, chips)
        outputs.append(out_rows)
        if tick < tick_count - 1:
            mine = lax.all_to_all(send, ("y", "x"), 0, 0).reshape(half, row_count, edge)
            if tick < tick_count - LAG:
                arrived[tick] = lax.ppermute(mine, "pipe", up)
            state = jnp.concatenate([mine, other_core(mine)], axis=0)
    sequence = lax.dynamic_slice_in_dim(jnp.stack(outputs), LAG * layer, step_count, 0)
    cells = cell.transpose(1, 0, 2).reshape(row_count, per_device * edge)
    return sequence[None], cells[None]


def solution(mesh):
    layers, width = mesh.devices.shape
    grid = Mesh(mesh.devices.reshape(layers, 4, width // 8, 2), ("pipe",) + WIDTH)
    return jax.shard_map(
        body,
        mesh=grid,
        in_specs=(
            P(),
            P("pipe", WIDTH, None, None, None, None),
            P("pipe", WIDTH, None, None, None, None),
            P("pipe", WIDTH, None, None),
            P("pipe", WIDTH, None, None),
            P("pipe", None, WIDTH),
        ),
        out_specs=(P("pipe", None, None, WIDTH), P("pipe", None, WIDTH)),
        check_vma=False,
    )
```

time: 938 us -> 308 us (0.33)
  waiting for transfers between devices: 757 us -> 105 us
  starting transfers between devices: 30.5 us -> 84.2 us
  matrix products: 39 us -> 0 us
  blocking collectives: 0 us -> 18 us
  Pallas kernels: 0 us -> 16.7 us
  other arithmetic: 53.1 us -> 39.4 us
  between operations: 14.1 us -> 1.46 us
    all_gather x18 -> x0, waiting for transfers between devices: 745 us -> none  [the longest x9 391 us: tick_body(): lower_full = lax.all_gather(shard_in, 'width', axis=1, tiled=True)]
    all_to_all x0 -> x10, waiting for transfers between devices: none -> 97.1 us  [body(): mine = lax.all_to_all(send, ('y', 'x'), 0, 0).reshape(half, row_count, edge)]
    dot_general x9 -> x0, matrix products: 39 us -> none  [tick_body(): jnp.einsum('rjgka,jgkab->rjgb', picked, weights, preferred_element_type=j...]
    all_to_all x0 -> x10, starting transfers between devices: none -> 37.7 us  [body(): mine = lax.all_to_all(send, ('y', 'x'), 0, 0).reshape(half, row_count, edge)]
    unnamed x10 -> x66, local copies, waits for them, and re-layouts: 0.7 us -> 37.1 us
    pallas_call x0 -> x11, other arithmetic: none -> 23.9 us  [state_step(): pl.pallas_call(functools.partial(state_kernel, step_count), out_shape=(ja...]
    gather x9 -> x0, local copies, waits for them, and re-layouts: 23.2 us -> none  [tick_body(): jnp.take(stacked, block_index, axis=1)]
    all_to_all x0 -> x1, blocking collectives: none -> 18 us  [body(): mine = lax.all_to_all(send, ('y', 'x'), 0, 0).reshape(half, row_count, edge)]
  transfers between devices with their start and end apart: 27 -> 41, of which waited for: 27 -> 16; matrix products, arithmetic and copies ran while one was open for 3% -> 13% of each run, Pallas kernels for 0% -> 5%
where the time goes in v1:
time: 308 us; the launch traced here: 306 us
  waiting for transfers between devices  105 us (34%)
  starting transfers between devices  84.2 us (27%)
  local copies, waits for them, and re-layouts  41.6 us (14%)
  other arithmetic  39.4 us (13%)
  blocking collectives  18 us (6%)
  Pallas kernels  16.7 us (5%)
    all_to_all x10, waiting for transfers between devices, body(): mine = lax.all_to_all(send, ('y', 'x'), 0, 0).reshape(half, row_count, edge)  97.1 us
    all_to_all x10, starting transfers between devices, body(): mine = lax.all_to_all(send, ('y', 'x'), 0, 0).reshape(half, row_count, edge)  37.7 us
    unnamed x66, local copies, waits for them, and re-layouts  37.1 us
    ppermute x10, starting transfers between devices, body(): arrived[tick] = lax.ppermute(mine, 'pipe', up)  24.5 us
    pallas_call x11, other arithmetic, state_step(): pl.pallas_call(functools.partial(state_kernel, step_count), out_shape=(ja...  23.9 us
    ppermute x21, starting transfers between devices, other_core(): return lax.ppermute(x, 'core', [(0, 1), (1, 0)])  22 us
    all_to_all x1, blocking collectives, body(): mine = lax.all_to_all(send, ('y', 'x'), 0, 0).reshape(half, row_count, edge)  18 us
    pallas_call x12, Pallas kernels, input_sums(): pl.pallas_call(input_kernel, out_shape=jax.ShapeDtypeStruct((rows, x.shap...  15.4 us
  transfers between devices with their start and end apart: 41, of which 16 were waited for; matrix products, arithmetic and copies ran while one was open for 13% of the time, Pallas kernels for 5%

profile of v1, /device:TPU:1, one launch (start us, length us, event | category | flops | bytes accessed | tf_op | source)
XLA Modules:
  0.0 306.0 jit_solution(15423886628626817678)
XLA Ops:
  2.2 4.6 %slice_bitcast_fusion = (bf16[4,8,128,128]{3,1,2,0:T(8,128)(2,1)S(1)}, bf16[4,8,128,128]{3,1,2,0:T(8,128)(2,1)}, bf16[4,8,128,128]{3,1,2,0:T(8,128)(2,1)}, bf16[...) fusion(bf16[6,32,16384]{2,1,0:T(8,128)(2,1)} %param.6), kind=kLoop, calls=%fused_computation.23 | loop fusion | bytes 12582912
  13.6 18.0 %all_to_all.55 = bf16[16,4,32,128]{3,2,1,0:T(8,128)(2,1)} all-to-all(bf16[16,4,32,128]{3,2,1,0:T(8,128)(2,1)S(1)} %get-tuple-element.38), channel_id=1, replica_groups=mesh['pipe'=4,'y'=4,'x'=4,'core'=2] {'y','x'}, dimensions={0} | all-to-all | bytes 1048576 | tf_op jit(solution)/shard_map/all_to_all | solution.py:134
  38.0 4.3 %collective-permute-start.2 = (bf16[64,32,128]{2,1,0:T(8,128)(2,1)}, bf16[64,32,128]{2,1,0:T(8,128)(2,1)}, u32[]{:S(2)}, u32[]{:S(2)}) collective-permute-start(bf16[64,32,128]{2,1,0:T(8,128)(2,1)} %bitcast.9), channel_id=1, source_target_pairs={{0,32},{32,64},{64,96},{1,33},{33,65},{65,97},{2,34},{34,66},{66,9... | collective-permute-start | bytes 1572872 | tf_op jit(solution)/shard_map/ppermute | solution.py:136
  44.3 2.2 state_step.23
  46.5 4.2 %all-to-all-start.1 = ((bf16[16,4,32,128]{3,2,1,0:T(8,128)(2,1)}), bf16[16,4,32,128]{3,2,1,0:T(8,128)(2,1)}, u32[]{:S(2)}, u32[]{:S(2)}) async-start(bf16[16,4,32,128]{3,2,1,0:T(8,128)(2,1)} %get-tuple-element.93), calls=%async_computation.1 | async-start | bytes 1048576 | tf_op jit(solution)/shard_map/all_to_all | solution.py:134
  50.7 2.4 collective-permute-done.2
  53.9 7.9 %all-to-all-done.1 = bf16[16,4,32,128]{3,2,1,0:T(8,128)(2,1)} async-done(((bf16[16,4,32,128]{3,2,1,0:T(8,128)(2,1)}), bf16[16,4,32,128]{3,2,1,0:T(8,128)(2,1)}, u32[]{:S(2)}, u32[]{:S(2)}) %all-to-all-start.1) | async-done | bytes 524320 | tf_op jit(solution)/shard_map/all_to_all | solution.py:134
  63.5 3.8 %collective-permute-start.5 = (bf16[64,32,128]{2,1,0:T(8,128)(2,1)}, bf16[64,32,128]{2,1,0:T(8,128)(2,1)}, u32[]{:S(2)}, u32[]{:S(2)}) collective-permute-start(bf16[64,32,128]{2,1,0:T(8,128)(2,1)} %bitcast.15), channel_id=1, source_target_pairs={{0,32},{32,64},{64,96},{1,33},{33,65},{65,97},{2,34},{34,66},{66,9... | collective-permute-start | bytes 1572872 | tf_op jit(solution)/shard_map/ppermute | solution.py:136
  74.1 4.2 %all-to-all-start.2 = ((bf16[16,4,32,128]{3,2,1,0:T(8,128)(2,1)}), bf16[16,4,32,128]{3,2,1,0:T(8,128)(2,1)}, u32[]{:S(2)}, u32[]{:S(2)}) async-start(bf16[16,4,32,128]{3,2,1,0:T(8,128)(2,1)} %get-tuple-element.99), calls=%async_computation.2 | async-start | bytes 1048576 | tf_op jit(solution)/shard_map/all_to_all | solution.py:134
  78.9 10.5 %all-to-all-done.2 = bf16[16,4,32,128]{3,2,1,0:T(8,128)(2,1)} async-done(((bf16[16,4,32,128]{3,2,1,0:T(8,128)(2,1)}), bf16[16,4,32,128]{3,2,1,0:T(8,128)(2,1)}, u32[]{:S(2)}, u32[]{:S(2)}) %all-to-all-start.2) | async-done | bytes 524320 | tf_op jit(solution)/shard_map/all_to_all | solution.py:134
  92.1 3.3 %collective-permute-start.8 = (bf16[64,32,128]{2,1,0:T(8,128)(2,1)}, bf16[64,32,128]{2,1,0:T(8,128)(2,1)}, u32[]{:S(2)}, u32[]{:S(2)}) collective-permute-start(bf16[64,32,128]{2,1,0:T(8,128)(2,1)} %bitcast.19), channel_id=1, source_target_pairs={{0,32},{32,64},{64,96},{1,33},{33,65},{65,97},{2,34},{34,66},{66,9... | collective-permute-start | bytes 1572872 | tf_op jit(solution)/shard_map/ppermute | solution.py:136
  95.3 2.2 maximum_select_fusion.1.x_ref
  102.4 2.2 state_step.21
  104.6 4.2 %all-to-all-start.3 = ((bf16[16,4,32,128]{3,2,1,0:T(8,128)(2,1)}), bf16[16,4,32,128]{3,2,1,0:T(8,128)(2,1)}, u32[]{:S(2)}, u32[]{:S(2)}) async-start(bf16[16,4,32,128]{3,2,1,0:T(8,128)(2,1)} %get-tuple-element.87), calls=%async_computation.3 | async-start | bytes 1048576 | tf_op jit(solution)/shard_map/all_to_all | solution.py:134
  109.2 10.7 %all-to-all-done.3 = bf16[16,4,32,128]{3,2,1,0:T(8,128)(2,1)} async-done(((bf16[16,4,32,128]{3,2,1,0:T(8,128)(2,1)}), bf16[16,4,32,128]{3,2,1,0:T(8,128)(2,1)}, u32[]{:S(2)}, u32[]{:S(2)}) %all-to-all-start.3) | async-done | bytes 524320 | tf_op jit(solution)/shard_map/all_to_all | solution.py:134
  132.5 3.6 %all-to-all-start.4 = ((bf16[16,4,32,128]{3,2,1,0:T(8,128)(2,1)}), bf16[16,4,32,128]{3,2,1,0:T(8,128)(2,1)S(1)}, u32[]{:S(2)}, u32[]{:S(2)}) async-start(bf16[16,4,32,128]{3,2,1,0:T(8,128)(2,1)} %get-tuple-element.81), calls=%async_computation.4 | async-start | bytes 1048576 | tf_op jit(solution)/shard_map/all_to_all | solution.py:134
  136.5 10.7 %all-to-all-done.4 = bf16[16,4,32,128]{3,2,1,0:T(8,128)(2,1)S(1)} async-done(((bf16[16,4,32,128]{3,2,1,0:T(8,128)(2,1)}), bf16[16,4,32,128]{3,2,1,0:T(8,128)(2,1)S(1)}, u32[]{:S(2)}, u32[]{:S(2)}) %all-to-all-start.4) | async-done | bytes 524320 | tf_op jit(solution)/shard_map/all_to_all | solution.py:134
  151.9 2.2 copy-done.5
  156.6 2.2 state_step.19
  158.8 3.6 %all-to-all-start.5 = ((bf16[16,4,32,128]{3,2,1,0:T(8,128)(2,1)}), bf16[16,4,32,128]{3,2,1,0:T(8,128)(2,1)S(1)}, u32[]{:S(2)}, u32[]{:S(2)}) async-start(bf16[16,4,32,128]{3,2,1,0:T(8,128)(2,1)} %get-tuple-element.105), calls=%async_computation.5 | async-start | bytes 1048576 | tf_op jit(solution)/shard_map/all_to_all | solution.py:134
  162.6 11.0 %all-to-all-done.5 = bf16[16,4,32,128]{3,2,1,0:T(8,128)(2,1)S(1)} async-done(((bf16[16,4,32,128]{3,2,1,0:T(8,128)(2,1)}), bf16[16,4,32,128]{3,2,1,0:T(8,128)(2,1)S(1)}, u32[]{:S(2)}, u32[]{:S(2)}) %all-to-all-start.5) | async-done | bytes 524320 | tf_op jit(solution)/shard_map/all_to_all | solution.py:134
  176.7 2.2 copy-done.6
  183.3 3.6 %all-to-all-start.6 = ((bf16[16,4,32,128]{3,2,1,0:T(8,128)(2,1)}), bf16[16,4,32,128]{3,2,1,0:T(8,128)(2,1)S(1)}, u32[]{:S(2)}, u32[]{:S(2)}) async-start(bf16[16,4,32,128]{3,2,1,0:T(8,128)(2,1)} %get-tuple-element.111), calls=%async_computation.6 | async-start | bytes 1048576 | tf_op jit(solution)/shard_map/all_to_all | solution.py:134
  188.7 9.2 %all-to-all-done.6 = bf16[16,4,32,128]{3,2,1,0:T(8,128)(2,1)S(1)} async-done(((bf16[16,4,32,128]{3,2,1,0:T(8,128)(2,1)}), bf16[16,4,32,128]{3,2,1,0:T(8,128)(2,1)S(1)}, u32[]{:S(2)}, u32[]{:S(2)}) %all-to-all-start.6) | async-done | bytes 524320 | tf_op jit(solution)/shard_map/all_to_all | solution.py:134
  208.1 3.6 %all-to-all-start.7 = ((bf16[16,4,32,128]{3,2,1,0:T(8,128)(2,1)}), bf16[16,4,32,128]{3,2,1,0:T(8,128)(2,1)S(1)}, u32[]{:S(2)}, u32[]{:S(2)}) async-start(bf16[16,4,32,128]{3,2,1,0:T(8,128)(2,1)} %get-tuple-element.117), calls=%async_computation.7 | async-start | bytes 1048576 | tf_op jit(solution)/shard_map/all_to_all | solution.py:134
  213.3 9.4 %all-to-all-done.7 = bf16[16,4,32,128]{3,2,1,0:T(8,128)(2,1)S(1)} async-done(((bf16[16,4,32,128]{3,2,1,0:T(8,128)(2,1)}), bf16[16,4,32,128]{3,2,1,0:T(8,128)(2,1)S(1)}, u32[]{:S(2)}, u32[]{:S(2)}) %all-to-all-start.7) | async-done | bytes 524320 | tf_op jit(solution)/shard_map/all_to_all | solution.py:134
  232.7 3.6 %all-to-all-start.8 = ((bf16[16,4,32,128]{3,2,1,0:T(8,128)(2,1)}), bf16[16,4,32,128]{3,2,1,0:T(8,128)(2,1)S(1)}, u32[]{:S(2)}, u32[]{:S(2)}) async-start(bf16[16,4,32,128]{3,2,1,0:T(8,128)(2,1)} %get-tuple-element.75), calls=%async_computation.8 | async-start | bytes 1048576 | tf_op jit(solution)/shard_map/all_to_all | solution.py:134
  238.1 9.2 %all-to-all-done.8 = bf16[16,4,32,128]{3,2,1,0:T(8,128)(2,1)S(1)} async-done(((bf16[16,4,32,128]{3,2,1,0:T(8,128)(2,1)}), bf16[16,4,32,128]{3,2,1,0:T(8,128)(2,1)S(1)}, u32[]{:S(2)}, u32[]{:S(2)}) %all-to-all-start.8) | async-done | bytes 524320 | tf_op jit(solution)/shard_map/all_to_all | solution.py:134
  257.3 3.6 %all-to-all-start.9 = ((bf16[16,4,32,128]{3,2,1,0:T(8,128)(2,1)}), bf16[16,4,32,128]{3,2,1,0:T(8,128)(2,1)S(1)}, u32[]{:S(2)}, u32[]{:S(2)}) async-start(bf16[16,4,32,128]{3,2,1,0:T(8,128)(2,1)} %get-tuple-element.129), calls=%async_computation.9 | async-start | bytes 1048576 | tf_op jit(solution)/shard_map/all_to_all | solution.py:134
  262.7 9.2 %all-to-all-done.9 = bf16[16,4,32,128]{3,2,1,0:T(8,128)(2,1)S(1)} async-done(((bf16[16,4,32,128]{3,2,1,0:T(8,128)(2,1)}), bf16[16,4,32,128]{3,2,1,0:T(8,128)(2,1)S(1)}, u32[]{:S(2)}, u32[]{:S(2)}) %all-to-all-start.9) | async-done | bytes 524320 | tf_op jit(solution)/shard_map/all_to_all | solution.py:134
  281.9 3.6 %all-to-all-start.10 = ((bf16[16,4,32,128]{3,2,1,0:T(8,128)(2,1)}), bf16[16,4,32,128]{3,2,1,0:T(8,128)(2,1)S(1)}, u32[]{:S(2)}, u32[]{:S(2)}) async-start(bf16[16,4,32,128]{3,2,1,0:T(8,128)(2,1)} %get-tuple-element.123), calls=%async_computation.10 | async-start | bytes 1048576 | tf_op jit(solution)/shard_map/all_to_all | solution.py:134
  287.4 9.2 %all-to-all-done.10 = bf16[16,4,32,128]{3,2,1,0:T(8,128)(2,1)S(1)} async-done(((bf16[16,4,32,128]{3,2,1,0:T(8,128)(2,1)}), bf16[16,4,32,128]{3,2,1,0:T(8,128)(2,1)S(1)}, u32[]{:S(2)}, u32[]{:S(2)}) %all-to-all-start.10) | async-done | bytes 524320 | tf_op jit(solution)/shard_map/all_to_all | solution.py:134
  (172 shorter events, 120.1 us)
Async XLA Ops:
  31.6 11.4 %collective-permute-start = (bf16[64,32,128]{2,1,0:T(8,128)(2,1)}, bf16[64,32,128]{2,1,0:T(8,128)(2,1)}, u32[]{:S(2)}, u32[]{:S(2)}) collective-permute-start(bf16[64,32,128]{2,1,0:T(8,128)(2,1)} %bitcast.9), channel_id=1, source_target_pairs={{0,1},{1,0},{2,3},{3,2},{4,5},{5,4},{6,7},{7,6},{8,9},{9,8},{10,11... | collective-permute-start | bytes 1572872 | tf_op jit(solution)/shard_map/ppermute | solution.py:87
  38.0 15.2 %collective-permute-start.2 = (bf16[64,32,128]{2,1,0:T(8,128)(2,1)}, bf16[64,32,128]{2,1,0:T(8,128)(2,1)}, u32[]{:S(2)}, u32[]{:S(2)}) collective-permute-start(bf16[64,32,128]{2,1,0:T(8,128)(2,1)} %bitcast.9), channel_id=1, source_target_pairs={{0,32},{32,64},{64,96},{1,33},{33,65},{65,97},{2,34},{34,66},{66,9... | collective-permute-start | bytes 1572872 | tf_op jit(solution)/shard_map/ppermute | solution.py:136
  46.5 15.3 %all-to-all-start.1 = ((bf16[16,4,32,128]{3,2,1,0:T(8,128)(2,1)}), bf16[16,4,32,128]{3,2,1,0:T(8,128)(2,1)}, u32[]{:S(2)}, u32[]{:S(2)}) async-start(bf16[16,4,32,128]{3,2,1,0:T(8,128)(2,1)} %get-tuple-element.93), calls=%async_computation.1 | async-start | bytes 1048576 | tf_op jit(solution)/shard_map/all_to_all | solution.py:134
  53.2 14.2 %collective-permute-start.3 = (bf16[64,32,128]{2,1,0:T(8,128)(2,1)}, bf16[64,32,128]{2,1,0:T(8,128)(2,1)}, u32[]{:S(2)}, u32[]{:S(2)}) collective-permute-start(bf16[64,32,128]{2,1,0:T(8,128)(2,1)} %collective-permute-done.2), channel_id=1, source_target_pairs={{0,1},{1,0},{2,3},{3,2},{4,5},{5,4},{6,7},{7,6},{8,9},{9,8},{10,11... | collective-permute-start | bytes 1572872 | tf_op jit(solution)/shard_map/ppermute | solution.py:87
  63.5 14.9 %collective-permute-start.5 = (bf16[64,32,128]{2,1,0:T(8,128)(2,1)}, bf16[64,32,128]{2,1,0:T(8,128)(2,1)}, u32[]{:S(2)}, u32[]{:S(2)}) collective-permute-start(bf16[64,32,128]{2,1,0:T(8,128)(2,1)} %bitcast.15), channel_id=1, source_target_pairs={{0,32},{32,64},{64,96},{1,33},{33,65},{65,97},{2,34},{34,66},{66,9... | collective-permute-start | bytes 1572872 | tf_op jit(solution)/shard_map/ppermute | solution.py:136
  74.1 15.3 %all-to-all-start.2 = ((bf16[16,4,32,128]{3,2,1,0:T(8,128)(2,1)}), bf16[16,4,32,128]{3,2,1,0:T(8,128)(2,1)}, u32[]{:S(2)}, u32[]{:S(2)}) async-start(bf16[16,4,32,128]{3,2,1,0:T(8,128)(2,1)} %get-tuple-element.99), calls=%async_computation.2 | async-start | bytes 1048576 | tf_op jit(solution)/shard_map/all_to_all | solution.py:134
  78.4 17.0 %collective-permute-start.6 = (bf16[64,32,128]{2,1,0:T(8,128)(2,1)}, bf16[64,32,128]{2,1,0:T(8,128)(2,1)}, u32[]{:S(2)}, u32[]{:S(2)}) collective-permute-start(bf16[64,32,128]{2,1,0:T(8,128)(2,1)} %collective-permute-done.5), channel_id=1, source_target_pairs={{0,1},{1,0},{2,3},{3,2},{4,5},{5,4},{6,7},{7,6},{8,9},{9,8},{10,11... | collective-permute-start | bytes 1572872 | tf_op jit(solution)/shard_map/ppermute | solution.py:87
  89.5 11.6 %collective-permute-start.4 = (bf16[64,32,128]{2,1,0:T(8,128)(2,1)}, bf16[64,32,128]{2,1,0:T(8,128)(2,1)}, u32[]{:S(2)}, u32[]{:S(2)}) collective-permute-start(bf16[64,32,128]{2,1,0:T(8,128)(2,1)} %bitcast.19), channel_id=1, source_target_pairs={{0,1},{1,0},{2,3},{3,2},{4,5},{5,4},{6,7},{7,6},{8,9},{9,8},{10,11... | collective-permute-start | bytes 1572872 | tf_op jit(solution)/shard_map/ppermute | solution.py:87
  92.1 16.7 %collective-permute-start.8 = (bf16[64,32,128]{2,1,0:T(8,128)(2,1)}, bf16[64,32,128]{2,1,0:T(8,128)(2,1)}, u32[]{:S(2)}, u32[]{:S(2)}) collective-permute-start(bf16[64,32,128]{2,1,0:T(8,128)(2,1)} %bitcast.19), channel_id=1, source_target_pairs={{0,32},{32,64},{64,96},{1,33},{33,65},{65,97},{2,34},{34,66},{66,9... | collective-permute-start | bytes 1572872 | tf_op jit(solution)/shard_map/ppermute | solution.py:136
  104.6 15.3 %all-to-all-start.3 = ((bf16[16,4,32,128]{3,2,1,0:T(8,128)(2,1)}), bf16[16,4,32,128]{3,2,1,0:T(8,128)(2,1)}, u32[]{:S(2)}, u32[]{:S(2)}) async-start(bf16[16,4,32,128]{3,2,1,0:T(8,128)(2,1)} %get-tuple-element.87), calls=%async_computation.3 | async-start | bytes 1048576 | tf_op jit(solution)/shard_map/all_to_all | solution.py:134
  108.8 14.9 %collective-permute-start.9 = (bf16[64,32,128]{2,1,0:T(8,128)(2,1)}, bf16[64,32,128]{2,1,0:T(8,128)(2,1)}, u32[]{:S(2)}, u32[]{:S(2)}) collective-permute-start(bf16[64,32,128]{2,1,0:T(8,128)(2,1)} %collective-permute-done.8), channel_id=1, source_target_pairs={{0,1},{1,0},{2,3},{3,2},{4,5},{5,4},{6,7},{7,6},{8,9},{9,8},{10,11... | collective-permute-start | bytes 1572872 | tf_op jit(solution)/shard_map/ppermute | solution.py:87
  121.5 14.6 %collective-permute-start.11 = (bf16[64,32,128]{2,1,0:T(8,128)(2,1)}, bf16[64,32,128]{2,1,0:T(8,128)(2,1)}, u32[]{:S(2)}, u32[]{:S(2)}) collective-permute-start(bf16[64,32,128]{2,1,0:T(8,128)(2,1)} %bitcast.23), channel_id=1, source_target_pairs={{0,32},{32,64},{64,96},{1,33},{33,65},{65,97},{2,34},{34,66},{66,9... | collective-permute-start | bytes 1572872 | tf_op jit(solution)/shard_map/ppermute | solution.py:136
  132.5 14.6 %all-to-all-start.4 = ((bf16[16,4,32,128]{3,2,1,0:T(8,128)(2,1)}), bf16[16,4,32,128]{3,2,1,0:T(8,128)(2,1)S(1)}, u32[]{:S(2)}, u32[]{:S(2)}) async-start(bf16[16,4,32,128]{3,2,1,0:T(8,128)(2,1)} %get-tuple-element.81), calls=%async_computation.4 | async-start | bytes 1048576 | tf_op jit(solution)/shard_map/all_to_all | solution.py:134
  136.1 14.0 %collective-permute-start.12 = (bf16[64,32,128]{2,1,0:T(8,128)(2,1)}, bf16[64,32,128]{2,1,0:T(8,128)(2,1)S(1)}, u32[]{:S(2)}, u32[]{:S(2)}) collective-permute-start(bf16[64,32,128]{2,1,0:T(8,128)(2,1)} %collective-permute-done.11), channel_id=1, source_target_pairs={{0,1},{1,0},{2,3},{3,2},{4,5},{5,4},{6,7},{7,6},{8,9},{9,8},{10,11... | collective-permute-start | bytes 1572872 | tf_op jit(solution)/shard_map/ppermute | solution.py:87
  148.8 13.6 %collective-permute-start.14 = (bf16[64,32,128]{2,1,0:T(8,128)(2,1)S(1)}, bf16[64,32,128]{2,1,0:T(8,128)(2,1)S(1)}, u32[]{:S(2)}, u32[]{:S(2)}) collective-permute-start(bf16[64,32,128]{2,1,0:T(8,128)(2,1)S(1)} %bitcast.141), channel_id=1, source_target_pairs={{0,32},{32,64},{64,96},{1,33},{33,65},{65,97},{2,34},{34,66},{66,9... | collective-permute-start | bytes 1572872 | tf_op jit(solution)/shard_map/ppermute | solution.py:136
  158.8 14.8 %all-to-all-start.5 = ((bf16[16,4,32,128]{3,2,1,0:T(8,128)(2,1)}), bf16[16,4,32,128]{3,2,1,0:T(8,128)(2,1)S(1)}, u32[]{:S(2)}, u32[]{:S(2)}) async-start(bf16[16,4,32,128]{3,2,1,0:T(8,128)(2,1)} %get-tuple-element.105), calls=%async_computation.5 | async-start | bytes 1048576 | tf_op jit(solution)/shard_map/all_to_all | solution.py:134
  162.4 14.2 %collective-permute-start.15 = (bf16[64,32,128]{2,1,0:T(8,128)(2,1)S(1)}, bf16[64,32,128]{2,1,0:T(8,128)(2,1)S(1)}, u32[]{:S(2)}, u32[]{:S(2)}) collective-permute-start(bf16[64,32,128]{2,1,0:T(8,128)(2,1)S(1)} %collective-permute-done.14), channel_id=1, source_target_pairs={{0,1},{1,0},{2,3},{3,2},{4,5},{5,4},{6,7},{7,6},{8,9},{9,8},{10,11... | collective-permute-start | bytes 1572872 | tf_op jit(solution)/shard_map/ppermute | solution.py:87
  174.8 13.1 %collective-permute-start.17 = (bf16[64,32,128]{2,1,0:T(8,128)(2,1)S(1)}, bf16[64,32,128]{2,1,0:T(8,128)(2,1)S(1)}, u32[]{:S(2)}, u32[]{:S(2)}) collective-permute-start(bf16[64,32,128]{2,1,0:T(8,128)(2,1)S(1)} %bitcast.144), channel_id=1, source_target_pairs={{0,32},{32,64},{64,96},{1,33},{33,65},{65,97},{2,34},{34,66},{66,9... | collective-permute-start | bytes 1572872 | tf_op jit(solution)/shard_map/ppermute | solution.py:136
  183.3 14.6 %all-to-all-start.6 = ((bf16[16,4,32,128]{3,2,1,0:T(8,128)(2,1)}), bf16[16,4,32,128]{3,2,1,0:T(8,128)(2,1)S(1)}, u32[]{:S(2)}, u32[]{:S(2)}) async-start(bf16[16,4,32,128]{3,2,1,0:T(8,128)(2,1)} %get-tuple-element.111), calls=%async_computation.6 | async-start | bytes 1048576 | tf_op jit(solution)/shard_map/all_to_all | solution.py:134
  187.9 13.5 %collective-permute-start.18 = (bf16[64,32,128]{2,1,0:T(8,128)(2,1)S(1)}, bf16[64,32,128]{2,1,0:T(8,128)(2,1)S(1)}, u32[]{:S(2)}, u32[]{:S(2)}) collective-permute-start(bf16[64,32,128]{2,1,0:T(8,128)(2,1)S(1)} %collective-permute-done.17), channel_id=1, source_target_pairs={{0,1},{1,0},{2,3},{3,2},{4,5},{5,4},{6,7},{7,6},{8,9},{9,8},{10,11... | collective-permute-start | bytes 1572872 | tf_op jit(solution)/shard_map/ppermute | solution.py:87
  199.3 13.2 %collective-permute-start.20 = (bf16[64,32,128]{2,1,0:T(8,128)(2,1)S(1)}, bf16[64,32,128]{2,1,0:T(8,128)(2,1)S(1)}, u32[]{:S(2)}, u32[]{:S(2)}) collective-permute-start(bf16[64,32,128]{2,1,0:T(8,128)(2,1)S(1)} %bitcast.147), channel_id=1, source_target_pairs={{0,32},{32,64},{64,96},{1,33},{33,65},{65,97},{2,34},{34,66},{66,9... | collective-permute-start | bytes 1572872 | tf_op jit(solution)/shard_map/ppermute | solution.py:136
  208.1 14.6 %all-to-all-start.7 = ((bf16[16,4,32,128]{3,2,1,0:T(8,128)(2,1)}), bf16[16,4,32,128]{3,2,1,0:T(8,128)(2,1)S(1)}, u32[]{:S(2)}, u32[]{:S(2)}) async-start(bf16[16,4,32,128]{3,2,1,0:T(8,128)(2,1)} %get-tuple-element.117), calls=%async_computation.7 | async-start | bytes 1048576 | tf_op jit(solution)/shard_map/all_to_all | solution.py:134
  212.5 13.5 %collective-permute-start.21 = (bf16[64,32,128]{2,1,0:T(8,128)(2,1)S(1)}, bf16[64,32,128]{2,1,0:T(8,128)(2,1)S(1)}, u32[]{:S(2)}, u32[]{:S(2)}) collective-permute-start(bf16[64,32,128]{2,1,0:T(8,128)(2,1)S(1)} %collective-permute-done.20), channel_id=1, source_target_pairs={{0,1},{1,0},{2,3},{3,2},{4,5},{5,4},{6,7},{7,6},{8,9},{9,8},{10,11... | collective-permute-start | bytes 1572872 | tf_op jit(solution)/shard_map/ppermute | solution.py:87
  224.1 13.2 %collective-permute-start.23 = (bf16[64,32,128]{2,1,0:T(8,128)(2,1)S(1)}, bf16[64,32,128]{2,1,0:T(8,128)(2,1)S(1)}, u32[]{:S(2)}, u32[]{:S(2)}) collective-permute-start(bf16[64,32,128]{2,1,0:T(8,128)(2,1)S(1)} %bitcast.150), channel_id=1, source_target_pairs={{0,32},{32,64},{64,96},{1,33},{33,65},{65,97},{2,34},{34,66},{66,9... | collective-permute-start | bytes 1572872 | tf_op jit(solution)/shard_map/ppermute | solution.py:136
  232.7 14.6 %all-to-all-start.8 = ((bf16[16,4,32,128]{3,2,1,0:T(8,128)(2,1)}), bf16[16,4,32,128]{3,2,1,0:T(8,128)(2,1)S(1)}, u32[]{:S(2)}, u32[]{:S(2)}) async-start(bf16[16,4,32,128]{3,2,1,0:T(8,128)(2,1)} %get-tuple-element.75), calls=%async_computation.8 | async-start | bytes 1048576 | tf_op jit(solution)/shard_map/all_to_all | solution.py:134
  237.3 13.3 %collective-permute-start.24 = (bf16[64,32,128]{2,1,0:T(8,128)(2,1)S(1)}, bf16[64,32,128]{2,1,0:T(8,128)(2,1)S(1)}, u32[]{:S(2)}, u32[]{:S(2)}) collective-permute-start(bf16[64,32,128]{2,1,0:T(8,128)(2,1)S(1)} %collective-permute-done.23), channel_id=1, source_target_pairs={{0,1},{1,0},{2,3},{3,2},{4,5},{5,4},{6,7},{7,6},{8,9},{9,8},{10,11... | collective-permute-start | bytes 1572872 | tf_op jit(solution)/shard_map/ppermute | solution.py:87
  248.7 13.2 %collective-permute-start.26 = (bf16[64,32,128]{2,1,0:T(8,128)(2,1)S(1)}, bf16[64,32,128]{2,1,0:T(8,128)(2,1)S(1)}, u32[]{:S(2)}, u32[]{:S(2)}) collective-permute-start(bf16[64,32,128]{2,1,0:T(8,128)(2,1)S(1)} %bitcast.153), channel_id=1, source_target_pairs={{0,32},{32,64},{64,96},{1,33},{33,65},{65,97},{2,34},{34,66},{66,9... | collective-permute-start | bytes 1572872 | tf_op jit(solution)/shard_map/ppermute | solution.py:136
  257.3 14.6 %all-to-all-start.9 = ((bf16[16,4,32,128]{3,2,1,0:T(8,128)(2,1)}), bf16[16,4,32,128]{3,2,1,0:T(8,128)(2,1)S(1)}, u32[]{:S(2)}, u32[]{:S(2)}) async-start(bf16[16,4,32,128]{3,2,1,0:T(8,128)(2,1)} %get-tuple-element.129), calls=%async_computation.9 | async-start | bytes 1048576 | tf_op jit(solution)/shard_map/all_to_all | solution.py:134
  262.0 13.3 %collective-permute-start.27 = (bf16[64,32,128]{2,1,0:T(8,128)(2,1)S(1)}, bf16[64,32,128]{2,1,0:T(8,128)(2,1)S(1)}, u32[]{:S(2)}, u32[]{:S(2)}) collective-permute-start(bf16[64,32,128]{2,1,0:T(8,128)(2,1)S(1)} %collective-permute-done.26), channel_id=1, source_target_pairs={{0,1},{1,0},{2,3},{3,2},{4,5},{5,4},{6,7},{7,6},{8,9},{9,8},{10,11... | collective-permute-start | bytes 1572872 | tf_op jit(solution)/shard_map/ppermute | solution.py:87
  273.4 13.2 %collective-permute-start.29 = (bf16[64,32,128]{2,1,0:T(8,128)(2,1)S(1)}, bf16[64,32,128]{2,1,0:T(8,128)(2,1)S(1)}, u32[]{:S(2)}, u32[]{:S(2)}) collective-permute-start(bf16[64,32,128]{2,1,0:T(8,128)(2,1)S(1)} %bitcast.156), channel_id=1, source_target_pairs={{0,32},{32,64},{64,96},{1,33},{33,65},{65,97},{2,34},{34,66},{66,9... | collective-permute-start | bytes 1572872 | tf_op jit(solution)/shard_map/ppermute | solution.py:136
  281.9 14.6 %all-to-all-start.10 = ((bf16[16,4,32,128]{3,2,1,0:T(8,128)(2,1)}), bf16[16,4,32,128]{3,2,1,0:T(8,128)(2,1)S(1)}, u32[]{:S(2)}, u32[]{:S(2)}) async-start(bf16[16,4,32,128]{3,2,1,0:T(8,128)(2,1)} %get-tuple-element.123), calls=%async_computation.10 | async-start | bytes 1048576 | tf_op jit(solution)/shard_map/all_to_all | solution.py:134
  286.6 11.4 %collective-permute-start.30 = (bf16[64,32,128]{2,1,0:T(8,128)(2,1)S(1)}, bf16[64,32,128]{2,1,0:T(8,128)(2,1)S(1)}, u32[]{:S(2)}, u32[]{:S(2)}) collective-permute-start(bf16[64,32,128]{2,1,0:T(8,128)(2,1)S(1)} %collective-permute-done.29), channel_id=1, source_target_pairs={{0,1},{1,0},{2,3},{3,2},{4,5},{5,4},{6,7},{7,6},{8,9},{9,8},{10,11... | collective-permute-start | bytes 1572872 | tf_op jit(solution)/shard_map/ppermute | solution.py:87
  (38 other events, 195.4 us)

commit v2 on v1

v2 whole, which is shorter than its diff:
```python
import functools

import jax
import jax.numpy as jnp
from jax import lax
from jax.experimental import pallas as pl
from jax.experimental.pallas import tpu as pltpu
from jax.sharding import Mesh
from jax.sharding import PartitionSpec as P

LAG = 2
F32 = jnp.float32
BF16 = jnp.bfloat16
WIDTH = ("y", "x", "core")
MIB = 2**20


def vmem():
    return pl.BlockSpec(memory_space=pltpu.VMEM)


def smem():
    return pl.BlockSpec(memory_space=pltpu.SMEM)


def held(x):
    return pltpu.with_memory_space_constraint(x, pltpu.VMEM)


def hbm():
    return pl.BlockSpec(memory_space=pltpu.HBM)


def unmoved(x):
    return pltpu.with_memory_space_constraint(x, pltpu.HBM)


def load_kernel(w_ref, out_ref):
    pltpu.sync_copy(w_ref, out_ref)


def load(w):
    return pl.pallas_call(
        load_kernel,
        out_shape=pltpu.VMEM(w.shape, w.dtype),
        in_specs=[hbm()],
        out_specs=vmem(),
        compiler_params=pltpu.CompilerParams(vmem_limit_bytes=2 * MIB),
        name="load_weights",
    )(unmoved(w))


def row_sums(pick, index_ref, w_ref, row):
    blocks = w_ref.shape[1]
    edge = w_ref.shape[2]
    picked = jnp.concatenate([pick(index_ref[row * blocks + k]) for k in range(blocks)], axis=1)
    return jnp.dot(picked, w_ref[row].reshape(blocks * edge, edge), preferred_element_type=F32)


def from_halves(mine_ref, other_ref):
    half = mine_ref.shape[0]

    def pick(i):
        return jnp.where(
            i < half, mine_ref[jnp.minimum(i, half - 1)], other_ref[jnp.maximum(i - half, 0)]
        )

    return pick


def from_rows(rows_ref, edge):
    return lambda i: rows_ref[:, pl.ds(pl.multiple_of(i * edge, edge), edge)]


def input_kernel(tick, step_count, layer_ref, index_ref, inputs_ref, mine_ref, other_ref, w_ref, bias_ref, out_ref, *scratch):
    edge = w_ref.shape[2]
    row_count = out_ref.shape[1]

    def fill(pick):
        for row in range(w_ref.shape[0]):
            bias = jnp.broadcast_to(bias_ref[row], (row_count, edge))
            out_ref[row] = row_sums(pick, index_ref, w_ref, row) + bias

    if tick >= step_count:
        fill(from_halves(mine_ref, other_ref))
        return
    fresh_ref, arrived = scratch

    @pl.when(layer_ref[0] == 0)
    def _():
        pltpu.make_async_copy(inputs_ref.at[tick], fresh_ref, arrived).start()
        pltpu.make_async_copy(inputs_ref.at[tick], fresh_ref, arrived).wait()
        fill(from_rows(fresh_ref, edge))

    @pl.when(layer_ref[0] != 0)
    def _():
        if mine_ref is None:
            out_ref[...] = jnp.zeros_like(out_ref)
        else:
            fill(from_halves(mine_ref, other_ref))


def without_lower(kernel):
    def run(layer_ref, index_ref, inputs_ref, *rest):
        kernel(layer_ref, index_ref, inputs_ref, None, None, *rest)

    return run


def input_sums(tick, layer, index, inputs, lower, w, bias):
    step_count, row_count, hidden = inputs.shape
    rows = w.shape[0]
    kernel = functools.partial(input_kernel, tick, step_count)
    return pl.pallas_call(
        kernel if lower else without_lower(kernel),
        out_shape=pltpu.VMEM((rows, row_count, w.shape[3]), F32),
        in_specs=[smem(), smem(), hbm()] + [vmem()] * (len(lower) + 2),
        out_specs=vmem(),
        scratch_shapes=[pltpu.VMEM((row_count, hidden), BF16), pltpu.SemaphoreType.DMA] if tick < step_count else [],
        compiler_params=pltpu.CompilerParams(vmem_limit_bytes=8 * MIB),
        cost_estimate=pl.CostEstimate(flops=2 * w.size * 32, bytes_accessed=w.size, transcendentals=0),
        name="input_sums",
    )(layer, index, unmoved(inputs), *[held(part) for part in lower], w, held(bias))


def gates_to_state(sums, before, started, running):
    cell = jax.nn.sigmoid(sums[1]) * before + jax.nn.sigmoid(sums[0]) * jnp.tanh(sums[2])
    output = jax.nn.sigmoid(sums[3]) * jnp.tanh(cell)
    output = jnp.where(started, output, 0.0).astype(BF16)
    return jnp.where(running, cell, before), output


def put(j, output, rows_out, send_out):
    edge = output.shape[1]
    rows_out[:, j * edge:(j + 1) * edge] = output
    for peer in range(send_out.shape[0]):
        send_out[peer, j] = output


def first_kernel(layer_ref, index_ref, inputs_ref, w_hbm, bias_ref, cell_out, rows_out, send_out, w_out, fresh_ref, arrived, loaded):
    per_device, row_count, edge = cell_out.shape
    fresh = pltpu.make_async_copy(inputs_ref.at[0], fresh_ref, arrived)
    fresh.start()
    loads = [
        pltpu.make_async_copy(w_hbm.at[pl.ds(4 * j, 4)], w_out.at[pl.ds(4 * j, 4)], loaded.at[j])
        for j in range(per_device)
    ]
    for copy in loads:
        copy.start()
    fresh.wait()
    started = layer_ref[0] == 0
    pick = from_rows(fresh_ref, edge)
    for j in range(per_device):
        loads[j].wait()
        sums = [
            row_sums(pick, index_ref, w_out, 4 * j + g) + jnp.broadcast_to(bias_ref[4 * j + g], (row_count, edge))
            for g in range(4)
        ]
        cell_out[j], output = gates_to_state(sums, jnp.zeros((row_count, edge), F32), started, started)
        put(j, output, rows_out, send_out)


def first_step(layer, index, inputs, w, bias, per_device, peers):
    _, row_count, hidden = inputs.shape
    rows, _, edge, _ = w.shape
    return pl.pallas_call(
        first_kernel,
        out_shape=(
            pltpu.VMEM((per_device, row_count, edge), F32),
            jax.ShapeDtypeStruct((row_count, per_device * edge), BF16),
            pltpu.VMEM((peers, per_device, row_count, edge), BF16),
            pltpu.VMEM(w.shape, w.dtype),
        ),
        in_specs=[smem(), smem(), hbm(), hbm(), vmem()],
        out_specs=(vmem(), vmem(), vmem(), vmem()),
        scratch_shapes=[
            pltpu.VMEM((row_count, hidden), BF16),
            pltpu.SemaphoreType.DMA,
            pltpu.SemaphoreType.DMA((per_device,)),
        ],
        compiler_params=pltpu.CompilerParams(vmem_limit_bytes=8 * MIB),
        name="first_step",
    )(layer, index, unmoved(inputs), unmoved(w), held(bias))


def state_kernel(step_count, step_ref, index_ref, mine_ref, other_ref, w_ref, partial_ref, cell_ref, cell_out, rows_out, send_out):
    step = step_ref[0]
    started = step >= 0
    running = started & (step < step_count)
    pick = from_halves(mine_ref, other_ref)
    for j in range(cell_ref.shape[0]):
        sums = [partial_ref[4 * j + g] + row_sums(pick, index_ref, w_ref, 4 * j + g) for g in range(4)]
        cell_out[j], output = gates_to_state(sums, cell_ref[j], started, running)
        put(j, output, rows_out, send_out)


def state_step(step, index, state, w, partial, cell, step_count, peers):
    per_device, row_count, edge = cell.shape
    return pl.pallas_call(
        functools.partial(state_kernel, step_count),
        out_shape=(
            pltpu.VMEM(cell.shape, F32),
            jax.ShapeDtypeStruct((row_count, per_device * edge), BF16),
            pltpu.VMEM((peers, per_device, row_count, edge), BF16),
        ),
        in_specs=[smem(), smem()] + [vmem()] * 5,
        out_specs=(vmem(), vmem(), vmem()),
        compiler_params=pltpu.CompilerParams(vmem_limit_bytes=8 * MIB),
        cost_estimate=pl.CostEstimate(flops=2 * w.size * 32, bytes_accessed=w.size, transcendentals=0),
        name="state_step",
    )(step, index, *[held(part) for part in state], w, partial, cell)


def other_core(x):
    return lax.ppermute(x, "core", [(0, 1), (1, 0)])


def body(inputs, in_blocks, rec_blocks, in_cols, rec_cols, bias):
    layer = lax.axis_index("pipe")
    layers = lax.axis_size("pipe")
    core = lax.axis_index("core")
    chips = lax.axis_size("y") * lax.axis_size("x")
    step_count, row_count, hidden = inputs.shape
    _, per_device, gates, kept, edge, _ = in_blocks.shape
    total = hidden // edge
    half = total // 2
    rows = per_device * gates

    def place(cols):
        device = cols // per_device
        return ((device % 2) ^ core) * half + (device // 2) * per_device + cols % per_device

    in_flat = in_cols.reshape(-1)
    in_index = jnp.where(layer == 0, in_flat, place(in_flat))
    rec_index = place(rec_cols.reshape(-1))
    offsets = bias[0].reshape(gates, per_device, edge).transpose(1, 0, 2).reshape(rows, 1, edge)
    layer_ref = layer.astype(jnp.int32).reshape(1)
    w_in = in_blocks.reshape(rows, kept, edge, edge)
    w_rec = rec_blocks.reshape(rows, kept, edge, edge)

    tick_count = step_count + LAG * (layers - 1)
    up = [(i, i + 1) for i in range(layers - 1)]
    cell, out_rows, send, w_in = first_step(layer_ref, in_index, inputs, w_in, offsets, per_device, chips)
    send, w_rec = lax.optimization_barrier((send, w_rec))
    w_rec = load(w_rec)
    arrived = {}
    outputs = [out_rows]
    for tick in range(1, tick_count):
        mine = lax.all_to_all(send, ("y", "x"), 0, 0).reshape(half, row_count, edge)
        lower = ()
        if tick >= LAG:
            low, _ = lax.optimization_barrier((arrived[tick - LAG], out_rows))
            lower = (low, other_core(low))
        partial = input_sums(tick, layer_ref, in_index, inputs, lower, w_in, offsets)
        mine, partial = lax.optimization_barrier((mine, partial))
        if tick <= tick_count - LAG:
            arrived[tick - 1] = lax.ppermute(mine, "pipe", up)
        state = (mine, other_core(mine))
        step = (tick - LAG * layer).astype(jnp.int32).reshape(1)
        cell, out_rows, send = state_step(step, rec_index, state, w_rec, partial, cell, step_count, chips)
        outputs.append(out_rows)
    sequence = lax.dynamic_slice_in_dim(jnp.stack(outputs), LAG * layer, step_count, 0)
    cells = cell.transpose(1, 0, 2).reshape(row_count, per_device * edge)
    return sequence[None], cells[None]


def solution(mesh):
    layers, width = mesh.devices.shape
    grid = Mesh(mesh.devices.reshape(layers, 4, width // 8, 2), ("pipe",) + WIDTH)
    return jax.shard_map(
        body,
        mesh=grid,
        in_specs=(
            P(),
            P("pipe", WIDTH, None, None, None, None),
            P("pipe", WIDTH, None, None, None, None),
            P("pipe", WIDTH, None, None),
            P("pipe", WIDTH, None, None),
            P("pipe", None, WIDTH),
        ),
        out_specs=(P("pipe", None, None, WIDTH), P("pipe", None, WIDTH)),
        check_vma=False,
    )
```

time: 308 us -> 361 us (1.17)
  waiting for transfers between devices: 105 us -> 145 us
  other arithmetic: 39.4 us -> 0.05 us
  Pallas kernels: 16.7 us -> 52.2 us
  starting transfers between devices: 84.2 us -> 105 us
  blocking collectives: 18 us -> 0 us
  local copies, waits for them, and re-layouts: 41.6 us -> 55.1 us
    ppermute x10, waiting for transfers between devices: 7.5 us -> 64.2 us  [body(): arrived[tick - 1] = lax.ppermute(mine, 'pipe', up)]
    pallas_call x13 -> x24, Pallas kernels: 16.7 us -> 52.2 us  [the longest x11 24.3 us: state_step(): pl.pallas_call(functools.partial(state_kernel, step_count), out_shape=(pl...]
    pallas_call x11 -> x0, other arithmetic: 23.9 us -> none  [state_step(): pl.pallas_call(functools.partial(state_kernel, step_count), out_shape=(ja...]
    all_to_all x10 -> x11, waiting for transfers between devices: 97.1 us -> 78.7 us  [body(): mine = lax.all_to_all(send, ('y', 'x'), 0, 0).reshape(half, row_count, edge)]
    all_to_all x1 -> x0, blocking collectives: 18 us -> none  [body(): mine = lax.all_to_all(send, ('y', 'x'), 0, 0).reshape(half, row_count, edge)]
    ppermute x10, starting transfers between devices: 24.5 us -> 40.9 us  [body(): arrived[tick - 1] = lax.ppermute(mine, 'pipe', up)]
    unnamed x66 -> x65, local copies, waits for them, and re-layouts: 37.1 us -> 52.8 us
    select_n x4 -> x0, other arithmetic: 7.78 us -> none  [body(): x = lower if fresh is None else jnp.where(layer == 0, fresh, lower)]
  transfers between devices with their start and end apart: 41 -> 42, of which waited for: 16 -> 22; matrix products, arithmetic and copies ran while one was open for 13% -> 0% of each run, Pallas kernels for 5% -> 13%
where the time goes in v2:
time: 361 us; the launch traced here: 358 us
  waiting for transfers between devices  145 us (40%)
  starting transfers between devices  105 us (29%)
  local copies, waits for them, and re-layouts  55.1 us (15%)
  Pallas kernels  52.2 us (14%)
    all_to_all x11, waiting for transfers between devices, body(): mine = lax.all_to_all(send, ('y', 'x'), 0, 0).reshape(half, row_count, edge)  78.7 us
    ppermute x10, waiting for transfers between devices, body(): arrived[tick - 1] = lax.ppermute(mine, 'pipe', up)  64.2 us
    unnamed x65, local copies, waits for them, and re-layouts  52.8 us
    all_to_all x11, starting transfers between devices, body(): mine = lax.all_to_all(send, ('y', 'x'), 0, 0).reshape(half, row_count, edge)  43.5 us
    ppermute x10, starting transfers between devices, body(): arrived[tick - 1] = lax.ppermute(mine, 'pipe', up)  40.9 us
    pallas_call x11, Pallas kernels, state_step(): pl.pallas_call(functools.partial(state_kernel, step_count), out_shape=(pl...  24.3 us
    pallas_call x11, Pallas kernels, input_sums(): pl.pallas_call(kernel if lower else without_lower(kernel), out_shape=pltp...  20.9 us
    ppermute x21, starting transfers between devices, other_core(): return lax.ppermute(x, 'core', [(0, 1), (1, 0)])  20.8 us
  transfers between devices with their start and end apart: 42, of which 22 were waited for; matrix products, arithmetic and copies ran while one was open for 0% of the time, Pallas kernels for 13%

profile of v2, /device:TPU:1, one launch (start us, length us, event | category | flops | bytes accessed | tf_op | source)
XLA Modules:
  0.0 358.4 jit_solution(9722951093779786602)
XLA Ops:
  2.2 4.8 %first_step.1 = (f32[4,32,128]{2,1,0:T(8,128)S(1)}, bf16[32,512]{1,0:T(8,128)(2,1)S(1)}, bf16[16,4,32,128]{3,2,1,0:T(8,128)(2,1)}, bf16[16,8,128,128]{3,2,1,0:T(8,128)(2,1)S(1)}) custom-call(s32[1]{0:T(128)} %bitcast.layer_ref, s32[128]{0:T(128)S(1)} %broadcast_select_fusion.index_ref, bf16[6,32,16384]{2,1,0:T(8,128)(2,1)} %inputs_ref.23, ...), custom_call_target="tpu_custom_call" | custom-call | tf_op jit(solution)/shard_map/first_step/pallas_call | solution.py:166
  9.0 7.6 %all-to-all-start = ((bf16[16,4,32,128]{3,2,1,0:T(8,128)(2,1)}), bf16[16,4,32,128]{3,2,1,0:T(8,128)(2,1)S(1)}, u32[]{:S(2)}, u32[]{:S(2)}) async-start(bf16[16,4,32,128]{3,2,1,0:T(8,128)(2,1)} %get-tuple-element.74), calls=%async_computation | async-start | bytes 1048576 | tf_op jit(solution)/shard_map/all_to_all | solution.py:249
  21.4 5.7 %all-to-all-done = bf16[16,4,32,128]{3,2,1,0:T(8,128)(2,1)S(1)} async-done(((bf16[16,4,32,128]{3,2,1,0:T(8,128)(2,1)}), bf16[16,4,32,128]{3,2,1,0:T(8,128)(2,1)S(1)}, u32[]{:S(2)}, u32[]{:S(2)}) %all-to-all-start) | async-done | bytes 524320 | tf_op jit(solution)/shard_map/all_to_all | solution.py:249
  53.1 6.6 %all-to-all-done.1 = bf16[16,4,32,128]{3,2,1,0:T(8,128)(2,1)S(1)} async-done(((bf16[16,4,32,128]{3,2,1,0:T(8,128)(2,1)}), bf16[16,4,32,128]{3,2,1,0:T(8,128)(2,1)S(1)}, u32[]{:S(2)}, u32[]{:S(2)}) %all-to-all-start.1) | async-done | bytes 524320 | tf_op jit(solution)/shard_map/all_to_all | solution.py:249
  60.8 4.1 %collective-permute-start.4 = (bf16[64,32,128]{2,1,0:T(8,128)(2,1)S(1)}, bf16[64,32,128]{2,1,0:T(8,128)(2,1)S(1)}, u32[]{:S(2)}, u32[]{:S(2)}) collective-permute-start(bf16[64,32,128]{2,1,0:T(8,128)(2,1)S(1)} %bitcast.66), channel_id=1, source_target_pairs={{0,32},{32,64},{64,96},{1,33},{33,65},{65,97},{2,34},{34,66},{66,9... | collective-permute-start | bytes 1572872 | tf_op jit(solution)/shard_map/ppermute | solution.py:257
  69.3 6.9 %collective-permute-done.4.mine_ref = bf16[64,32,128]{2,1,0:T(8,128)(2,1)S(1)} collective-permute-done((bf16[64,32,128]{2,1,0:T(8,128)(2,1)S(1)}, bf16[64,32,128]{2,1,0:T(8,128)(2,1)S(1)}, u32[]{:S(2)}, u32[]{:S(2)}) %collective-permute-start.4) | collective-permute-done | bytes 524320 | tf_op jit(solution)/shard_map/ppermute | solution.py:257
  85.4 6.6 %all-to-all-done.2 = bf16[16,4,32,128]{3,2,1,0:T(8,128)(2,1)S(1)} async-done(((bf16[16,4,32,128]{3,2,1,0:T(8,128)(2,1)}), bf16[16,4,32,128]{3,2,1,0:T(8,128)(2,1)S(1)}, u32[]{:S(2)}, u32[]{:S(2)}) %all-to-all-start.2) | async-done | bytes 524320 | tf_op jit(solution)/shard_map/all_to_all | solution.py:249
  93.1 4.1 %collective-permute-start.7 = (bf16[64,32,128]{2,1,0:T(8,128)(2,1)S(1)}, bf16[64,32,128]{2,1,0:T(8,128)(2,1)S(1)}, u32[]{:S(2)}, u32[]{:S(2)}) collective-permute-start(bf16[64,32,128]{2,1,0:T(8,128)(2,1)S(1)} %bitcast.69), channel_id=1, source_target_pairs={{0,32},{32,64},{64,96},{1,33},{33,65},{65,97},{2,34},{34,66},{66,9... | collective-permute-start | bytes 1572872 | tf_op jit(solution)/shard_map/ppermute | solution.py:257
  101.6 6.9 %collective-permute-done.7.mine_ref = bf16[64,32,128]{2,1,0:T(8,128)(2,1)S(1)} collective-permute-done((bf16[64,32,128]{2,1,0:T(8,128)(2,1)S(1)}, bf16[64,32,128]{2,1,0:T(8,128)(2,1)S(1)}, u32[]{:S(2)}, u32[]{:S(2)}) %collective-permute-start.7) | collective-permute-done | bytes 524320 | tf_op jit(solution)/shard_map/ppermute | solution.py:257
  117.6 6.6 %all-to-all-done.3 = bf16[16,4,32,128]{3,2,1,0:T(8,128)(2,1)S(1)} async-done(((bf16[16,4,32,128]{3,2,1,0:T(8,128)(2,1)}), bf16[16,4,32,128]{3,2,1,0:T(8,128)(2,1)S(1)}, u32[]{:S(2)}, u32[]{:S(2)}) %all-to-all-start.3) | async-done | bytes 524320 | tf_op jit(solution)/shard_map/all_to_all | solution.py:249
  125.3 4.3 %collective-permute-start.10 = (bf16[64,32,128]{2,1,0:T(8,128)(2,1)S(1)}, bf16[64,32,128]{2,1,0:T(8,128)(2,1)S(1)}, u32[]{:S(2)}, u32[]{:S(2)}) collective-permute-start(bf16[64,32,128]{2,1,0:T(8,128)(2,1)S(1)} %bitcast.72), channel_id=1, source_target_pairs={{0,32},{32,64},{64,96},{1,33},{33,65},{65,97},{2,34},{34,66},{66,9... | collective-permute-start | bytes 1572872 | tf_op jit(solution)/shard_map/ppermute | solution.py:257
  134.0 6.7 %collective-permute-done.10.mine_ref = bf16[64,32,128]{2,1,0:T(8,128)(2,1)S(1)} collective-permute-done((bf16[64,32,128]{2,1,0:T(8,128)(2,1)S(1)}, bf16[64,32,128]{2,1,0:T(8,128)(2,1)S(1)}, u32[]{:S(2)}, u32[]{:S(2)}) %collective-permute-start.10) | collective-permute-done | bytes 524320 | tf_op jit(solution)/shard_map/ppermute | solution.py:257
  149.9 6.6 %all-to-all-done.4 = bf16[16,4,32,128]{3,2,1,0:T(8,128)(2,1)S(1)} async-done(((bf16[16,4,32,128]{3,2,1,0:T(8,128)(2,1)}), bf16[16,4,32,128]{3,2,1,0:T(8,128)(2,1)S(1)}, u32[]{:S(2)}, u32[]{:S(2)}) %all-to-all-start.4) | async-done | bytes 524320 | tf_op jit(solution)/shard_map/all_to_all | solution.py:249
  157.6 4.1 %collective-permute-start.13 = (bf16[64,32,128]{2,1,0:T(8,128)(2,1)S(1)}, bf16[64,32,128]{2,1,0:T(8,128)(2,1)S(1)}, u32[]{:S(2)}, u32[]{:S(2)}) collective-permute-start(bf16[64,32,128]{2,1,0:T(8,128)(2,1)S(1)} %bitcast.75), channel_id=1, source_target_pairs={{0,32},{32,64},{64,96},{1,33},{33,65},{65,97},{2,34},{34,66},{66,9... | collective-permute-start | bytes 1572872 | tf_op jit(solution)/shard_map/ppermute | solution.py:257
  166.1 6.9 %collective-permute-done.13.mine_ref = bf16[64,32,128]{2,1,0:T(8,128)(2,1)S(1)} collective-permute-done((bf16[64,32,128]{2,1,0:T(8,128)(2,1)S(1)}, bf16[64,32,128]{2,1,0:T(8,128)(2,1)S(1)}, u32[]{:S(2)}, u32[]{:S(2)}) %collective-permute-start.13) | collective-permute-done | bytes 524320 | tf_op jit(solution)/shard_map/ppermute | solution.py:257
  180.9 7.8 %all-to-all-done.5 = bf16[16,4,32,128]{3,2,1,0:T(8,128)(2,1)S(1)} async-done(((bf16[16,4,32,128]{3,2,1,0:T(8,128)(2,1)}), bf16[16,4,32,128]{3,2,1,0:T(8,128)(2,1)S(1)}, u32[]{:S(2)}, u32[]{:S(2)}) %all-to-all-start.5) | async-done | bytes 524320 | tf_op jit(solution)/shard_map/all_to_all | solution.py:249
  189.8 4.1 %collective-permute-start.16 = (bf16[64,32,128]{2,1,0:T(8,128)(2,1)S(1)}, bf16[64,32,128]{2,1,0:T(8,128)(2,1)S(1)}, u32[]{:S(2)}, u32[]{:S(2)}) collective-permute-start(bf16[64,32,128]{2,1,0:T(8,128)(2,1)S(1)} %bitcast.78), channel_id=1, source_target_pairs={{0,32},{32,64},{64,96},{1,33},{33,65},{65,97},{2,34},{34,66},{66,9... | collective-permute-start | bytes 1572872 | tf_op jit(solution)/shard_map/ppermute | solution.py:257
  198.4 6.9 %collective-permute-done.16.mine_ref = bf16[64,32,128]{2,1,0:T(8,128)(2,1)S(1)} collective-permute-done((bf16[64,32,128]{2,1,0:T(8,128)(2,1)S(1)}, bf16[64,32,128]{2,1,0:T(8,128)(2,1)S(1)}, u32[]{:S(2)}, u32[]{:S(2)}) %collective-permute-start.16) | collective-permute-done | bytes 524320 | tf_op jit(solution)/shard_map/ppermute | solution.py:257
  213.2 7.8 %all-to-all-done.6 = bf16[16,4,32,128]{3,2,1,0:T(8,128)(2,1)S(1)} async-done(((bf16[16,4,32,128]{3,2,1,0:T(8,128)(2,1)}), bf16[16,4,32,128]{3,2,1,0:T(8,128)(2,1)S(1)}, u32[]{:S(2)}, u32[]{:S(2)}) %all-to-all-start.6) | async-done | bytes 524320 | tf_op jit(solution)/shard_map/all_to_all | solution.py:249
  222.1 4.1 %collective-permute-start.19 = (bf16[64,32,128]{2,1,0:T(8,128)(2,1)S(1)}, bf16[64,32,128]{2,1,0:T(8,128)(2,1)S(1)}, u32[]{:S(2)}, u32[]{:S(2)}) collective-permute-start(bf16[64,32,128]{2,1,0:T(8,128)(2,1)S(1)} %bitcast.81), channel_id=1, source_target_pairs={{0,32},{32,64},{64,96},{1,33},{33,65},{65,97},{2,34},{34,66},{66,9... | collective-permute-start | bytes 1572872 | tf_op jit(solution)/shard_map/ppermute | solution.py:257
  230.6 6.9 %collective-permute-done.19.mine_ref = bf16[64,32,128]{2,1,0:T(8,128)(2,1)S(1)} collective-permute-done((bf16[64,32,128]{2,1,0:T(8,128)(2,1)S(1)}, bf16[64,32,128]{2,1,0:T(8,128)(2,1)S(1)}, u32[]{:S(2)}, u32[]{:S(2)}) %collective-permute-start.19) | collective-permute-done | bytes 524320 | tf_op jit(solution)/shard_map/ppermute | solution.py:257
  245.4 7.8 %all-to-all-done.7 = bf16[16,4,32,128]{3,2,1,0:T(8,128)(2,1)S(1)} async-done(((bf16[16,4,32,128]{3,2,1,0:T(8,128)(2,1)}), bf16[16,4,32,128]{3,2,1,0:T(8,128)(2,1)S(1)}, u32[]{:S(2)}, u32[]{:S(2)}) %all-to-all-start.7) | async-done | bytes 524320 | tf_op jit(solution)/shard_map/all_to_all | solution.py:249
  254.3 4.1 %collective-permute-start.22 = (bf16[64,32,128]{2,1,0:T(8,128)(2,1)S(1)}, bf16[64,32,128]{2,1,0:T(8,128)(2,1)S(1)}, u32[]{:S(2)}, u32[]{:S(2)}) collective-permute-start(bf16[64,32,128]{2,1,0:T(8,128)(2,1)S(1)} %bitcast.84), channel_id=1, source_target_pairs={{0,32},{32,64},{64,96},{1,33},{33,65},{65,97},{2,34},{34,66},{66,9... | collective-permute-start | bytes 1572872 | tf_op jit(solution)/shard_map/ppermute | solution.py:257
  262.9 6.9 %collective-permute-done.22.mine_ref = bf16[64,32,128]{2,1,0:T(8,128)(2,1)S(1)} collective-permute-done((bf16[64,32,128]{2,1,0:T(8,128)(2,1)S(1)}, bf16[64,32,128]{2,1,0:T(8,128)(2,1)S(1)}, u32[]{:S(2)}, u32[]{:S(2)}) %collective-permute-start.22) | collective-permute-done | bytes 524320 | tf_op jit(solution)/shard_map/ppermute | solution.py:257
  270.5 3.8 %all-to-all-start.8 = ((bf16[16,4,32,128]{3,2,1,0:T(8,128)(2,1)}), bf16[16,4,32,128]{3,2,1,0:T(8,128)(2,1)S(1)}, u32[]{:S(2)}, u32[]{:S(2)}) async-start(bf16[16,4,32,128]{3,2,1,0:T(8,128)(2,1)} %get-tuple-element.123), calls=%async_computation.8 | async-start | bytes 1048576 | tf_op jit(solution)/shard_map/all_to_all | solution.py:249
  277.9 7.6 %all-to-all-done.8 = bf16[16,4,32,128]{3,2,1,0:T(8,128)(2,1)S(1)} async-done(((bf16[16,4,32,128]{3,2,1,0:T(8,128)(2,1)}), bf16[16,4,32,128]{3,2,1,0:T(8,128)(2,1)S(1)}, u32[]{:S(2)}, u32[]{:S(2)}) %all-to-all-start.8) | async-done | bytes 524320 | tf_op jit(solution)/shard_map/all_to_all | solution.py:249
  286.6 4.1 %collective-permute-start.25 = (bf16[64,32,128]{2,1,0:T(8,128)(2,1)S(1)}, bf16[64,32,128]{2,1,0:T(8,128)(2,1)S(1)}, u32[]{:S(2)}, u32[]{:S(2)}) collective-permute-start(bf16[64,32,128]{2,1,0:T(8,128)(2,1)S(1)} %bitcast.87), channel_id=1, source_target_pairs={{0,32},{32,64},{64,96},{1,33},{33,65},{65,97},{2,34},{34,66},{66,9... | collective-permute-start | bytes 1572872 | tf_op jit(solution)/shard_map/ppermute | solution.py:257
  295.1 6.9 %collective-permute-done.25.mine_ref = bf16[64,32,128]{2,1,0:T(8,128)(2,1)S(1)} collective-permute-done((bf16[64,32,128]{2,1,0:T(8,128)(2,1)S(1)}, bf16[64,32,128]{2,1,0:T(8,128)(2,1)S(1)}, u32[]{:S(2)}, u32[]{:S(2)}) %collective-permute-start.25) | collective-permute-done | bytes 524320 | tf_op jit(solution)/shard_map/ppermute | solution.py:257
  310.0 7.8 %all-to-all-done.9 = bf16[16,4,32,128]{3,2,1,0:T(8,128)(2,1)S(1)} async-done(((bf16[16,4,32,128]{3,2,1,0:T(8,128)(2,1)}), bf16[16,4,32,128]{3,2,1,0:T(8,128)(2,1)S(1)}, u32[]{:S(2)}, u32[]{:S(2)}) %all-to-all-start.9) | async-done | bytes 524320 | tf_op jit(solution)/shard_map/all_to_all | solution.py:249
  318.8 4.1 %collective-permute-start.28 = (bf16[64,32,128]{2,1,0:T(8,128)(2,1)S(1)}, bf16[64,32,128]{2,1,0:T(8,128)(2,1)S(1)}, u32[]{:S(2)}, u32[]{:S(2)}) collective-permute-start(bf16[64,32,128]{2,1,0:T(8,128)(2,1)S(1)} %bitcast.58), channel_id=1, source_target_pairs={{0,32},{32,64},{64,96},{1,33},{33,65},{65,97},{2,34},{34,66},{66,9... | collective-permute-start | bytes 1572872 | tf_op jit(solution)/shard_map/ppermute | solution.py:257
  327.4 6.9 %collective-permute-done.28.mine_ref = bf16[64,32,128]{2,1,0:T(8,128)(2,1)S(1)} collective-permute-done((bf16[64,32,128]{2,1,0:T(8,128)(2,1)S(1)}, bf16[64,32,128]{2,1,0:T(8,128)(2,1)S(1)}, u32[]{:S(2)}, u32[]{:S(2)}) %collective-permute-start.28) | collective-permute-done | bytes 524320 | tf_op jit(solution)/shard_map/ppermute | solution.py:257
  342.2 7.8 %all-to-all-done.10 = bf16[16,4,32,128]{3,2,1,0:T(8,128)(2,1)S(1)} async-done(((bf16[16,4,32,128]{3,2,1,0:T(8,128)(2,1)}), bf16[16,4,32,128]{3,2,1,0:T(8,128)(2,1)S(1)}, u32[]{:S(2)}, u32[]{:S(2)}) %all-to-all-start.10) | async-done | bytes 524320 | tf_op jit(solution)/shard_map/all_to_all | solution.py:249
  (149 shorter events, 162.9 us)
Async XLA Ops:
  9.0 18.1 %all-to-all-start = ((bf16[16,4,32,128]{3,2,1,0:T(8,128)(2,1)}), bf16[16,4,32,128]{3,2,1,0:T(8,128)(2,1)S(1)}, u32[]{:S(2)}, u32[]{:S(2)}) async-start(bf16[16,4,32,128]{3,2,1,0:T(8,128)(2,1)} %get-tuple-element.74), calls=%async_computation | async-start | bytes 1048576 | tf_op jit(solution)/shard_map/all_to_all | solution.py:249
  27.1 9.9 %collective-permute-start = (bf16[64,32,128]{2,1,0:T(8,128)(2,1)S(1)}, bf16[64,32,128]{2,1,0:T(8,128)(2,1)S(1)}, u32[]{:S(2)}, u32[]{:S(2)}) collective-permute-start(bf16[64,32,128]{2,1,0:T(8,128)(2,1)S(1)} %bitcast.62), channel_id=1, source_target_pairs={{0,1},{1,0},{2,3},{3,2},{4,5},{5,4},{6,7},{7,6},{8,9},{9,8},{10,11... | collective-permute-start | bytes 1572872 | tf_op jit(solution)/shard_map/ppermute | solution.py:215
  29.1 14.7 %collective-permute-start.1 = (bf16[64,32,128]{2,1,0:T(8,128)(2,1)S(1)}, bf16[64,32,128]{2,1,0:T(8,128)(2,1)S(1)}, u32[]{:S(2)}, u32[]{:S(2)}) collective-permute-start(bf16[64,32,128]{2,1,0:T(8,128)(2,1)S(1)} %bitcast.63), channel_id=1, source_target_pairs={{0,32},{32,64},{64,96},{1,33},{33,65},{65,97},{2,34},{34,66},{66,9... | collective-permute-start | bytes 1572872 | tf_op jit(solution)/shard_map/ppermute | solution.py:257
  44.8 15.0 %all-to-all-start.1 = ((bf16[16,4,32,128]{3,2,1,0:T(8,128)(2,1)}), bf16[16,4,32,128]{3,2,1,0:T(8,128)(2,1)S(1)}, u32[]{:S(2)}, u32[]{:S(2)}) async-start(bf16[16,4,32,128]{3,2,1,0:T(8,128)(2,1)} %get-tuple-element.81), calls=%async_computation.1 | async-start | bytes 1048576 | tf_op jit(solution)/shard_map/all_to_all | solution.py:249
  59.7 5.2 %collective-permute-start.3 = (bf16[64,32,128]{2,1,0:T(8,128)(2,1)S(1)}, bf16[64,32,128]{2,1,0:T(8,128)(2,1)S(1)}, u32[]{:S(2)}, u32[]{:S(2)}) collective-permute-start(bf16[64,32,128]{2,1,0:T(8,128)(2,1)S(1)} %bitcast.65), channel_id=1, source_target_pairs={{0,1},{1,0},{2,3},{3,2},{4,5},{5,4},{6,7},{7,6},{8,9},{9,8},{10,11... | collective-permute-start | bytes 1572872 | tf_op jit(solution)/shard_map/ppermute | solution.py:215
  60.8 15.4 %collective-permute-start.4 = (bf16[64,32,128]{2,1,0:T(8,128)(2,1)S(1)}, bf16[64,32,128]{2,1,0:T(8,128)(2,1)S(1)}, u32[]{:S(2)}, u32[]{:S(2)}) collective-permute-start(bf16[64,32,128]{2,1,0:T(8,128)(2,1)S(1)} %bitcast.66), channel_id=1, source_target_pairs={{0,32},{32,64},{64,96},{1,33},{33,65},{65,97},{2,34},{34,66},{66,9... | collective-permute-start | bytes 1572872 | tf_op jit(solution)/shard_map/ppermute | solution.py:257
  77.0 15.0 %all-to-all-start.2 = ((bf16[16,4,32,128]{3,2,1,0:T(8,128)(2,1)}), bf16[16,4,32,128]{3,2,1,0:T(8,128)(2,1)S(1)}, u32[]{:S(2)}, u32[]{:S(2)}) async-start(bf16[16,4,32,128]{3,2,1,0:T(8,128)(2,1)} %get-tuple-element.87), calls=%async_computation.2 | async-start | bytes 1048576 | tf_op jit(solution)/shard_map/all_to_all | solution.py:249
  92.0 5.2 %collective-permute-start.6 = (bf16[64,32,128]{2,1,0:T(8,128)(2,1)S(1)}, bf16[64,32,128]{2,1,0:T(8,128)(2,1)S(1)}, u32[]{:S(2)}, u32[]{:S(2)}) collective-permute-start(bf16[64,32,128]{2,1,0:T(8,128)(2,1)S(1)} %bitcast.68), channel_id=1, source_target_pairs={{0,1},{1,0},{2,3},{3,2},{4,5},{5,4},{6,7},{7,6},{8,9},{9,8},{10,11... | collective-permute-start | bytes 1572872 | tf_op jit(solution)/shard_map/ppermute | solution.py:215
  93.1 15.4 %collective-permute-start.7 = (bf16[64,32,128]{2,1,0:T(8,128)(2,1)S(1)}, bf16[64,32,128]{2,1,0:T(8,128)(2,1)S(1)}, u32[]{:S(2)}, u32[]{:S(2)}) collective-permute-start(bf16[64,32,128]{2,1,0:T(8,128)(2,1)S(1)} %bitcast.69), channel_id=1, source_target_pairs={{0,32},{32,64},{64,96},{1,33},{33,65},{65,97},{2,34},{34,66},{66,9... | collective-permute-start | bytes 1572872 | tf_op jit(solution)/shard_map/ppermute | solution.py:257
  109.3 15.0 %all-to-all-start.3 = ((bf16[16,4,32,128]{3,2,1,0:T(8,128)(2,1)}), bf16[16,4,32,128]{3,2,1,0:T(8,128)(2,1)S(1)}, u32[]{:S(2)}, u32[]{:S(2)}) async-start(bf16[16,4,32,128]{3,2,1,0:T(8,128)(2,1)} %get-tuple-element.93), calls=%async_computation.3 | async-start | bytes 1048576 | tf_op jit(solution)/shard_map/all_to_all | solution.py:249
  124.2 5.4 %collective-permute-start.9 = (bf16[64,32,128]{2,1,0:T(8,128)(2,1)S(1)}, bf16[64,32,128]{2,1,0:T(8,128)(2,1)S(1)}, u32[]{:S(2)}, u32[]{:S(2)}) collective-permute-start(bf16[64,32,128]{2,1,0:T(8,128)(2,1)S(1)} %bitcast.71), channel_id=1, source_target_pairs={{0,1},{1,0},{2,3},{3,2},{4,5},{5,4},{6,7},{7,6},{8,9},{9,8},{10,11... | collective-permute-start | bytes 1572872 | tf_op jit(solution)/shard_map/ppermute | solution.py:215
  125.3 15.4 %collective-permute-start.10 = (bf16[64,32,128]{2,1,0:T(8,128)(2,1)S(1)}, bf16[64,32,128]{2,1,0:T(8,128)(2,1)S(1)}, u32[]{:S(2)}, u32[]{:S(2)}) collective-permute-start(bf16[64,32,128]{2,1,0:T(8,128)(2,1)S(1)} %bitcast.72), channel_id=1, source_target_pairs={{0,32},{32,64},{64,96},{1,33},{33,65},{65,97},{2,34},{34,66},{66,9... | collective-permute-start | bytes 1572872 | tf_op jit(solution)/shard_map/ppermute | solution.py:257
  141.5 15.0 %all-to-all-start.4 = ((bf16[16,4,32,128]{3,2,1,0:T(8,128)(2,1)}), bf16[16,4,32,128]{3,2,1,0:T(8,128)(2,1)S(1)}, u32[]{:S(2)}, u32[]{:S(2)}) async-start(bf16[16,4,32,128]{3,2,1,0:T(8,128)(2,1)} %get-tuple-element.99), calls=%async_computation.4 | async-start | bytes 1048576 | tf_op jit(solution)/shard_map/all_to_all | solution.py:249
  156.5 5.2 %collective-permute-start.12 = (bf16[64,32,128]{2,1,0:T(8,128)(2,1)S(1)}, bf16[64,32,128]{2,1,0:T(8,128)(2,1)S(1)}, u32[]{:S(2)}, u32[]{:S(2)}) collective-permute-start(bf16[64,32,128]{2,1,0:T(8,128)(2,1)S(1)} %bitcast.74), channel_id=1, source_target_pairs={{0,1},{1,0},{2,3},{3,2},{4,5},{5,4},{6,7},{7,6},{8,9},{9,8},{10,11... | collective-permute-start | bytes 1572872 | tf_op jit(solution)/shard_map/ppermute | solution.py:215
  157.6 15.4 %collective-permute-start.13 = (bf16[64,32,128]{2,1,0:T(8,128)(2,1)S(1)}, bf16[64,32,128]{2,1,0:T(8,128)(2,1)S(1)}, u32[]{:S(2)}, u32[]{:S(2)}) collective-permute-start(bf16[64,32,128]{2,1,0:T(8,128)(2,1)S(1)} %bitcast.75), channel_id=1, source_target_pairs={{0,32},{32,64},{64,96},{1,33},{33,65},{65,97},{2,34},{34,66},{66,9... | collective-permute-start | bytes 1572872 | tf_op jit(solution)/shard_map/ppermute | solution.py:257
  173.8 15.0 %all-to-all-start.5 = ((bf16[16,4,32,128]{3,2,1,0:T(8,128)(2,1)}), bf16[16,4,32,128]{3,2,1,0:T(8,128)(2,1)S(1)}, u32[]{:S(2)}, u32[]{:S(2)}) async-start(bf16[16,4,32,128]{3,2,1,0:T(8,128)(2,1)} %get-tuple-element.105), calls=%async_computation.5 | async-start | bytes 1048576 | tf_op jit(solution)/shard_map/all_to_all | solution.py:249
  188.7 5.2 %collective-permute-start.15 = (bf16[64,32,128]{2,1,0:T(8,128)(2,1)S(1)}, bf16[64,32,128]{2,1,0:T(8,128)(2,1)S(1)}, u32[]{:S(2)}, u32[]{:S(2)}) collective-permute-start(bf16[64,32,128]{2,1,0:T(8,128)(2,1)S(1)} %bitcast.77), channel_id=1, source_target_pairs={{0,1},{1,0},{2,3},{3,2},{4,5},{5,4},{6,7},{7,6},{8,9},{9,8},{10,11... | collective-permute-start | bytes 1572872 | tf_op jit(solution)/shard_map/ppermute | solution.py:215
  189.8 15.4 %collective-permute-start.16 = (bf16[64,32,128]{2,1,0:T(8,128)(2,1)S(1)}, bf16[64,32,128]{2,1,0:T(8,128)(2,1)S(1)}, u32[]{:S(2)}, u32[]{:S(2)}) collective-permute-start(bf16[64,32,128]{2,1,0:T(8,128)(2,1)S(1)} %bitcast.78), channel_id=1, source_target_pairs={{0,32},{32,64},{64,96},{1,33},{33,65},{65,97},{2,34},{34,66},{66,9... | collective-permute-start | bytes 1572872 | tf_op jit(solution)/shard_map/ppermute | solution.py:257
  206.0 15.0 %all-to-all-start.6 = ((bf16[16,4,32,128]{3,2,1,0:T(8,128)(2,1)}), bf16[16,4,32,128]{3,2,1,0:T(8,128)(2,1)S(1)}, u32[]{:S(2)}, u32[]{:S(2)}) async-start(bf16[16,4,32,128]{3,2,1,0:T(8,128)(2,1)} %get-tuple-element.111), calls=%async_computation.6 | async-start | bytes 1048576 | tf_op jit(solution)/shard_map/all_to_all | solution.py:249
  221.0 5.2 %collective-permute-start.18 = (bf16[64,32,128]{2,1,0:T(8,128)(2,1)S(1)}, bf16[64,32,128]{2,1,0:T(8,128)(2,1)S(1)}, u32[]{:S(2)}, u32[]{:S(2)}) collective-permute-start(bf16[64,32,128]{2,1,0:T(8,128)(2,1)S(1)} %bitcast.80), channel_id=1, source_target_pairs={{0,1},{1,0},{2,3},{3,2},{4,5},{5,4},{6,7},{7,6},{8,9},{9,8},{10,11... | collective-permute-start | bytes 1572872 | tf_op jit(solution)/shard_map/ppermute | solution.py:215
  222.1 15.4 %collective-permute-start.19 = (bf16[64,32,128]{2,1,0:T(8,128)(2,1)S(1)}, bf16[64,32,128]{2,1,0:T(8,128)(2,1)S(1)}, u32[]{:S(2)}, u32[]{:S(2)}) collective-permute-start(bf16[64,32,128]{2,1,0:T(8,128)(2,1)S(1)} %bitcast.81), channel_id=1, source_target_pairs={{0,32},{32,64},{64,96},{1,33},{33,65},{65,97},{2,34},{34,66},{66,9... | collective-permute-start | bytes 1572872 | tf_op jit(solution)/shard_map/ppermute | solution.py:257
  238.3 15.0 %all-to-all-start.7 = ((bf16[16,4,32,128]{3,2,1,0:T(8,128)(2,1)}), bf16[16,4,32,128]{3,2,1,0:T(8,128)(2,1)S(1)}, u32[]{:S(2)}, u32[]{:S(2)}) async-start(bf16[16,4,32,128]{3,2,1,0:T(8,128)(2,1)} %get-tuple-element.117), calls=%async_computation.7 | async-start | bytes 1048576 | tf_op jit(solution)/shard_map/all_to_all | solution.py:249
  253.2 5.2 %collective-permute-start.21 = (bf16[64,32,128]{2,1,0:T(8,128)(2,1)S(1)}, bf16[64,32,128]{2,1,0:T(8,128)(2,1)S(1)}, u32[]{:S(2)}, u32[]{:S(2)}) collective-permute-start(bf16[64,32,128]{2,1,0:T(8,128)(2,1)S(1)} %bitcast.83), channel_id=1, source_target_pairs={{0,1},{1,0},{2,3},{3,2},{4,5},{5,4},{6,7},{7,6},{8,9},{9,8},{10,11... | collective-permute-start | bytes 1572872 | tf_op jit(solution)/shard_map/ppermute | solution.py:215
  254.3 15.4 %collective-permute-start.22 = (bf16[64,32,128]{2,1,0:T(8,128)(2,1)S(1)}, bf16[64,32,128]{2,1,0:T(8,128)(2,1)S(1)}, u32[]{:S(2)}, u32[]{:S(2)}) collective-permute-start(bf16[64,32,128]{2,1,0:T(8,128)(2,1)S(1)} %bitcast.84), channel_id=1, source_target_pairs={{0,32},{32,64},{64,96},{1,33},{33,65},{65,97},{2,34},{34,66},{66,9... | collective-permute-start | bytes 1572872 | tf_op jit(solution)/shard_map/ppermute | solution.py:257
  269.8 4.6 %collective-permute-start.23 = (bf16[64,32,128]{2,1,0:T(8,128)(2,1)S(1)}, bf16[64,32,128]{2,1,0:T(8,128)(2,1)S(1)}, u32[]{:S(2)}, u32[]{:S(2)}) collective-permute-start(bf16[64,32,128]{2,1,0:T(8,128)(2,1)S(1)} %collective-permute-done.22.mine_ref), channel_id=1, source_target_pairs={{0,1},{1,0},{2,3},{3,2},{4,5},{5,4},{6,7},{7,6},{8,9},{9,8},{10,11... | collective-permute-start | bytes 1572872 | tf_op jit(solution)/shard_map/ppermute | solution.py:215
  270.5 15.0 %all-to-all-start.8 = ((bf16[16,4,32,128]{3,2,1,0:T(8,128)(2,1)}), bf16[16,4,32,128]{3,2,1,0:T(8,128)(2,1)S(1)}, u32[]{:S(2)}, u32[]{:S(2)}) async-start(bf16[16,4,32,128]{3,2,1,0:T(8,128)(2,1)} %get-tuple-element.123), calls=%async_computation.8 | async-start | bytes 1048576 | tf_op jit(solution)/shard_map/all_to_all | solution.py:249
  285.5 5.2 %collective-permute-start.24 = (bf16[64,32,128]{2,1,0:T(8,128)(2,1)S(1)}, bf16[64,32,128]{2,1,0:T(8,128)(2,1)S(1)}, u32[]{:S(2)}, u32[]{:S(2)}) collective-permute-start(bf16[64,32,128]{2,1,0:T(8,128)(2,1)S(1)} %bitcast.86), channel_id=1, source_target_pairs={{0,1},{1,0},{2,3},{3,2},{4,5},{5,4},{6,7},{7,6},{8,9},{9,8},{10,11... | collective-permute-start | bytes 1572872 | tf_op jit(solution)/shard_map/ppermute | solution.py:215
  286.6 15.4 %collective-permute-start.25 = (bf16[64,32,128]{2,1,0:T(8,128)(2,1)S(1)}, bf16[64,32,128]{2,1,0:T(8,128)(2,1)S(1)}, u32[]{:S(2)}, u32[]{:S(2)}) collective-permute-start(bf16[64,32,128]{2,1,0:T(8,128)(2,1)S(1)} %bitcast.87), channel_id=1, source_target_pairs={{0,32},{32,64},{64,96},{1,33},{33,65},{65,97},{2,34},{34,66},{66,9... | collective-permute-start | bytes 1572872 | tf_op jit(solution)/shard_map/ppermute | solution.py:257
  302.8 15.0 %all-to-all-start.9 = ((bf16[16,4,32,128]{3,2,1,0:T(8,128)(2,1)}), bf16[16,4,32,128]{3,2,1,0:T(8,128)(2,1)S(1)}, u32[]{:S(2)}, u32[]{:S(2)}) async-start(bf16[16,4,32,128]{3,2,1,0:T(8,128)(2,1)} %get-tuple-element.129), calls=%async_computation.9 | async-start | bytes 1048576 | tf_op jit(solution)/shard_map/all_to_all | solution.py:249
  317.7 5.3 %collective-permute-start.27 = (bf16[64,32,128]{2,1,0:T(8,128)(2,1)S(1)}, bf16[64,32,128]{2,1,0:T(8,128)(2,1)S(1)}, u32[]{:S(2)}, u32[]{:S(2)}) collective-permute-start(bf16[64,32,128]{2,1,0:T(8,128)(2,1)S(1)} %bitcast.57), channel_id=1, source_target_pairs={{0,1},{1,0},{2,3},{3,2},{4,5},{5,4},{6,7},{7,6},{8,9},{9,8},{10,11... | collective-permute-start | bytes 1572872 | tf_op jit(solution)/shard_map/ppermute | solution.py:215
  318.8 15.4 %collective-permute-start.28 = (bf16[64,32,128]{2,1,0:T(8,128)(2,1)S(1)}, bf16[64,32,128]{2,1,0:T(8,128)(2,1)S(1)}, u32[]{:S(2)}, u32[]{:S(2)}) collective-permute-start(bf16[64,32,128]{2,1,0:T(8,128)(2,1)S(1)} %bitcast.58), channel_id=1, source_target_pairs={{0,32},{32,64},{64,96},{1,33},{33,65},{65,97},{2,34},{34,66},{66,9... | collective-permute-start | bytes 1572872 | tf_op jit(solution)/shard_map/ppermute | solution.py:257
  335.0 15.0 %all-to-all-start.10 = ((bf16[16,4,32,128]{3,2,1,0:T(8,128)(2,1)}), bf16[16,4,32,128]{3,2,1,0:T(8,128)(2,1)S(1)}, u32[]{:S(2)}, u32[]{:S(2)}) async-start(bf16[16,4,32,128]{3,2,1,0:T(8,128)(2,1)} %get-tuple-element.135), calls=%async_computation.10 | async-start | bytes 1048576 | tf_op jit(solution)/shard_map/all_to_all | solution.py:249
  (37 other events, 119.3 us)

commit v3 on v2

v3 whole, which is shorter than its diff:
```python
import functools
import math

import jax
import jax.numpy as jnp
from jax import lax
from jax.experimental import pallas as pl
from jax.experimental.pallas import tpu as pltpu
from jax.sharding import Mesh
from jax.sharding import PartitionSpec as P

LAG = 2
F32 = jnp.float32
BF16 = jnp.bfloat16
WIDTH = ("y", "x", "core")
MIB = 2**20


def vmem():
    return pl.BlockSpec(memory_space=pltpu.VMEM)


def smem():
    return pl.BlockSpec(memory_space=pltpu.SMEM)


def held(x):
    return pltpu.with_memory_space_constraint(x, pltpu.VMEM)


def hbm():
    return pl.BlockSpec(memory_space=pltpu.HBM)


def unmoved(x):
    return pltpu.with_memory_space_constraint(x, pltpu.HBM)


def group(ref, j, size):
    return ref.at[pl.ds(size * j, size)]


def stream(w_hbm, w_ref, loaded):
    groups = loaded.shape[0]
    size = w_ref.shape[0] // groups
    copies = [
        pltpu.make_async_copy(group(w_hbm, j, size), group(w_ref, j, size), loaded.at[j])
        for j in range(groups)
    ]
    for copy in copies:
        copy.start()
    return copies


def load_kernel(w_ref, after_ref, out_ref, loaded):
    for copy in stream(w_ref, out_ref, loaded):
        copy.wait()


def load(w, after):
    return pl.pallas_call(
        load_kernel,
        out_shape=pltpu.VMEM(w.shape, w.dtype),
        in_specs=[hbm(), pl.BlockSpec(memory_space=pl.ANY)],
        out_specs=vmem(),
        scratch_shapes=[pltpu.SemaphoreType.DMA((8,))],
        compiler_params=pltpu.CompilerParams(vmem_limit_bytes=8 * MIB),
        cost_estimate=pl.CostEstimate(flops=0, bytes_accessed=2 * w.size, transcendentals=0),
        name="load_weights",
    )(unmoved(w), after)


def row_sums(pick, index_ref, w_ref, row):
    blocks = w_ref.shape[1]
    edge = w_ref.shape[2]
    picked = jnp.concatenate([pick(index_ref[row * blocks + k]) for k in range(blocks)], axis=1)
    return jnp.dot(picked, w_ref[row].reshape(blocks * edge, edge), preferred_element_type=F32)


def from_halves(mine_ref, other_ref):
    half = mine_ref.shape[0]

    def pick(i):
        return jnp.where(
            i < half, mine_ref[jnp.minimum(i, half - 1)], other_ref[jnp.maximum(i - half, 0)]
        )

    return pick


def from_rows(rows_ref, edge):
    return lambda i: rows_ref[:, pl.ds(pl.multiple_of(i * edge, edge), edge)]


def input_kernel(tick, step_count, *refs):
    layer_ref, index_ref = refs[:2]
    fresh_ref = refs[2] if tick < step_count else None
    lower_refs = refs[-5:-3] if tick >= LAG else None
    w_ref, bias_ref, out_ref = refs[-3:]
    edge = w_ref.shape[2]
    row_count = out_ref.shape[1]

    def fill(pick):
        for row in range(w_ref.shape[0]):
            bias = jnp.broadcast_to(bias_ref[row], (row_count, edge))
            out_ref[row] = row_sums(pick, index_ref, w_ref, row) + bias

    step = tick - LAG * layer_ref[0]
    if fresh_ref is not None:
        @pl.when(layer_ref[0] == 0)
        def _():
            fill(from_rows(fresh_ref, edge))

    if lower_refs is not None:
        @pl.when((layer_ref[0] != 0) & (step >= 0) & (step < step_count))
        def _():
            fill(from_halves(*lower_refs))


def input_sums(tick, layer, index, fresh, lower, w, bias, step_count):
    rows = w.shape[0]
    x = [held(part) for part in ((fresh,) if tick < step_count else ()) + lower]
    row_count = (fresh if fresh is not None else lower[0]).shape[-2]
    return pl.pallas_call(
        functools.partial(input_kernel, tick, step_count),
        out_shape=pltpu.VMEM((rows, row_count, w.shape[3]), F32),
        in_specs=[smem(), smem()] + [vmem()] * (len(x) + 2),
        out_specs=vmem(),
        compiler_params=pltpu.CompilerParams(vmem_limit_bytes=8 * MIB),
        cost_estimate=pl.CostEstimate(flops=2 * w.size * 32, bytes_accessed=w.size, transcendentals=0),
        name="input_sums",
    )(layer, index, *x, held(w), held(bias))


def gates_to_state(sums, before):
    cell = jax.nn.sigmoid(sums[1]) * before + jax.nn.sigmoid(sums[0]) * jnp.tanh(sums[2])
    output = jax.nn.sigmoid(sums[3]) * jnp.tanh(cell)
    return cell, output.astype(BF16)


class Sender:
    def __init__(self, send_out, spread_ref, sent):
        self.send_out, self.spread_ref, self.sent = send_out, spread_ref, sent
        self.copies = []

    def put(self, j, output):
        for peer in range(self.spread_ref.shape[1]):
            self.spread_ref[j, peer] = output
        copy = pltpu.make_async_copy(self.spread_ref.at[j], self.send_out.at[:, j], self.sent.at[j])
        copy.start()
        self.copies.append(copy)

    def finish(self):
        for copy in self.copies:
            copy.wait()


def send_scratch(cell_shape, peers):
    per_device, row_count, edge = cell_shape
    return [pltpu.VMEM((per_device, peers, row_count, edge), BF16), pltpu.SemaphoreType.DMA((per_device,))]


def state_out(cell_shape, peers):
    per_device, row_count, edge = cell_shape
    return (
        pltpu.VMEM(cell_shape, F32),
        jax.ShapeDtypeStruct((row_count, per_device * edge), BF16),
        pltpu.HBM((peers, *cell_shape), BF16),
    )


def first_kernel(layer_ref, index_ref, inputs_ref, w_hbm, bias_ref, cell_out, rows_out, send_out, next_out, fresh_ref, w_out, arrived, loaded, spread_ref, sent):
    per_device, row_count, edge = cell_out.shape
    fresh = pltpu.make_async_copy(inputs_ref.at[0], fresh_ref, arrived.at[0])
    later = pltpu.make_async_copy(inputs_ref.at[1], next_out, arrived.at[1])
    fresh.start()
    copies = stream(w_hbm, w_out, loaded)
    later.start()

    @pl.when(layer_ref[0] == 0)
    def _():
        fresh.wait()
        sender = Sender(send_out, spread_ref, sent)
        pick = from_rows(fresh_ref, edge)
        for j, copy in enumerate(copies):
            copy.wait()
            sums = [
                row_sums(pick, index_ref, w_out, 4 * j + g) + jnp.broadcast_to(bias_ref[4 * j + g], (row_count, edge))
                for g in range(4)
            ]
            cell_out[j], output = gates_to_state(sums, jnp.zeros((row_count, edge), F32))
            rows_out[:, j * edge:(j + 1) * edge] = output
            sender.put(j, output)
        sender.finish()

    @pl.when(layer_ref[0] != 0)
    def _():
        idle = Sender(send_out, spread_ref, sent)
        for j in range(per_device):
            idle.put(j, jnp.zeros((row_count, edge), BF16))
        for ref in (cell_out, rows_out):
            ref[...] = jnp.zeros_like(ref)
        idle.finish()
        fresh.wait()
        for copy in copies:
            copy.wait()

    later.wait()


def first_step(layer, index, inputs, w, bias, per_device, peers):
    _, row_count, hidden = inputs.shape
    edge = w.shape[2]
    return pl.pallas_call(
        first_kernel,
        out_shape=state_out((per_device, row_count, edge), peers)
        + (pltpu.VMEM((row_count, hidden), BF16),),
        in_specs=[smem(), smem(), hbm(), hbm(), vmem()],
        out_specs=(vmem(), vmem(), hbm(), vmem()),
        scratch_shapes=[
            pltpu.VMEM((row_count, hidden), BF16),
            pltpu.VMEM(w.shape, w.dtype),
            pltpu.SemaphoreType.DMA((2,)),
            pltpu.SemaphoreType.DMA((per_device,)),
            *send_scratch((per_device, row_count, edge), peers),
        ],
        compiler_params=pltpu.CompilerParams(vmem_limit_bytes=12 * MIB),
        name="first_step",
    )(layer, index, unmoved(inputs), unmoved(w), held(bias))


def state_kernel(tick, step_count, layer_ref, index_ref, inputs_ref, mine_ref, other_ref, w_ref, partial_ref, cell_ref, cell_out, rows_out, send_out, *rest):
    *fetch, spread_ref, sent = rest
    step = tick - LAG * layer_ref[0]
    active = (step >= 0) & (step < step_count)
    edge = cell_ref.shape[2]
    is_first = layer_ref[0] == 0
    if fetch:
        next_out, arrived = fetch
        later = pltpu.make_async_copy(inputs_ref.at[tick + 1], next_out, arrived)
        pl.when(is_first)(later.start)

    @pl.when(active)
    def _():
        pick = from_halves(mine_ref, other_ref)
        sender = Sender(send_out, spread_ref, sent)
        for j in range(cell_ref.shape[0]):
            sums = [partial_ref[4 * j + g] + row_sums(pick, index_ref, w_ref, 4 * j + g) for g in range(4)]
            cell_out[j], output = gates_to_state(sums, cell_ref[j])
            rows_out[:, j * edge:(j + 1) * edge] = output
            sender.put(j, output)
        sender.finish()

    @pl.when(jnp.logical_not(active))
    def _():
        idle = Sender(send_out, spread_ref, sent)
        for j in range(cell_ref.shape[0]):
            idle.put(j, jnp.zeros(cell_ref.shape[1:], BF16))
        cell_out[...] = cell_ref[...]
        rows_out[...] = jnp.zeros_like(rows_out)
        idle.finish()

    if fetch:
        pl.when(is_first)(later.wait)


def state_step(tick, layer, index, state, w, partial, cell, inputs, peers):
    step_count, row_count, hidden = inputs.shape
    fetch = tick + 1 < step_count
    outs = pl.pallas_call(
        functools.partial(state_kernel, tick, step_count),
        out_shape=state_out(cell.shape, peers) + ((pltpu.VMEM((row_count, hidden), BF16),) if fetch else ()),
        in_specs=[smem(), smem(), hbm()] + [vmem()] * 5,
        out_specs=(vmem(), vmem(), hbm()) + (vmem(),) * fetch,
        scratch_shapes=[pltpu.SemaphoreType.DMA] * fetch + send_scratch(cell.shape, peers),
        compiler_params=pltpu.CompilerParams(vmem_limit_bytes=8 * MIB),
        cost_estimate=pl.CostEstimate(flops=2 * w.size * 32, bytes_accessed=w.size, transcendentals=0),
        name="state_step",
    )(layer, index, unmoved(inputs), *[held(part) for part in state], held(w), partial, cell)
    return outs if fetch else (*outs, None)


def exchange(x, target):
    sizes = [lax.axis_size(axis) for axis in ("pipe",) + WIDTH]
    route = []
    for source in range(math.prod(sizes)):
        place, rest = [], source
        for size in reversed(sizes):
            place.insert(0, rest % size)
            rest //= size
        to = 0
        for size, at in zip(sizes, target(*place)):
            to = to * size + at % size
        route.append((source, to))
    return lax.ppermute(x, ("pipe",) + WIDTH, route)


def other_core(x):
    return exchange(x, lambda layer, y, x_at, core: (layer, y, x_at, 1 - core))


def upward(x):
    return exchange(x, lambda layer, y, x_at, core: (layer + 1, y, x_at, core))


def body(inputs, in_blocks, rec_blocks, in_cols, rec_cols, bias):
    layer = lax.axis_index("pipe")
    layers = lax.axis_size("pipe")
    core = lax.axis_index("core")
    step_count, row_count, hidden = inputs.shape
    _, per_device, gates, kept, edge, _ = in_blocks.shape
    total = hidden // edge
    half = total // 2
    rows = per_device * gates

    chips = lax.axis_size("y") * lax.axis_size("x")

    def place(cols):
        device = cols // per_device
        return ((device % 2) ^ core) * half + (device // 2) * per_device + cols % per_device

    in_flat = in_cols.reshape(-1)
    in_index = jnp.where(layer == 0, in_flat, place(in_flat))
    rec_index = place(rec_cols.reshape(-1))
    offsets = bias[0].reshape(gates, per_device, edge).transpose(1, 0, 2).reshape(rows, 1, edge)
    layer_ref = layer.astype(jnp.int32).reshape(1)
    w_in = in_blocks.reshape(rows, kept, edge, edge)
    w_rec = rec_blocks.reshape(rows, kept, edge, edge)

    tick_count = step_count + LAG * (layers - 1)
    steps = [tick - LAG * layer for tick in range(tick_count)]
    fed = [(layer > 0) & (step >= 0) & (step < step_count) for step in steps]
    layer_ref, fed, in_index, rec_index = lax.optimization_barrier((layer_ref, fed, in_index, rec_index))
    cell, out_rows, send, fresh = first_step(layer_ref, in_index, inputs, w_in, offsets, per_device, chips)
    arrived = {}
    outputs = [out_rows]
    for tick in range(1, tick_count):
        mine = lax.all_to_all(send, ("y", "x"), 0, 0).reshape(half, row_count, edge)
        lower = ()
        if tick >= LAG:
            low = arrived[tick - LAG]
            lower = (low, lax.cond(fed[tick], other_core, jnp.zeros_like, low))
        partial = input_sums(tick, layer_ref, in_index, fresh, lower, w_in, offsets, step_count)
        mine, partial = lax.optimization_barrier((mine, partial))
        other = other_core(mine)
        if tick <= tick_count - LAG:
            arrived[tick - 1] = upward(mine)
        state = (mine, other)
        cell, out_rows, send, fresh = state_step(tick, layer_ref, rec_index, state, load(w_rec, mine), partial, cell, inputs, chips)
        outputs.append(out_rows)
    sequence = lax.dynamic_slice_in_dim(jnp.stack(outputs), LAG * layer, step_count, 0)
    cells = cell.transpose(1, 0, 2).reshape(row_count, per_device * edge)
    return sequence[None], cells[None]


def solution(mesh):
    layers, width = mesh.devices.shape
    grid = Mesh(mesh.devices.reshape(layers, 4, width // 8, 2), ("pipe",) + WIDTH)
    return jax.shard_map(
        body,
        mesh=grid,
        in_specs=(
            P(),
            P("pipe", WIDTH, None, None, None, None),
            P("pipe", WIDTH, None, None, None, None),
            P("pipe", WIDTH, None, None),
            P("pipe", WIDTH, None, None),
            P("pipe", None, WIDTH),
        ),
        out_specs=(P("pipe", None, None, WIDTH), P("pipe", None, WIDTH)),
        check_vma=False,
    )
```

time: 361 us -> 245 us (0.68)
  waiting for transfers between devices: 145 us -> 73.3 us
  starting transfers between devices: 105 us -> 68.5 us
  local copies, waits for them, and re-layouts: 55.1 us -> 36.5 us
  Pallas kernels: 52.2 us -> 63.4 us
    all_to_all x11, waiting for transfers between devices: 78.7 us -> 11 us  [body(): mine = lax.all_to_all(send, ('y', 'x'), 0, 0).reshape(half, row_count, edge)]
    ppermute x31 -> x21, starting transfers between devices: 61.6 us -> 25.1 us  [exchange(): return lax.ppermute(x, ('pipe',) + WIDTH, route)]
    unnamed x65 -> x37, local copies, waits for them, and re-layouts: 52.8 us -> 24.8 us
    pallas_call x1 -> x11, Pallas kernels: 2.19 us -> 24.4 us  [load(): pl.pallas_call(load_kernel, out_shape=pltpu.VMEM(w.shape, w.dtype), in_sp...]
    pallas_call x23, Pallas kernels: 50 us -> 39 us  [the longest x11 19.3 us: state_step(): pl.pallas_call(functools.partial(state_kernel, tick, step_count), out_sha...]
    another operation x0 -> x10, local copies, waits for them, and re-layouts: none -> 8.73 us
    ppermute x31 -> x21, waiting for transfers between devices: 65.8 us -> 62.3 us  [exchange(): return lax.ppermute(x, ('pipe',) + WIDTH, route)]
  transfers between devices with their start and end apart: 42 -> 32, of which waited for: 22 -> 19; matrix products, arithmetic and copies ran while one was open for 0% -> 4% of each run, Pallas kernels for 13% -> 24%
where the time goes in v3:
time: 245 us; the launch traced here: 243 us
  waiting for transfers between devices  73.3 us (30%)
  starting transfers between devices  68.5 us (28%)
  Pallas kernels  63.4 us (26%)
  local copies, waits for them, and re-layouts  36.5 us (15%)
    ppermute x21, waiting for transfers between devices, exchange(): return lax.ppermute(x, ('pipe',) + WIDTH, route)  62.3 us
    all_to_all x11, starting transfers between devices, body(): mine = lax.all_to_all(send, ('y', 'x'), 0, 0).reshape(half, row_count, edge)  43.4 us
    ppermute x21, starting transfers between devices, exchange(): return lax.ppermute(x, ('pipe',) + WIDTH, route)  25.1 us
    unnamed x37, local copies, waits for them, and re-layouts  24.8 us
    pallas_call x11, Pallas kernels, load(): pl.pallas_call(load_kernel, out_shape=pltpu.VMEM(w.shape, w.dtype), in_sp...  24.4 us
    pallas_call x11, Pallas kernels, state_step(): pl.pallas_call(functools.partial(state_kernel, tick, step_count), out_sha...  19.3 us
    pallas_call x11, Pallas kernels, input_sums(): pl.pallas_call(functools.partial(input_kernel, tick, step_count), out_sha...  15.3 us
    all_to_all x11, waiting for transfers between devices, body(): mine = lax.all_to_all(send, ('y', 'x'), 0, 0).reshape(half, row_count, edge)  11 us
  transfers between devices with their start and end apart: 32, of which 19 were waited for; matrix products, arithmetic and copies ran while one was open for 4% of the time, Pallas kernels for 24%

profile of v3, /device:TPU:1, one launch (start us, length us, event | category | flops | bytes accessed | tf_op | source)
XLA Modules:
  0.0 243.1 jit_solution(7517368950100843761)
XLA Ops:
  3.1 4.4 %first_step.1 = (f32[4,32,128]{2,1,0:T(8,128)S(1)}, bf16[32,512]{1,0:T(8,128)(2,1)S(1)}, bf16[16,4,32,128]{3,2,1,0:T(8,128)(2,1)}, bf16[32,16384]{1,0:T(8,128)(2,1)S(1)}) custom-call(s32[1]{0:T(128)} %bitcast.layer_ref.refs_0_, s32[128]{0:T(128)S(1)} %get-tuple-element.118.index_ref.refs_1_, bf16[6,32,16384]{2,1,0:T(8,128)(2,1)} %inputs_ref.23, ...), custom_call_target="tpu_custom_call" | custom-call | tf_op jit(solution)/shard_map/first_step/pallas_call | solution.py:214
  7.5 7.6 %all-to-all-start = ((bf16[16,4,32,128]{3,2,1,0:T(8,128)(2,1)}), bf16[16,4,32,128]{3,2,1,0:T(8,128)(2,1)S(1)}, u32[]{:S(2)}, u32[]{:S(2)}) async-start(bf16[16,4,32,128]{3,2,1,0:T(8,128)(2,1)} %get-tuple-element.121), calls=%async_computation | async-start | bytes 1048576 | tf_op jit(solution)/shard_map/all_to_all | solution.py:338
  18.6 7.0 %all-to-all-done = bf16[16,4,32,128]{3,2,1,0:T(8,128)(2,1)S(1)} async-done(((bf16[16,4,32,128]{3,2,1,0:T(8,128)(2,1)}), bf16[16,4,32,128]{3,2,1,0:T(8,128)(2,1)S(1)}, u32[]{:S(2)}, u32[]{:S(2)}) %all-to-all-start) | async-done | bytes 524320 | tf_op jit(solution)/shard_map/all_to_all | solution.py:338
  28.4 2.2 load_weights.11.w_ref
  32.8 3.6 %all-to-all-start.1 = ((bf16[16,4,32,128]{3,2,1,0:T(8,128)(2,1)}), bf16[16,4,32,128]{3,2,1,0:T(8,128)(2,1)S(1)}, u32[]{:S(2)}, u32[]{:S(2)}) async-start(bf16[16,4,32,128]{3,2,1,0:T(8,128)(2,1)} %get-tuple-element.127), calls=%async_computation.1 | async-start | bytes 1048576 | tf_op jit(solution)/shard_map/all_to_all | solution.py:338
  36.4 6.4 %collective-permute-done.11.refs_3_ = bf16[64,32,128]{2,1,0:T(8,128)(2,1)S(1)} collective-permute-done((bf16[64,32,128]{2,1,0:T(8,128)(2,1)S(1)}, bf16[64,32,128]{2,1,0:T(8,128)(2,1)S(1)}, u32[]{:S(2)}, u32[]{:S(2)}) %collective-permute-start.11) | collective-permute-done | bytes 524320 | tf_op jit(solution)/shard_map/ppermute | solution.py:295
  49.8 2.2 load_weights.12.w_ref
  54.1 3.6 %all-to-all-start.2 = ((bf16[16,4,32,128]{3,2,1,0:T(8,128)(2,1)}), bf16[16,4,32,128]{3,2,1,0:T(8,128)(2,1)S(1)}, u32[]{:S(2)}, u32[]{:S(2)}) async-start(bf16[16,4,32,128]{3,2,1,0:T(8,128)(2,1)} %get-tuple-element.134), calls=%async_computation.2 | async-start | bytes 1048576 | tf_op jit(solution)/shard_map/all_to_all | solution.py:338
  57.7 5.9 %collective-permute-done.13.refs_3_ = bf16[64,32,128]{2,1,0:T(8,128)(2,1)S(1)} collective-permute-done((bf16[64,32,128]{2,1,0:T(8,128)(2,1)S(1)}, bf16[64,32,128]{2,1,0:T(8,128)(2,1)S(1)}, u32[]{:S(2)}, u32[]{:S(2)}) %collective-permute-start.13) | collective-permute-done | bytes 524320 | tf_op jit(solution)/shard_map/ppermute | solution.py:295
  71.5 2.2 load_weights.13.w_ref
  75.9 3.6 %all-to-all-start.3 = ((bf16[16,4,32,128]{3,2,1,0:T(8,128)(2,1)}), bf16[16,4,32,128]{3,2,1,0:T(8,128)(2,1)S(1)}, u32[]{:S(2)}, u32[]{:S(2)}) async-start(bf16[16,4,32,128]{3,2,1,0:T(8,128)(2,1)} %get-tuple-element.141), calls=%async_computation.3 | async-start | bytes 1048576 | tf_op jit(solution)/shard_map/all_to_all | solution.py:338
  79.5 5.5 %collective-permute-done.15.refs_3_ = bf16[64,32,128]{2,1,0:T(8,128)(2,1)S(1)} collective-permute-done((bf16[64,32,128]{2,1,0:T(8,128)(2,1)S(1)}, bf16[64,32,128]{2,1,0:T(8,128)(2,1)S(1)}, u32[]{:S(2)}, u32[]{:S(2)}) %collective-permute-start.15) | collective-permute-done | bytes 524320 | tf_op jit(solution)/shard_map/ppermute | solution.py:295
  92.3 2.2 load_weights.14.w_ref
  96.6 3.6 %all-to-all-start.4 = ((bf16[16,4,32,128]{3,2,1,0:T(8,128)(2,1)}), bf16[16,4,32,128]{3,2,1,0:T(8,128)(2,1)S(1)}, u32[]{:S(2)}, u32[]{:S(2)}) async-start(bf16[16,4,32,128]{3,2,1,0:T(8,128)(2,1)} %get-tuple-element.148), calls=%async_computation.4 | async-start | bytes 1048576 | tf_op jit(solution)/shard_map/all_to_all | solution.py:338
  100.2 6.5 %collective-permute-done.17.refs_3_ = bf16[64,32,128]{2,1,0:T(8,128)(2,1)S(1)} collective-permute-done((bf16[64,32,128]{2,1,0:T(8,128)(2,1)S(1)}, bf16[64,32,128]{2,1,0:T(8,128)(2,1)S(1)}, u32[]{:S(2)}, u32[]{:S(2)}) %collective-permute-start.17) | collective-permute-done | bytes 524320 | tf_op jit(solution)/shard_map/ppermute | solution.py:295
  112.8 2.2 load_weights.15.w_ref
  117.2 3.6 %all-to-all-start.5 = ((bf16[16,4,32,128]{3,2,1,0:T(8,128)(2,1)}), bf16[16,4,32,128]{3,2,1,0:T(8,128)(2,1)S(1)}, u32[]{:S(2)}, u32[]{:S(2)}) async-start(bf16[16,4,32,128]{3,2,1,0:T(8,128)(2,1)} %get-tuple-element.155), calls=%async_computation.5 | async-start | bytes 1048576 | tf_op jit(solution)/shard_map/all_to_all | solution.py:338
  120.8 6.7 %collective-permute-done.19.refs_2_ = bf16[64,32,128]{2,1,0:T(8,128)(2,1)S(1)} collective-permute-done((bf16[64,32,128]{2,1,0:T(8,128)(2,1)S(1)}, bf16[64,32,128]{2,1,0:T(8,128)(2,1)S(1)}, u32[]{:S(2)}, u32[]{:S(2)}) %collective-permute-start.19) | collective-permute-done | bytes 524320 | tf_op jit(solution)/shard_map/ppermute | solution.py:295
  134.2 2.2 load_weights.16.w_ref
  137.9 3.6 %all-to-all-start.6 = ((bf16[16,4,32,128]{3,2,1,0:T(8,128)(2,1)}), bf16[16,4,32,128]{3,2,1,0:T(8,128)(2,1)S(1)}, u32[]{:S(2)}, u32[]{:S(2)}) async-start(bf16[16,4,32,128]{3,2,1,0:T(8,128)(2,1)} %get-tuple-element.161), calls=%async_computation.6 | async-start | bytes 1048576 | tf_op jit(solution)/shard_map/all_to_all | solution.py:338
  141.5 6.5 %collective-permute-done.21.refs_2_ = bf16[64,32,128]{2,1,0:T(8,128)(2,1)S(1)} collective-permute-done((bf16[64,32,128]{2,1,0:T(8,128)(2,1)S(1)}, bf16[64,32,128]{2,1,0:T(8,128)(2,1)S(1)}, u32[]{:S(2)}, u32[]{:S(2)}) %collective-permute-start.21) | collective-permute-done | bytes 524320 | tf_op jit(solution)/shard_map/ppermute | solution.py:295
  156.0 2.2 load_weights.17.w_ref
  159.9 3.6 %all-to-all-start.7 = ((bf16[16,4,32,128]{3,2,1,0:T(8,128)(2,1)}), bf16[16,4,32,128]{3,2,1,0:T(8,128)(2,1)S(1)}, u32[]{:S(2)}, u32[]{:S(2)}) async-start(bf16[16,4,32,128]{3,2,1,0:T(8,128)(2,1)} %get-tuple-element.167), calls=%async_computation.7 | async-start | bytes 1048576 | tf_op jit(solution)/shard_map/all_to_all | solution.py:338
  163.5 5.2 %collective-permute-done.23.refs_2_ = bf16[64,32,128]{2,1,0:T(8,128)(2,1)S(1)} collective-permute-done((bf16[64,32,128]{2,1,0:T(8,128)(2,1)S(1)}, bf16[64,32,128]{2,1,0:T(8,128)(2,1)S(1)}, u32[]{:S(2)}, u32[]{:S(2)}) %collective-permute-start.23) | collective-permute-done | bytes 524320 | tf_op jit(solution)/shard_map/ppermute | solution.py:295
  180.6 3.6 %all-to-all-start.8 = ((bf16[16,4,32,128]{3,2,1,0:T(8,128)(2,1)}), bf16[16,4,32,128]{3,2,1,0:T(8,128)(2,1)S(1)}, u32[]{:S(2)}, u32[]{:S(2)}) async-start(bf16[16,4,32,128]{3,2,1,0:T(8,128)(2,1)} %get-tuple-element.173), calls=%async_computation.8 | async-start | bytes 1048576 | tf_op jit(solution)/shard_map/all_to_all | solution.py:338
  184.2 6.5 %collective-permute-done.25.refs_2_ = bf16[64,32,128]{2,1,0:T(8,128)(2,1)S(1)} collective-permute-done((bf16[64,32,128]{2,1,0:T(8,128)(2,1)S(1)}, bf16[64,32,128]{2,1,0:T(8,128)(2,1)S(1)}, u32[]{:S(2)}, u32[]{:S(2)}) %collective-permute-start.25) | collective-permute-done | bytes 524320 | tf_op jit(solution)/shard_map/ppermute | solution.py:295
  197.5 2.2 load_weights.19.w_ref
  201.1 3.6 %all-to-all-start.9 = ((bf16[16,4,32,128]{3,2,1,0:T(8,128)(2,1)}), bf16[16,4,32,128]{3,2,1,0:T(8,128)(2,1)S(1)}, u32[]{:S(2)}, u32[]{:S(2)}) async-start(bf16[16,4,32,128]{3,2,1,0:T(8,128)(2,1)} %get-tuple-element.179), calls=%async_computation.9 | async-start | bytes 1048576 | tf_op jit(solution)/shard_map/all_to_all | solution.py:338
  204.8 6.6 %collective-permute-done.27.refs_2_ = bf16[64,32,128]{2,1,0:T(8,128)(2,1)S(1)} collective-permute-done((bf16[64,32,128]{2,1,0:T(8,128)(2,1)S(1)}, bf16[64,32,128]{2,1,0:T(8,128)(2,1)S(1)}, u32[]{:S(2)}, u32[]{:S(2)}) %collective-permute-start.27) | collective-permute-done | bytes 524320 | tf_op jit(solution)/shard_map/ppermute | solution.py:295
  221.9 3.6 %all-to-all-start.10 = ((bf16[16,4,32,128]{3,2,1,0:T(8,128)(2,1)}), bf16[16,4,32,128]{3,2,1,0:T(8,128)(2,1)S(1)}, u32[]{:S(2)}, u32[]{:S(2)}) async-start(bf16[16,4,32,128]{3,2,1,0:T(8,128)(2,1)} %get-tuple-element.185), calls=%async_computation.10 | async-start | bytes 1048576 | tf_op jit(solution)/shard_map/all_to_all | solution.py:338
  225.6 6.4 %collective-permute-done.29.refs_2_ = bf16[64,32,128]{2,1,0:T(8,128)(2,1)S(1)} collective-permute-done((bf16[64,32,128]{2,1,0:T(8,128)(2,1)S(1)}, bf16[64,32,128]{2,1,0:T(8,128)(2,1)S(1)}, u32[]{:S(2)}, u32[]{:S(2)}) %collective-permute-start.29) | collective-permute-done | bytes 524320 | tf_op jit(solution)/shard_map/ppermute | solution.py:295
  238.0 2.2 load_weights.21.w_ref
  (130 shorter events, 113.5 us)
Async XLA Ops:
  7.5 18.1 %all-to-all-start = ((bf16[16,4,32,128]{3,2,1,0:T(8,128)(2,1)}), bf16[16,4,32,128]{3,2,1,0:T(8,128)(2,1)S(1)}, u32[]{:S(2)}, u32[]{:S(2)}) async-start(bf16[16,4,32,128]{3,2,1,0:T(8,128)(2,1)} %get-tuple-element.121), calls=%async_computation | async-start | bytes 1048576 | tf_op jit(solution)/shard_map/all_to_all | solution.py:338
  25.6 5.1 %collective-permute-start.10 = (bf16[64,32,128]{2,1,0:T(8,128)(2,1)S(1)}, bf16[64,32,128]{2,1,0:T(8,128)(2,1)S(1)}, u32[]{:S(2)}, u32[]{:S(2)}) collective-permute-start(bf16[64,32,128]{2,1,0:T(8,128)(2,1)S(1)} %bitcast.97), channel_id=1, source_target_pairs={{0,1},{1,0},{2,3},{3,2},{4,5},{5,4},{6,7},{7,6},{8,9},{9,8},{10,11... | collective-permute-start | bytes 1572872 | tf_op jit(solution)/shard_map/ppermute | solution.py:295
  27.6 15.3 %collective-permute-start.11 = (bf16[64,32,128]{2,1,0:T(8,128)(2,1)S(1)}, bf16[64,32,128]{2,1,0:T(8,128)(2,1)S(1)}, u32[]{:S(2)}, u32[]{:S(2)}) collective-permute-start(bf16[64,32,128]{2,1,0:T(8,128)(2,1)S(1)} %bitcast.98), channel_id=1, source_target_pairs={{0,32},{1,33},{2,34},{3,35},{4,36},{5,37},{6,38},{7,39},{8,40},{9,... | collective-permute-start | bytes 1572872 | tf_op jit(solution)/shard_map/ppermute | solution.py:295
  32.8 15.0 %all-to-all-start.1 = ((bf16[16,4,32,128]{3,2,1,0:T(8,128)(2,1)}), bf16[16,4,32,128]{3,2,1,0:T(8,128)(2,1)S(1)}, u32[]{:S(2)}, u32[]{:S(2)}) async-start(bf16[16,4,32,128]{3,2,1,0:T(8,128)(2,1)} %get-tuple-element.127), calls=%async_computation.1 | async-start | bytes 1048576 | tf_op jit(solution)/shard_map/all_to_all | solution.py:338
  47.8 4.2 %collective-permute-start.12 = (bf16[64,32,128]{2,1,0:T(8,128)(2,1)S(1)}, bf16[64,32,128]{2,1,0:T(8,128)(2,1)S(1)}, u32[]{:S(2)}, u32[]{:S(2)}) collective-permute-start(bf16[64,32,128]{2,1,0:T(8,128)(2,1)S(1)} %bitcast.69), channel_id=1, source_target_pairs={{0,1},{1,0},{2,3},{3,2},{4,5},{5,4},{6,7},{7,6},{8,9},{9,8},{10,11... | collective-permute-start | bytes 1572872 | tf_op jit(solution)/shard_map/ppermute | solution.py:295
  48.8 14.8 %collective-permute-start.13 = (bf16[64,32,128]{2,1,0:T(8,128)(2,1)S(1)}, bf16[64,32,128]{2,1,0:T(8,128)(2,1)S(1)}, u32[]{:S(2)}, u32[]{:S(2)}) collective-permute-start(bf16[64,32,128]{2,1,0:T(8,128)(2,1)S(1)} %bitcast.70), channel_id=1, source_target_pairs={{0,32},{1,33},{2,34},{3,35},{4,36},{5,37},{6,38},{7,39},{8,40},{9,... | collective-permute-start | bytes 1572872 | tf_op jit(solution)/shard_map/ppermute | solution.py:295
  54.1 14.6 %all-to-all-start.2 = ((bf16[16,4,32,128]{3,2,1,0:T(8,128)(2,1)}), bf16[16,4,32,128]{3,2,1,0:T(8,128)(2,1)S(1)}, u32[]{:S(2)}, u32[]{:S(2)}) async-start(bf16[16,4,32,128]{3,2,1,0:T(8,128)(2,1)} %get-tuple-element.134), calls=%async_computation.2 | async-start | bytes 1048576 | tf_op jit(solution)/shard_map/all_to_all | solution.py:338
  68.8 5.0 %collective-permute-start.14 = (bf16[64,32,128]{2,1,0:T(8,128)(2,1)S(1)}, bf16[64,32,128]{2,1,0:T(8,128)(2,1)S(1)}, u32[]{:S(2)}, u32[]{:S(2)}) collective-permute-start(bf16[64,32,128]{2,1,0:T(8,128)(2,1)S(1)} %bitcast.73), channel_id=1, source_target_pairs={{0,1},{1,0},{2,3},{3,2},{4,5},{5,4},{6,7},{7,6},{8,9},{9,8},{10,11... | collective-permute-start | bytes 1572872 | tf_op jit(solution)/shard_map/ppermute | solution.py:295
  70.2 14.8 %collective-permute-start.15 = (bf16[64,32,128]{2,1,0:T(8,128)(2,1)S(1)}, bf16[64,32,128]{2,1,0:T(8,128)(2,1)S(1)}, u32[]{:S(2)}, u32[]{:S(2)}) collective-permute-start(bf16[64,32,128]{2,1,0:T(8,128)(2,1)S(1)} %bitcast.74), channel_id=1, source_target_pairs={{0,32},{1,33},{2,34},{3,35},{4,36},{5,37},{6,38},{7,39},{8,40},{9,... | collective-permute-start | bytes 1572872 | tf_op jit(solution)/shard_map/ppermute | solution.py:295
  75.9 14.6 %all-to-all-start.3 = ((bf16[16,4,32,128]{3,2,1,0:T(8,128)(2,1)}), bf16[16,4,32,128]{3,2,1,0:T(8,128)(2,1)S(1)}, u32[]{:S(2)}, u32[]{:S(2)}) async-start(bf16[16,4,32,128]{3,2,1,0:T(8,128)(2,1)} %get-tuple-element.141), calls=%async_computation.3 | async-start | bytes 1048576 | tf_op jit(solution)/shard_map/all_to_all | solution.py:338
  90.5 3.9 %collective-permute-start.16 = (bf16[64,32,128]{2,1,0:T(8,128)(2,1)S(1)}, bf16[64,32,128]{2,1,0:T(8,128)(2,1)S(1)}, u32[]{:S(2)}, u32[]{:S(2)}) collective-permute-start(bf16[64,32,128]{2,1,0:T(8,128)(2,1)S(1)} %bitcast.77), channel_id=1, source_target_pairs={{0,1},{1,0},{2,3},{3,2},{4,5},{5,4},{6,7},{7,6},{8,9},{9,8},{10,11... | collective-permute-start | bytes 1572872 | tf_op jit(solution)/shard_map/ppermute | solution.py:295
  91.9 14.8 %collective-permute-start.17 = (bf16[64,32,128]{2,1,0:T(8,128)(2,1)S(1)}, bf16[64,32,128]{2,1,0:T(8,128)(2,1)S(1)}, u32[]{:S(2)}, u32[]{:S(2)}) collective-permute-start(bf16[64,32,128]{2,1,0:T(8,128)(2,1)S(1)} %bitcast.78), channel_id=1, source_target_pairs={{0,32},{1,33},{2,34},{3,35},{4,36},{5,37},{6,38},{7,39},{8,40},{9,... | collective-permute-start | bytes 1572872 | tf_op jit(solution)/shard_map/ppermute | solution.py:295
  96.6 15.0 %all-to-all-start.4 = ((bf16[16,4,32,128]{3,2,1,0:T(8,128)(2,1)}), bf16[16,4,32,128]{3,2,1,0:T(8,128)(2,1)S(1)}, u32[]{:S(2)}, u32[]{:S(2)}) async-start(bf16[16,4,32,128]{3,2,1,0:T(8,128)(2,1)} %get-tuple-element.148), calls=%async_computation.4 | async-start | bytes 1048576 | tf_op jit(solution)/shard_map/all_to_all | solution.py:338
  111.6 3.4 %collective-permute-start.18 = (bf16[64,32,128]{2,1,0:T(8,128)(2,1)S(1)}, bf16[64,32,128]{2,1,0:T(8,128)(2,1)S(1)}, u32[]{:S(2)}, u32[]{:S(2)}) collective-permute-start(bf16[64,32,128]{2,1,0:T(8,128)(2,1)S(1)} %bitcast.81), channel_id=1, source_target_pairs={{0,1},{1,0},{2,3},{3,2},{4,5},{5,4},{6,7},{7,6},{8,9},{9,8},{10,11... | collective-permute-start | bytes 1572872 | tf_op jit(solution)/shard_map/ppermute | solution.py:295
  112.7 14.8 %collective-permute-start.19 = (bf16[64,32,128]{2,1,0:T(8,128)(2,1)S(1)}, bf16[64,32,128]{2,1,0:T(8,128)(2,1)S(1)}, u32[]{:S(2)}, u32[]{:S(2)}) collective-permute-start(bf16[64,32,128]{2,1,0:T(8,128)(2,1)S(1)} %bitcast.82), channel_id=1, source_target_pairs={{0,32},{1,33},{2,34},{3,35},{4,36},{5,37},{6,38},{7,39},{8,40},{9,... | collective-permute-start | bytes 1572872 | tf_op jit(solution)/shard_map/ppermute | solution.py:295
  117.2 14.5 %all-to-all-start.5 = ((bf16[16,4,32,128]{3,2,1,0:T(8,128)(2,1)}), bf16[16,4,32,128]{3,2,1,0:T(8,128)(2,1)S(1)}, u32[]{:S(2)}, u32[]{:S(2)}) async-start(bf16[16,4,32,128]{3,2,1,0:T(8,128)(2,1)} %get-tuple-element.155), calls=%async_computation.5 | async-start | bytes 1048576 | tf_op jit(solution)/shard_map/all_to_all | solution.py:338
  131.7 4.8 %collective-permute-start.20 = (bf16[64,32,128]{2,1,0:T(8,128)(2,1)S(1)}, bf16[64,32,128]{2,1,0:T(8,128)(2,1)S(1)}, u32[]{:S(2)}, u32[]{:S(2)}) collective-permute-start(bf16[64,32,128]{2,1,0:T(8,128)(2,1)S(1)} %bitcast.85), channel_id=1, source_target_pairs={{0,1},{1,0},{2,3},{3,2},{4,5},{5,4},{6,7},{7,6},{8,9},{9,8},{10,11... | collective-permute-start | bytes 1572872 | tf_op jit(solution)/shard_map/ppermute | solution.py:295
  133.2 14.8 %collective-permute-start.21 = (bf16[64,32,128]{2,1,0:T(8,128)(2,1)S(1)}, bf16[64,32,128]{2,1,0:T(8,128)(2,1)S(1)}, u32[]{:S(2)}, u32[]{:S(2)}) collective-permute-start(bf16[64,32,128]{2,1,0:T(8,128)(2,1)S(1)} %bitcast.86), channel_id=1, source_target_pairs={{0,32},{1,33},{2,34},{3,35},{4,36},{5,37},{6,38},{7,39},{8,40},{9,... | collective-permute-start | bytes 1572872 | tf_op jit(solution)/shard_map/ppermute | solution.py:295
  137.9 14.6 %all-to-all-start.6 = ((bf16[16,4,32,128]{3,2,1,0:T(8,128)(2,1)}), bf16[16,4,32,128]{3,2,1,0:T(8,128)(2,1)S(1)}, u32[]{:S(2)}, u32[]{:S(2)}) async-start(bf16[16,4,32,128]{3,2,1,0:T(8,128)(2,1)} %get-tuple-element.161), calls=%async_computation.6 | async-start | bytes 1048576 | tf_op jit(solution)/shard_map/all_to_all | solution.py:338
  152.5 5.7 %collective-permute-start.22 = (bf16[64,32,128]{2,1,0:T(8,128)(2,1)S(1)}, bf16[64,32,128]{2,1,0:T(8,128)(2,1)S(1)}, u32[]{:S(2)}, u32[]{:S(2)}) collective-permute-start(bf16[64,32,128]{2,1,0:T(8,128)(2,1)S(1)} %bitcast.89), channel_id=1, source_target_pairs={{0,1},{1,0},{2,3},{3,2},{4,5},{5,4},{6,7},{7,6},{8,9},{9,8},{10,11... | collective-permute-start | bytes 1572872 | tf_op jit(solution)/shard_map/ppermute | solution.py:295
  153.9 14.8 %collective-permute-start.23 = (bf16[64,32,128]{2,1,0:T(8,128)(2,1)S(1)}, bf16[64,32,128]{2,1,0:T(8,128)(2,1)S(1)}, u32[]{:S(2)}, u32[]{:S(2)}) collective-permute-start(bf16[64,32,128]{2,1,0:T(8,128)(2,1)S(1)} %bitcast.90), channel_id=1, source_target_pairs={{0,32},{1,33},{2,34},{3,35},{4,36},{5,37},{6,38},{7,39},{8,40},{9,... | collective-permute-start | bytes 1572872 | tf_op jit(solution)/shard_map/ppermute | solution.py:295
  159.9 14.6 %all-to-all-start.7 = ((bf16[16,4,32,128]{3,2,1,0:T(8,128)(2,1)}), bf16[16,4,32,128]{3,2,1,0:T(8,128)(2,1)S(1)}, u32[]{:S(2)}, u32[]{:S(2)}) async-start(bf16[16,4,32,128]{3,2,1,0:T(8,128)(2,1)} %get-tuple-element.167), calls=%async_computation.7 | async-start | bytes 1048576 | tf_op jit(solution)/shard_map/all_to_all | solution.py:338
  174.5 4.6 %collective-permute-start.24 = (bf16[64,32,128]{2,1,0:T(8,128)(2,1)S(1)}, bf16[64,32,128]{2,1,0:T(8,128)(2,1)S(1)}, u32[]{:S(2)}, u32[]{:S(2)}) collective-permute-start(bf16[64,32,128]{2,1,0:T(8,128)(2,1)S(1)} %bitcast.93), channel_id=1, source_target_pairs={{0,1},{1,0},{2,3},{3,2},{4,5},{5,4},{6,7},{7,6},{8,9},{9,8},{10,11... | collective-permute-start | bytes 1572872 | tf_op jit(solution)/shard_map/ppermute | solution.py:295
  175.9 14.8 %collective-permute-start.25 = (bf16[64,32,128]{2,1,0:T(8,128)(2,1)S(1)}, bf16[64,32,128]{2,1,0:T(8,128)(2,1)S(1)}, u32[]{:S(2)}, u32[]{:S(2)}) collective-permute-start(bf16[64,32,128]{2,1,0:T(8,128)(2,1)S(1)} %bitcast.94), channel_id=1, source_target_pairs={{0,32},{1,33},{2,34},{3,35},{4,36},{5,37},{6,38},{7,39},{8,40},{9,... | collective-permute-start | bytes 1572872 | tf_op jit(solution)/shard_map/ppermute | solution.py:295
  180.6 14.6 %all-to-all-start.8 = ((bf16[16,4,32,128]{3,2,1,0:T(8,128)(2,1)}), bf16[16,4,32,128]{3,2,1,0:T(8,128)(2,1)S(1)}, u32[]{:S(2)}, u32[]{:S(2)}) async-start(bf16[16,4,32,128]{3,2,1,0:T(8,128)(2,1)} %get-tuple-element.173), calls=%async_computation.8 | async-start | bytes 1048576 | tf_op jit(solution)/shard_map/all_to_all | solution.py:338
  195.2 4.5 %collective-permute-start.26 = (bf16[64,32,128]{2,1,0:T(8,128)(2,1)S(1)}, bf16[64,32,128]{2,1,0:T(8,128)(2,1)S(1)}, u32[]{:S(2)}, u32[]{:S(2)}) collective-permute-start(bf16[64,32,128]{2,1,0:T(8,128)(2,1)S(1)} %bitcast.62), channel_id=1, source_target_pairs={{0,1},{1,0},{2,3},{3,2},{4,5},{5,4},{6,7},{7,6},{8,9},{9,8},{10,11... | collective-permute-start | bytes 1572872 | tf_op jit(solution)/shard_map/ppermute | solution.py:295
  196.6 14.8 %collective-permute-start.27 = (bf16[64,32,128]{2,1,0:T(8,128)(2,1)S(1)}, bf16[64,32,128]{2,1,0:T(8,128)(2,1)S(1)}, u32[]{:S(2)}, u32[]{:S(2)}) collective-permute-start(bf16[64,32,128]{2,1,0:T(8,128)(2,1)S(1)} %bitcast.63), channel_id=1, source_target_pairs={{0,32},{1,33},{2,34},{3,35},{4,36},{5,37},{6,38},{7,39},{8,40},{9,... | collective-permute-start | bytes 1572872 | tf_op jit(solution)/shard_map/ppermute | solution.py:295
  201.1 14.6 %all-to-all-start.9 = ((bf16[16,4,32,128]{3,2,1,0:T(8,128)(2,1)}), bf16[16,4,32,128]{3,2,1,0:T(8,128)(2,1)S(1)}, u32[]{:S(2)}, u32[]{:S(2)}) async-start(bf16[16,4,32,128]{3,2,1,0:T(8,128)(2,1)} %get-tuple-element.179), calls=%async_computation.9 | async-start | bytes 1048576 | tf_op jit(solution)/shard_map/all_to_all | solution.py:338
  215.8 4.7 %collective-permute-start.28 = (bf16[64,32,128]{2,1,0:T(8,128)(2,1)S(1)}, bf16[64,32,128]{2,1,0:T(8,128)(2,1)S(1)}, u32[]{:S(2)}, u32[]{:S(2)}) collective-permute-start(bf16[64,32,128]{2,1,0:T(8,128)(2,1)S(1)} %bitcast.58), channel_id=1, source_target_pairs={{0,1},{1,0},{2,3},{3,2},{4,5},{5,4},{6,7},{7,6},{8,9},{9,8},{10,11... | collective-permute-start | bytes 1572872 | tf_op jit(solution)/shard_map/ppermute | solution.py:295
  217.2 14.8 %collective-permute-start.29 = (bf16[64,32,128]{2,1,0:T(8,128)(2,1)S(1)}, bf16[64,32,128]{2,1,0:T(8,128)(2,1)S(1)}, u32[]{:S(2)}, u32[]{:S(2)}) collective-permute-start(bf16[64,32,128]{2,1,0:T(8,128)(2,1)S(1)} %bitcast.59), channel_id=1, source_target_pairs={{0,32},{1,33},{2,34},{3,35},{4,36},{5,37},{6,38},{7,39},{8,40},{9,... | collective-permute-start | bytes 1572872 | tf_op jit(solution)/shard_map/ppermute | solution.py:295
  221.9 14.6 %all-to-all-start.10 = ((bf16[16,4,32,128]{3,2,1,0:T(8,128)(2,1)}), bf16[16,4,32,128]{3,2,1,0:T(8,128)(2,1)S(1)}, u32[]{:S(2)}, u32[]{:S(2)}) async-start(bf16[16,4,32,128]{3,2,1,0:T(8,128)(2,1)} %get-tuple-element.185), calls=%async_computation.10 | async-start | bytes 1048576 | tf_op jit(solution)/shard_map/all_to_all | solution.py:338
  236.6 3.7 %collective-permute-start.30 = (bf16[64,32,128]{2,1,0:T(8,128)(2,1)S(1)}, bf16[64,32,128]{2,1,0:T(8,128)(2,1)S(1)}, u32[]{:S(2)}, u32[]{:S(2)}) collective-permute-start(bf16[64,32,128]{2,1,0:T(8,128)(2,1)S(1)} %bitcast.66), channel_id=1, source_target_pairs={{0,1},{1,0},{2,3},{3,2},{4,5},{5,4},{6,7},{7,6},{8,9},{9,8},{10,11... | collective-permute-start | bytes 1572872 | tf_op jit(solution)/shard_map/ppermute | solution.py:295
  (13 other events, 36.8 us)

commit v4 on v3

--- a/solution.py
+++ b/solution.py
@@ -92,44 +92,66 @@
     return lambda i: rows_ref[:, pl.ds(pl.multiple_of(i * edge, edge), edge)]
 
 
-def input_kernel(tick, step_count, *refs):
-    layer_ref, index_ref = refs[:2]
-    fresh_ref = refs[2] if tick < step_count else None
-    lower_refs = refs[-5:-3] if tick >= LAG else None
-    w_ref, bias_ref, out_ref = refs[-3:]
-    edge = w_ref.shape[2]
-    row_count = out_ref.shape[1]
-
-    def fill(pick):
-        for row in range(w_ref.shape[0]):
-            bias = jnp.broadcast_to(bias_ref[row], (row_count, edge))
-            out_ref[row] = row_sums(pick, index_ref, w_ref, row) + bias
-
-    step = tick - LAG * layer_ref[0]
-    if fresh_ref is not None:
-        @pl.when(layer_ref[0] == 0)
-        def _():
-            fill(from_rows(fresh_ref, edge))
-
-    if lower_refs is not None:
-        @pl.when((layer_ref[0] != 0) & (step >= 0) & (step < step_count))
-        def _():
-            fill(from_halves(*lower_refs))
-
-
-def input_sums(tick, layer, index, fresh, lower, w, bias, step_count):
+def lower_kernel(index_ref, mine_ref, other_ref, w_ref, bias_ref, out_ref):
+    pick = from_halves(mine_ref, other_ref)
+    for row in range(w_ref.shape[0]):
+        out_ref[row] = row_sums(pick, index_ref, w_ref, row) + bias_ref[row]
+
+
+def lower_sums(low, inputs, index, w, bias):
+    other = other_core(low)
     rows = w.shape[0]
-    x = [held(part) for part in ((fresh,) if tick < step_count else ()) + lower]
-    row_count = (fresh if fresh is not None else lower[0]).shape[-2]
-    return pl.pallas_call(
-        functools.partial(input_kernel, tick, step_count),
-        out_shape=pltpu.VMEM((rows, row_count, w.shape[3]), F32),
-        in_specs=[smem(), smem()] + [vmem()] * (len(x) + 2),
+    return pl.pallas_call(
+        lower_kernel,
+        out_shape=pltpu.VMEM((rows, low.shape[1], w.shape[3]), F32),
+        in_specs=[smem()] + [vmem()] * 4,
         out_specs=vmem(),
         compiler_params=pltpu.CompilerParams(vmem_limit_bytes=8 * MIB),
         cost_estimate=pl.CostEstimate(flops=2 * w.size * 32, bytes_accessed=w.size, transcendentals=0),
-        name="input_sums",
-    )(layer, index, *x, held(w), held(bias))
+        name="lower_sums",
+    )(index, held(low), held(other), held(load(w, low)), held(bias))
+
+
+def fresh_kernel(tick, layer_ref, index_ref, inputs_ref, w_hbm, bias_ref, out_ref, fresh_ref, w_ref, arrived, loaded):
+    edge = w_ref.shape[2]
+
+    @pl.when(layer_ref[0] == 0)
+    def _():
+        fresh = pltpu.make_async_copy(inputs_ref.at[tick], fresh_ref, arrived)
+        fresh.start()
+        copies = stream(w_hbm, w_ref, loaded)
+        fresh.wait()
+        pick = from_rows(fresh_ref, edge)
+        for j, copy in enumerate(copies):
+            copy.wait()
+            for row in range(4 * j, 4 * j + 4):
+                out_ref[row] = row_sums(pick, index_ref, w_ref, row) + bias_ref[row]
+
+
+def fresh_scratch(inputs, w, groups):
+    return [
+        pltpu.VMEM(inputs.shape[1:], BF16),
+        pltpu.VMEM(w.shape, w.dtype),
+        pltpu.SemaphoreType.DMA,
+        pltpu.SemaphoreType.DMA((groups,)),
+    ]
+
+
+def fresh_sums(tick, groups, layer, inputs, index, w, bias):
+    return pl.pallas_call(
+        functools.partial(fresh_kernel, tick),
+        out_shape=pltpu.VMEM((w.shape[0], inputs.shape[1], w.shape[3]), F32),
+        in_specs=[smem(), smem(), hbm(), hbm(), vmem()],
+        out_specs=vmem(),
+        scratch_shapes=fresh_scratch(inputs, w, groups),
+        compiler_params=pltpu.CompilerParams(vmem_limit_bytes=12 * MIB),
+        cost_estimate=pl.CostEstimate(flops=2 * w.size * 32, bytes_accessed=2 * w.size, transcendentals=0),
+        name="fresh_sums",
+    )(layer, index, unmoved(inputs), unmoved(w), held(bias))
+
+
+def no_sums(low, inputs, index, w, bias):
+    return jnp.zeros((w.shape[0], low.shape[1], w.shape[3]), F32)
 
 
 def gates_to_state(sums, before):
@@ -169,25 +191,20 @@
     )
 
 
-def first_kernel(layer_ref, index_ref, inputs_ref, w_hbm, bias_ref, cell_out, rows_out, send_out, next_out, fresh_ref, w_out, arrived, loaded, spread_ref, sent):
+def first_kernel(layer_ref, index_ref, inputs_ref, w_hbm, bias_ref, cell_out, rows_out, send_out, fresh_ref, w_out, arrived, loaded, spread_ref, sent):
     per_device, row_count, edge = cell_out.shape
-    fresh = pltpu.make_async_copy(inputs_ref.at[0], fresh_ref, arrived.at[0])
-    later = pltpu.make_async_copy(inputs_ref.at[1], next_out, arrived.at[1])
-    fresh.start()
-    copies = stream(w_hbm, w_out, loaded)
-    later.start()
 
     @pl.when(layer_ref[0] == 0)
     def _():
+        fresh = pltpu.make_async_copy(inputs_ref.at[0], fresh_ref, arrived)
+        fresh.start()
+        copies = stream(w_hbm, w_out, loaded)
         fresh.wait()
         sender = Sender(send_out, spread_ref, sent)
         pick = from_rows(fresh_ref, edge)
         for j, copy in enumerate(copies):
             copy.wait()
-            sums = [
-                row_sums(pick, index_ref, w_out, 4 * j + g) + jnp.broadcast_to(bias_ref[4 * j + g], (row_count, edge))
-                for g in range(4)
-            ]
+            sums = [row_sums(pick, index_ref, w_out, 4 * j + g) + bias_ref[4 * j + g] for g in range(4)]
             cell_out[j], output = gates_to_state(sums, jnp.zeros((row_count, edge), F32))
             rows_out[:, j * edge:(j + 1) * edge] = output
             sender.put(j, output)
@@ -201,11 +218,6 @@
         for ref in (cell_out, rows_out):
             ref[...] = jnp.zeros_like(ref)
         idle.finish()
-        fresh.wait()
-        for copy in copies:
-            copy.wait()
-
-    later.wait()
 
 
 def first_step(layer, index, inputs, w, bias, per_device, peers):
@@ -213,38 +225,25 @@
     edge = w.shape[2]
     return pl.pallas_call(
         first_kernel,
-        out_shape=state_out((per_device, row_count, edge), peers)
-        + (pltpu.VMEM((row_count, hidden), BF16),),
+        out_shape=state_out((per_device, row_count, edge), peers),
         in_specs=[smem(), smem(), hbm(), hbm(), vmem()],
-        out_specs=(vmem(), vmem(), hbm(), vmem()),
-        scratch_shapes=[
-            pltpu.VMEM((row_count, hidden), BF16),
-            pltpu.VMEM(w.shape, w.dtype),
-            pltpu.SemaphoreType.DMA((2,)),
-            pltpu.SemaphoreType.DMA((per_device,)),
-            *send_scratch((per_device, row_count, edge), peers),
-        ],
+        out_specs=(vmem(), vmem(), hbm()),
+        scratch_shapes=fresh_scratch(inputs, w, per_device) + send_scratch((per_device, row_count, edge), peers),
         compiler_params=pltpu.CompilerParams(vmem_limit_bytes=12 * MIB),
         name="first_step",
     )(layer, index, unmoved(inputs), unmoved(w), held(bias))
 
 
-def state_kernel(tick, step_count, layer_ref, index_ref, inputs_ref, mine_ref, other_ref, w_ref, partial_ref, cell_ref, cell_out, rows_out, send_out, *rest):
-    *fetch, spread_ref, sent = rest
+def state_kernel(tick, step_count, layer_ref, index_ref, mine_ref, other_ref, w_ref, partial_ref, cell_ref, token_ref, cell_out, rows_out, send_out, spread_ref, sent):
     step = tick - LAG * layer_ref[0]
     active = (step >= 0) & (step < step_count)
-    edge = cell_ref.shape[2]
-    is_first = layer_ref[0] == 0
-    if fetch:
-        next_out, arrived = fetch
-        later = pltpu.make_async_copy(inputs_ref.at[tick + 1], next_out, arrived)
-        pl.when(is_first)(later.start)
+    per_device, _, edge = cell_ref.shape
 
     @pl.when(active)
     def _():
         pick = from_halves(mine_ref, other_ref)
         sender = Sender(send_out, spread_ref, sent)
-        for j in range(cell_ref.shape[0]):
+        for j in range(per_device):
             sums = [partial_ref[4 * j + g] + row_sums(pick, index_ref, w_ref, 4 * j + g) for g in range(4)]
             cell_out[j], output = gates_to_state(sums, cell_ref[j])
             rows_out[:, j * edge:(j + 1) * edge] = output
@@ -254,30 +253,24 @@
     @pl.when(jnp.logical_not(active))
     def _():
         idle = Sender(send_out, spread_ref, sent)
-        for j in range(cell_ref.shape[0]):
+        for j in range(per_device):
             idle.put(j, jnp.zeros(cell_ref.shape[1:], BF16))
         cell_out[...] = cell_ref[...]
         rows_out[...] = jnp.zeros_like(rows_out)
         idle.finish()
 
-    if fetch:
-        pl.when(is_first)(later.wait)
-
-
-def state_step(tick, layer, index, state, w, partial, cell, inputs, peers):
-    step_count, row_count, hidden = inputs.shape
-    fetch = tick + 1 < step_count
-    outs = pl.pallas_call(
+
+def state_step(tick, layer, index, state, w, partial, cell, step_count, peers, token):
+    return pl.pallas_call(
         functools.partial(state_kernel, tick, step_count),
-        out_shape=state_out(cell.shape, peers) + ((pltpu.VMEM((row_count, hidden), BF16),) if fetch else ()),
-        in_specs=[smem(), smem(), hbm()] + [vmem()] * 5,
-        out_specs=(vmem(), vmem(), hbm()) + (vmem(),) * fetch,
-        scratch_shapes=[pltpu.SemaphoreType.DMA] * fetch + send_scratch(cell.shape, peers),
+        out_shape=state_out(cell.shape, peers),
+        in_specs=[smem(), smem()] + [vmem()] * 6,
+        out_specs=(vmem(), vmem(), hbm()),
+        scratch_shapes=send_scratch(cell.shape, peers),
         compiler_params=pltpu.CompilerParams(vmem_limit_bytes=8 * MIB),
         cost_estimate=pl.CostEstimate(flops=2 * w.size * 32, bytes_accessed=w.size, transcendentals=0),
         name="state_step",
-    )(layer, index, unmoved(inputs), *[held(part) for part in state], held(w), partial, cell)
-    return outs if fetch else (*outs, None)
+    )(layer, index, *[held(part) for part in state], held(w), partial, cell, token)
 
 
 def exchange(x, target):
@@ -303,6 +296,22 @@
     return exchange(x, lambda layer, y, x_at, core: (layer + 1, y, x_at, core))
 
 
+def mark_kernel(x_ref, out_ref):
+    out_ref[...] = x_ref[0, :8].astype(F32)
+
+
+def mark(x, size):
+    return pl.pallas_call(
+        mark_kernel,
+        out_shape=pltpu.VMEM((8, x.shape[2]), F32),
+        in_specs=[vmem()],
+        out_specs=vmem(),
+        compiler_params=pltpu.CompilerParams(vmem_limit_bytes=2 * MIB),
+        cost_estimate=pl.CostEstimate(flops=size, bytes_accessed=4096, transcendentals=0),
+        name="mark",
+    )(held(x))
+
+
 def body(inputs, in_blocks, rec_blocks, in_cols, rec_cols, bias):
     layer = lax.axis_index("pipe")
     layers = lax.axis_size("pipe")
@@ -331,22 +340,23 @@
     steps = [tick - LAG * layer for tick in range(tick_count)]
     fed = [(layer > 0) & (step >= 0) & (step < step_count) for step in steps]
     layer_ref, fed, in_index, rec_index = lax.optimization_barrier((layer_ref, fed, in_index, rec_index))
-    cell, out_rows, send, fresh = first_step(layer_ref, in_index, inputs, w_in, offsets, per_device, chips)
+    cell, out_rows, send = first_step(layer_ref, in_index, inputs, w_in, offsets, per_device, chips)
     arrived = {}
     outputs = [out_rows]
     for tick in range(1, tick_count):
         mine = lax.all_to_all(send, ("y", "x"), 0, 0).reshape(half, row_count, edge)
-        lower = ()
-        if tick >= LAG:
-            low = arrived[tick - LAG]
-            lower = (low, lax.cond(fed[tick], other_core, jnp.zeros_like, low))
-        partial = input_sums(tick, layer_ref, in_index, fresh, lower, w_in, offsets, step_count)
+        fresh = functools.partial(fresh_sums, tick, per_device, layer_ref)
+        if tick < LAG:
+            partial = fresh(inputs, in_index, w_in, offsets)
+        else:
+            idle = (lambda low, *args: fresh(*args)) if tick < step_count else no_sums
+            partial = lax.cond(fed[tick], lower_sums, idle, arrived[tick - LAG], inputs, in_index, w_in, offsets)
         mine, partial = lax.optimization_barrier((mine, partial))
         other = other_core(mine)
         if tick <= tick_count - LAG:
             arrived[tick - 1] = upward(mine)
         state = (mine, other)
-        cell, out_rows, send, fresh = state_step(tick, layer_ref, rec_index, state, load(w_rec, mine), partial, cell, inputs, chips)
+        cell, out_rows, send = state_step(tick, layer_ref, rec_index, state, w_rec, partial, cell, step_count, chips, mark(mine, 1024 * w_rec.size))
         outputs.append(out_rows)
     sequence = lax.dynamic_slice_in_dim(jnp.stack(outputs), LAG * layer, step_count, 0)
     cells = cell.transpose(1, 0, 2).reshape(row_count, per_device * edge)

time: 245 us -> 229 us (0.935)
  waiting for transfers between devices: 73.3 us -> 117 us
  local copies, waits for them, and re-layouts: 36.5 us -> 4.52 us
  Pallas kernels: 63.4 us -> 43.5 us
  starting transfers between devices: 68.5 us -> 60.1 us
    ppermute x21, waiting for transfers between devices: 62.3 us -> 95.4 us  [exchange(): return lax.ppermute(x, ('pipe',) + WIDTH, route)]
    unnamed x37, local copies, waits for them, and re-layouts: 24.8 us -> 1.44 us
    pallas_call x22 -> x16, Pallas kernels: 39.6 us -> 19.9 us  [the longest x5 19.9 us: fresh_sums(): pl.pallas_call(functools.partial(fresh_kernel, tick), out_shape=pltpu.VME...]
    all_to_all x11, waiting for transfers between devices: 11 us -> 21.6 us  [body(): mine = lax.all_to_all(send, ('y', 'x'), 0, 0).reshape(half, row_count, edge)]
    ppermute x21, starting transfers between devices: 25.1 us -> 16.4 us  [exchange(): return lax.ppermute(x, ('pipe',) + WIDTH, route)]
    another operation x10 -> x6, local copies, waits for them, and re-layouts: 8.73 us -> 0.11 us
  transfers between devices with their start and end apart: 32 -> 32, of which waited for: 19 -> 28; matrix products, arithmetic and copies ran while one was open for 4% -> 0% of each run, Pallas kernels for 24% -> 17%
where the time goes in v4:
time: 229 us; the launch traced here: 227 us
  waiting for transfers between devices  117 us (51%)
  starting transfers between devices  60.1 us (26%)
  Pallas kernels  43.5 us (19%)
  local copies, waits for them, and re-layouts  4.52 us (2%)
    ppermute x21, waiting for transfers between devices, exchange(): return lax.ppermute(x, ('pipe',) + WIDTH, route)  95.4 us
    all_to_all x11, starting transfers between devices, body(): mine = lax.all_to_all(send, ('y', 'x'), 0, 0).reshape(half, row_count, edge)  43.6 us
    all_to_all x11, waiting for transfers between devices, body(): mine = lax.all_to_all(send, ('y', 'x'), 0, 0).reshape(half, row_count, edge)  21.6 us
    pallas_call x5, Pallas kernels, fresh_sums(): pl.pallas_call(functools.partial(fresh_kernel, tick), out_shape=pltpu.VME...  19.9 us
    pallas_call x11, Pallas kernels, state_step(): pl.pallas_call(functools.partial(state_kernel, tick, step_count), out_sha...  18.9 us
    ppermute x21, starting transfers between devices, exchange(): return lax.ppermute(x, ('pipe',) + WIDTH, route)  16.4 us
    pallas_call x1, Pallas kernels, first_step(): pl.pallas_call(first_kernel, out_shape=state_out((per_device, row_count,...  4.69 us
  transfers between devices with their start and end apart: 32, of which 28 were waited for; matrix products, arithmetic and copies ran while one was open for 0% of the time, Pallas kernels for 17%

profile of v4, /device:TPU:1, one launch (start us, length us, event | category | flops | bytes accessed | tf_op | source)
XLA Modules:
  0.0 226.6 jit_solution(5220120376585605307)
XLA Ops:
  3.1 4.7 %first_step.1 = (f32[4,32,128]{2,1,0:T(8,128)S(1)}, bf16[32,512]{1,0:T(8,128)(2,1)S(1)}, bf16[16,4,32,128]{3,2,1,0:T(8,128)(2,1)}) custom-call(s32[1]{0:T(128)} %bitcast.layer_ref, s32[128]{0:T(128)S(1)} %get-tuple-element.283.index_ref, bf16[6,32,16384]{2,1,0:T(8,128)(2,1)} %inputs_ref.3, bf16[16,8,128,128]{3,2,1,0:T(8,128)(2,1)} %bitcast.117, ...), custom_call_target="tpu_custom_call" | custom-call | tf_op jit(solution)/shard_map/first_step/pallas_call | solution.py:226
  7.8 7.6 %all-to-all-start = ((bf16[16,4,32,128]{3,2,1,0:T(8,128)(2,1)}), bf16[16,4,32,128]{3,2,1,0:T(8,128)(2,1)S(1)}, u32[]{:S(2)}, u32[]{:S(2)}) async-start(bf16[16,4,32,128]{3,2,1,0:T(8,128)(2,1)} %get-tuple-element.286), calls=%async_computation | async-start | bytes 1048576 | tf_op jit(solution)/shard_map/all_to_all | solution.py:347
  15.4 4.0 %fresh_sums.9.partial_ref = f32[16,32,128]{2,1,0:T(8,128)S(1)} custom-call(s32[1]{0:T(128)} %bitcast.layer_ref, s32[128]{0:T(128)S(1)} %get-tuple-element.283.index_ref, bf16[6,32,16384]{2,1,0:T(8,128)(2,1)} %inputs_ref.3, bf16[16,8,128,128]{3,2,1,0:T(8,128)(2,1)} %bitcast.118, f32[16,1,128]{2,1,0:T(1,128)S(1)} %bitcast.58), custom_call_target="tpu_custom_call" | custom-call | flops 134217728 | bytes 4194304 | tf_op jit(solution)/shard_map/fresh_sums/pallas_call | solution.py:141
  19.3 6.5 %all-to-all-done = bf16[16,4,32,128]{3,2,1,0:T(8,128)(2,1)S(1)} async-done(((bf16[16,4,32,128]{3,2,1,0:T(8,128)(2,1)}), bf16[16,4,32,128]{3,2,1,0:T(8,128)(2,1)S(1)}, u32[]{:S(2)}, u32[]{:S(2)}) %all-to-all-start) | async-done | bytes 524320 | tf_op jit(solution)/shard_map/all_to_all | solution.py:347
  31.5 3.6 %all-to-all-start.1 = ((bf16[16,4,32,128]{3,2,1,0:T(8,128)(2,1)}), bf16[16,4,32,128]{3,2,1,0:T(8,128)(2,1)S(1)}, u32[]{:S(2)}, u32[]{:S(2)}) async-start(bf16[16,4,32,128]{3,2,1,0:T(8,128)(2,1)} %get-tuple-element.291), calls=%async_computation.1 | async-start | bytes 1048576 | tf_op jit(solution)/shard_map/all_to_all | solution.py:347
  35.1 7.5 %collective-permute-done.11 = bf16[64,32,128]{2,1,0:T(8,128)(2,1)S(1)} collective-permute-done((bf16[64,32,128]{2,1,0:T(8,128)(2,1)S(1)}, bf16[64,32,128]{2,1,0:T(8,128)(2,1)S(1)}, u32[]{:S(2)}, u32[]{:S(2)}) %collective-permute-start.11) | collective-permute-done | bytes 524320 | tf_op jit(solution)/shard_map/ppermute | solution.py:288
  42.6 4.0 %conditional.10 = (f32[16,32,128]{2,1,0:T(8,128)S(1)}) conditional(s32[]{:T(128)} %convert_element_type.30, (s32[1]{0:T(128)}, s32[128]{0:T(128)S(1)}, bf16[6,32,16384]{2,1,0:T(8,128)(2,1)}, bf16[16,8,128,128]{3,2,1,0:T(8,128)(2,1)}, f32[16,1,128]{2,1,0:T(1,128)S(1)}) %tuple.146, (bf16[64,32,128]{2,1,0:T(8,128)(2,1)S(1)}, ...), branch_computations={%region_0.1_spmd, %region_1.2_spmd} | conditional | flops 134217728 | bytes 8388656 | solution.py:353
  42.6 4.0 %fresh_sums.5 = f32[16,32,128]{2,1,0:T(8,128)S(1)} custom-call(s32[1]{0:T(128)} %get-tuple-element.139.layer_ref, s32[128]{0:T(128)S(1)} %get-tuple-element.140.index_ref, bf16[6,32,16384]{2,1,0:T(8,128)(2,1)} %get-tuple-element.141.inputs_ref, bf16[16,8,128,128]{3,2,1,0:T(8,128)(2,1)} %get-tuple-element.142.w_hbm, f32[16,1,128]{2,1,0:T(1,128)S(1)} %get-tuple-element.148.bias_ref), custom_call_target="tpu_custom_call" | custom-call | flops 134217728 | bytes 4194304 | tf_op jit(solution)/shard_map/cond/branch_0_fun/fresh_sums/pallas_call | solution.py:141
  51.1 3.6 %all-to-all-start.2 = ((bf16[16,4,32,128]{3,2,1,0:T(8,128)(2,1)}), bf16[16,4,32,128]{3,2,1,0:T(8,128)(2,1)S(1)}, u32[]{:S(2)}, u32[]{:S(2)}) async-start(bf16[16,4,32,128]{3,2,1,0:T(8,128)(2,1)} %get-tuple-element.297), calls=%async_computation.2 | async-start | bytes 1048576 | tf_op jit(solution)/shard_map/all_to_all | solution.py:347
  54.7 7.5 %collective-permute-done.13 = bf16[64,32,128]{2,1,0:T(8,128)(2,1)S(1)} collective-permute-done((bf16[64,32,128]{2,1,0:T(8,128)(2,1)S(1)}, bf16[64,32,128]{2,1,0:T(8,128)(2,1)S(1)}, u32[]{:S(2)}, u32[]{:S(2)}) %collective-permute-start.13) | collective-permute-done | bytes 524320 | tf_op jit(solution)/shard_map/ppermute | solution.py:288
  62.2 4.0 %conditional.11 = (f32[16,32,128]{2,1,0:T(8,128)S(1)}) conditional(s32[]{:T(128)} %convert_element_type.31, (s32[1]{0:T(128)}, s32[128]{0:T(128)S(1)}, bf16[6,32,16384]{2,1,0:T(8,128)(2,1)}, bf16[16,8,128,128]{3,2,1,0:T(8,128)(2,1)}, f32[16,1,128]{2,1,0:T(1,128)S(1)}) %tuple.148, (bf16[64,32,128]{2,1,0:T(8,128)(2,1)S(1)}, ...), branch_computations={%region_2.3_spmd, %region_3.4_spmd} | conditional | flops 134217728 | bytes 8388656 | solution.py:353
  62.2 4.0 %fresh_sums.6 = f32[16,32,128]{2,1,0:T(8,128)S(1)} custom-call(s32[1]{0:T(128)} %get-tuple-element.154.layer_ref, s32[128]{0:T(128)S(1)} %get-tuple-element.160.index_ref, bf16[6,32,16384]{2,1,0:T(8,128)(2,1)} %get-tuple-element.161.inputs_ref, bf16[16,8,128,128]{3,2,1,0:T(8,128)(2,1)} %get-tuple-element.162.w_hbm, f32[16,1,128]{2,1,0:T(1,128)S(1)} %get-tuple-element.163.bias_ref), custom_call_target="tpu_custom_call" | custom-call | flops 134217728 | bytes 4194304 | tf_op jit(solution)/shard_map/cond/branch_0_fun/fresh_sums/pallas_call | solution.py:141
  70.8 3.6 %all-to-all-start.3 = ((bf16[16,4,32,128]{3,2,1,0:T(8,128)(2,1)}), bf16[16,4,32,128]{3,2,1,0:T(8,128)(2,1)S(1)}, u32[]{:S(2)}, u32[]{:S(2)}) async-start(bf16[16,4,32,128]{3,2,1,0:T(8,128)(2,1)} %get-tuple-element.303), calls=%async_computation.3 | async-start | bytes 1048576 | tf_op jit(solution)/shard_map/all_to_all | solution.py:347
  74.4 7.5 %collective-permute-done.15 = bf16[64,32,128]{2,1,0:T(8,128)(2,1)S(1)} collective-permute-done((bf16[64,32,128]{2,1,0:T(8,128)(2,1)S(1)}, bf16[64,32,128]{2,1,0:T(8,128)(2,1)S(1)}, u32[]{:S(2)}, u32[]{:S(2)}) %collective-permute-start.15) | collective-permute-done | bytes 524320 | tf_op jit(solution)/shard_map/ppermute | solution.py:288
  81.9 4.2 %conditional.12 = (f32[16,32,128]{2,1,0:T(8,128)S(1)}) conditional(s32[]{:T(128)} %convert_element_type.32, (s32[1]{0:T(128)}, s32[128]{0:T(128)S(1)}, bf16[6,32,16384]{2,1,0:T(8,128)(2,1)}, bf16[16,8,128,128]{3,2,1,0:T(8,128)(2,1)}, f32[16,1,128]{2,1,0:T(1,128)S(1)}) %tuple.150, (bf16[64,32,128]{2,1,0:T(8,128)(2,1)S(1)}, ...), branch_computations={%region_4.5_spmd, %region_5.6_spmd} | conditional | flops 134217728 | bytes 8388656 | solution.py:353
  81.9 4.0 %fresh_sums.7 = f32[16,32,128]{2,1,0:T(8,128)S(1)} custom-call(s32[1]{0:T(128)} %get-tuple-element.168.layer_ref, s32[128]{0:T(128)S(1)} %get-tuple-element.169.index_ref, bf16[6,32,16384]{2,1,0:T(8,128)(2,1)} %get-tuple-element.170.inputs_ref, bf16[16,8,128,128]{3,2,1,0:T(8,128)(2,1)} %get-tuple-element.171.w_hbm, f32[16,1,128]{2,1,0:T(1,128)S(1)} %get-tuple-element.172.bias_ref), custom_call_target="tpu_custom_call" | custom-call | flops 134217728 | bytes 4194304 | tf_op jit(solution)/shard_map/cond/branch_0_fun/fresh_sums/pallas_call | solution.py:141
  90.6 3.6 %all-to-all-start.4 = ((bf16[16,4,32,128]{3,2,1,0:T(8,128)(2,1)}), bf16[16,4,32,128]{3,2,1,0:T(8,128)(2,1)S(1)}, u32[]{:S(2)}, u32[]{:S(2)}) async-start(bf16[16,4,32,128]{3,2,1,0:T(8,128)(2,1)} %get-tuple-element.309), calls=%async_computation.4 | async-start | bytes 1048576 | tf_op jit(solution)/shard_map/all_to_all | solution.py:347
  94.2 7.5 %collective-permute-done.17 = bf16[64,32,128]{2,1,0:T(8,128)(2,1)S(1)} collective-permute-done((bf16[64,32,128]{2,1,0:T(8,128)(2,1)S(1)}, bf16[64,32,128]{2,1,0:T(8,128)(2,1)S(1)}, u32[]{:S(2)}, u32[]{:S(2)}) %collective-permute-start.17) | collective-permute-done | bytes 524320 | tf_op jit(solution)/shard_map/ppermute | solution.py:288
  101.7 4.0 %conditional.13 = (f32[16,32,128]{2,1,0:T(8,128)S(1)}) conditional(s32[]{:T(128)} %convert_element_type.33, (s32[1]{0:T(128)}, s32[128]{0:T(128)S(1)}, bf16[6,32,16384]{2,1,0:T(8,128)(2,1)}, bf16[16,8,128,128]{3,2,1,0:T(8,128)(2,1)}, f32[16,1,128]{2,1,0:T(1,128)S(1)}) %tuple.152, (bf16[64,32,128]{2,1,0:T(8,128)(2,1)S(1)}, ...), branch_computations={%region_6.7_spmd, %region_7.8_spmd} | conditional | flops 134217728 | bytes 8388656 | solution.py:353
  101.7 4.0 %fresh_sums.8 = f32[16,32,128]{2,1,0:T(8,128)S(1)} custom-call(s32[1]{0:T(128)} %get-tuple-element.177.layer_ref, s32[128]{0:T(128)S(1)} %get-tuple-element.178.index_ref, bf16[6,32,16384]{2,1,0:T(8,128)(2,1)} %get-tuple-element.179.inputs_ref, bf16[16,8,128,128]{3,2,1,0:T(8,128)(2,1)} %get-tuple-element.180.w_hbm, f32[16,1,128]{2,1,0:T(1,128)S(1)} %get-tuple-element.181.bias_ref), custom_call_target="tpu_custom_call" | custom-call | flops 134217728 | bytes 4194304 | tf_op jit(solution)/shard_map/cond/branch_0_fun/fresh_sums/pallas_call | solution.py:141
  110.3 3.6 %all-to-all-start.5 = ((bf16[16,4,32,128]{3,2,1,0:T(8,128)(2,1)}), bf16[16,4,32,128]{3,2,1,0:T(8,128)(2,1)S(1)}, u32[]{:S(2)}, u32[]{:S(2)}) async-start(bf16[16,4,32,128]{3,2,1,0:T(8,128)(2,1)} %get-tuple-element.315), calls=%async_computation.5 | async-start | bytes 1048576 | tf_op jit(solution)/shard_map/all_to_all | solution.py:347
  113.9 7.5 %collective-permute-done.19 = bf16[64,32,128]{2,1,0:T(8,128)(2,1)S(1)} collective-permute-done((bf16[64,32,128]{2,1,0:T(8,128)(2,1)S(1)}, bf16[64,32,128]{2,1,0:T(8,128)(2,1)S(1)}, u32[]{:S(2)}, u32[]{:S(2)}) %collective-permute-start.19) | collective-permute-done | bytes 524320 | tf_op jit(solution)/shard_map/ppermute | solution.py:288
  129.3 3.6 %all-to-all-start.6 = ((bf16[16,4,32,128]{3,2,1,0:T(8,128)(2,1)}), bf16[16,4,32,128]{3,2,1,0:T(8,128)(2,1)S(1)}, u32[]{:S(2)}, u32[]{:S(2)}) async-start(bf16[16,4,32,128]{3,2,1,0:T(8,128)(2,1)} %get-tuple-element.321), calls=%async_computation.6 | async-start | bytes 1048576 | tf_op jit(solution)/shard_map/all_to_all | solution.py:347
  132.9 8.2 %collective-permute-done.21 = bf16[64,32,128]{2,1,0:T(8,128)(2,1)S(1)} collective-permute-done((bf16[64,32,128]{2,1,0:T(8,128)(2,1)S(1)}, bf16[64,32,128]{2,1,0:T(8,128)(2,1)S(1)}, u32[]{:S(2)}, u32[]{:S(2)}) %collective-permute-start.21) | collective-permute-done | bytes 524320 | tf_op jit(solution)/shard_map/ppermute | solution.py:288
  148.3 3.8 %all-to-all-start.7 = ((bf16[16,4,32,128]{3,2,1,0:T(8,128)(2,1)}), bf16[16,4,32,128]{3,2,1,0:T(8,128)(2,1)S(1)}, u32[]{:S(2)}, u32[]{:S(2)}) async-start(bf16[16,4,32,128]{3,2,1,0:T(8,128)(2,1)} %get-tuple-element.327), calls=%async_computation.7 | async-start | bytes 1048576 | tf_op jit(solution)/shard_map/all_to_all | solution.py:347
  152.1 8.0 %collective-permute-done.23 = bf16[64,32,128]{2,1,0:T(8,128)(2,1)S(1)} collective-permute-done((bf16[64,32,128]{2,1,0:T(8,128)(2,1)S(1)}, bf16[64,32,128]{2,1,0:T(8,128)(2,1)S(1)}, u32[]{:S(2)}, u32[]{:S(2)}) %collective-permute-start.23) | collective-permute-done | bytes 524320 | tf_op jit(solution)/shard_map/ppermute | solution.py:288
  167.6 3.6 %all-to-all-start.8 = ((bf16[16,4,32,128]{3,2,1,0:T(8,128)(2,1)}), bf16[16,4,32,128]{3,2,1,0:T(8,128)(2,1)S(1)}, u32[]{:S(2)}, u32[]{:S(2)}) async-start(bf16[16,4,32,128]{3,2,1,0:T(8,128)(2,1)} %get-tuple-element.333), calls=%async_computation.8 | async-start | bytes 1048576 | tf_op jit(solution)/shard_map/all_to_all | solution.py:347
  171.2 8.2 %collective-permute-done.25 = bf16[64,32,128]{2,1,0:T(8,128)(2,1)S(1)} collective-permute-done((bf16[64,32,128]{2,1,0:T(8,128)(2,1)S(1)}, bf16[64,32,128]{2,1,0:T(8,128)(2,1)S(1)}, u32[]{:S(2)}, u32[]{:S(2)}) %collective-permute-start.25) | collective-permute-done | bytes 524320 | tf_op jit(solution)/shard_map/ppermute | solution.py:288
  187.2 3.6 %all-to-all-start.9 = ((bf16[16,4,32,128]{3,2,1,0:T(8,128)(2,1)}), bf16[16,4,32,128]{3,2,1,0:T(8,128)(2,1)S(1)}, u32[]{:S(2)}, u32[]{:S(2)}) async-start(bf16[16,4,32,128]{3,2,1,0:T(8,128)(2,1)} %get-tuple-element.339), calls=%async_computation.9 | async-start | bytes 1048576 | tf_op jit(solution)/shard_map/all_to_all | solution.py:347
  190.8 8.1 %collective-permute-done.27 = bf16[64,32,128]{2,1,0:T(8,128)(2,1)S(1)} collective-permute-done((bf16[64,32,128]{2,1,0:T(8,128)(2,1)S(1)}, bf16[64,32,128]{2,1,0:T(8,128)(2,1)S(1)}, u32[]{:S(2)}, u32[]{:S(2)}) %collective-permute-start.27) | collective-permute-done | bytes 524320 | tf_op jit(solution)/shard_map/ppermute | solution.py:288
  206.2 3.6 %all-to-all-start.10 = ((bf16[16,4,32,128]{3,2,1,0:T(8,128)(2,1)}), bf16[16,4,32,128]{3,2,1,0:T(8,128)(2,1)S(1)}, u32[]{:S(2)}, u32[]{:S(2)}) async-start(bf16[16,4,32,128]{3,2,1,0:T(8,128)(2,1)} %get-tuple-element.345), calls=%async_computation.10 | async-start | bytes 1048576 | tf_op jit(solution)/shard_map/all_to_all | solution.py:347
  209.9 9.4 %collective-permute-done.29 = bf16[64,32,128]{2,1,0:T(8,128)(2,1)S(1)} collective-permute-done((bf16[64,32,128]{2,1,0:T(8,128)(2,1)S(1)}, bf16[64,32,128]{2,1,0:T(8,128)(2,1)S(1)}, u32[]{:S(2)}, u32[]{:S(2)}) %collective-permute-start.29) | collective-permute-done | bytes 524320 | tf_op jit(solution)/shard_map/ppermute | solution.py:288
  (120 shorter events, 71.1 us)
Async XLA Ops:
  7.8 18.1 %all-to-all-start = ((bf16[16,4,32,128]{3,2,1,0:T(8,128)(2,1)}), bf16[16,4,32,128]{3,2,1,0:T(8,128)(2,1)S(1)}, u32[]{:S(2)}, u32[]{:S(2)}) async-start(bf16[16,4,32,128]{3,2,1,0:T(8,128)(2,1)} %get-tuple-element.286), calls=%async_computation | async-start | bytes 1048576 | tf_op jit(solution)/shard_map/all_to_all | solution.py:347
  25.9 3.5 %collective-permute-start.10 = (bf16[64,32,128]{2,1,0:T(8,128)(2,1)S(1)}, bf16[64,32,128]{2,1,0:T(8,128)(2,1)S(1)}, u32[]{:S(2)}, u32[]{:S(2)}) collective-permute-start(bf16[64,32,128]{2,1,0:T(8,128)(2,1)S(1)} %bitcast.112), channel_id=1, source_target_pairs={{0,1},{1,0},{2,3},{3,2},{4,5},{5,4},{6,7},{7,6},{8,9},{9,8},{10,11... | collective-permute-start | bytes 1572872 | tf_op jit(solution)/shard_map/ppermute | solution.py:288
  27.8 14.8 %collective-permute-start.11 = (bf16[64,32,128]{2,1,0:T(8,128)(2,1)S(1)}, bf16[64,32,128]{2,1,0:T(8,128)(2,1)S(1)}, u32[]{:S(2)}, u32[]{:S(2)}) collective-permute-start(bf16[64,32,128]{2,1,0:T(8,128)(2,1)S(1)} %bitcast.113), channel_id=1, source_target_pairs={{0,32},{1,33},{2,34},{3,35},{4,36},{5,37},{6,38},{7,39},{8,40},{9,... | collective-permute-start | bytes 1572872 | tf_op jit(solution)/shard_map/ppermute | solution.py:288
  31.5 15.2 %all-to-all-start.1 = ((bf16[16,4,32,128]{3,2,1,0:T(8,128)(2,1)}), bf16[16,4,32,128]{3,2,1,0:T(8,128)(2,1)S(1)}, u32[]{:S(2)}, u32[]{:S(2)}) async-start(bf16[16,4,32,128]{3,2,1,0:T(8,128)(2,1)} %get-tuple-element.291), calls=%async_computation.1 | async-start | bytes 1048576 | tf_op jit(solution)/shard_map/all_to_all | solution.py:347
  46.7 2.4 %collective-permute-start.12 = (bf16[64,32,128]{2,1,0:T(8,128)(2,1)S(1)}, bf16[64,32,128]{2,1,0:T(8,128)(2,1)S(1)}, u32[]{:S(2)}, u32[]{:S(2)}) collective-permute-start(bf16[64,32,128]{2,1,0:T(8,128)(2,1)S(1)} %bitcast.96), channel_id=1, source_target_pairs={{0,1},{1,0},{2,3},{3,2},{4,5},{5,4},{6,7},{7,6},{8,9},{9,8},{10,11... | collective-permute-start | bytes 1572872 | tf_op jit(solution)/shard_map/ppermute | solution.py:288
  47.5 14.7 %collective-permute-start.13 = (bf16[64,32,128]{2,1,0:T(8,128)(2,1)S(1)}, bf16[64,32,128]{2,1,0:T(8,128)(2,1)S(1)}, u32[]{:S(2)}, u32[]{:S(2)}) collective-permute-start(bf16[64,32,128]{2,1,0:T(8,128)(2,1)S(1)} %bitcast.97), channel_id=1, source_target_pairs={{0,32},{1,33},{2,34},{3,35},{4,36},{5,37},{6,38},{7,39},{8,40},{9,... | collective-permute-start | bytes 1572872 | tf_op jit(solution)/shard_map/ppermute | solution.py:288
  51.1 15.1 %all-to-all-start.2 = ((bf16[16,4,32,128]{3,2,1,0:T(8,128)(2,1)}), bf16[16,4,32,128]{3,2,1,0:T(8,128)(2,1)S(1)}, u32[]{:S(2)}, u32[]{:S(2)}) async-start(bf16[16,4,32,128]{3,2,1,0:T(8,128)(2,1)} %get-tuple-element.297), calls=%async_computation.2 | async-start | bytes 1048576 | tf_op jit(solution)/shard_map/all_to_all | solution.py:347
  66.2 2.5 %collective-permute-start.14 = (bf16[64,32,128]{2,1,0:T(8,128)(2,1)S(1)}, bf16[64,32,128]{2,1,0:T(8,128)(2,1)S(1)}, u32[]{:S(2)}, u32[]{:S(2)}) collective-permute-start(bf16[64,32,128]{2,1,0:T(8,128)(2,1)S(1)} %bitcast.104), channel_id=1, source_target_pairs={{0,1},{1,0},{2,3},{3,2},{4,5},{5,4},{6,7},{7,6},{8,9},{9,8},{10,11... | collective-permute-start | bytes 1572872 | tf_op jit(solution)/shard_map/ppermute | solution.py:288
  67.2 14.7 %collective-permute-start.15 = (bf16[64,32,128]{2,1,0:T(8,128)(2,1)S(1)}, bf16[64,32,128]{2,1,0:T(8,128)(2,1)S(1)}, u32[]{:S(2)}, u32[]{:S(2)}) collective-permute-start(bf16[64,32,128]{2,1,0:T(8,128)(2,1)S(1)} %bitcast.105), channel_id=1, source_target_pairs={{0,32},{1,33},{2,34},{3,35},{4,36},{5,37},{6,38},{7,39},{8,40},{9,... | collective-permute-start | bytes 1572872 | tf_op jit(solution)/shard_map/ppermute | solution.py:288
  70.8 15.3 %all-to-all-start.3 = ((bf16[16,4,32,128]{3,2,1,0:T(8,128)(2,1)}), bf16[16,4,32,128]{3,2,1,0:T(8,128)(2,1)S(1)}, u32[]{:S(2)}, u32[]{:S(2)}) async-start(bf16[16,4,32,128]{3,2,1,0:T(8,128)(2,1)} %get-tuple-element.303), calls=%async_computation.3 | async-start | bytes 1048576 | tf_op jit(solution)/shard_map/all_to_all | solution.py:347
  86.1 2.4 %collective-permute-start.16 = (bf16[64,32,128]{2,1,0:T(8,128)(2,1)S(1)}, bf16[64,32,128]{2,1,0:T(8,128)(2,1)S(1)}, u32[]{:S(2)}, u32[]{:S(2)}) collective-permute-start(bf16[64,32,128]{2,1,0:T(8,128)(2,1)S(1)} %bitcast.108), channel_id=1, source_target_pairs={{0,1},{1,0},{2,3},{3,2},{4,5},{5,4},{6,7},{7,6},{8,9},{9,8},{10,11... | collective-permute-start | bytes 1572872 | tf_op jit(solution)/shard_map/ppermute | solution.py:288
  87.0 14.7 %collective-permute-start.17 = (bf16[64,32,128]{2,1,0:T(8,128)(2,1)S(1)}, bf16[64,32,128]{2,1,0:T(8,128)(2,1)S(1)}, u32[]{:S(2)}, u32[]{:S(2)}) collective-permute-start(bf16[64,32,128]{2,1,0:T(8,128)(2,1)S(1)} %bitcast.109), channel_id=1, source_target_pairs={{0,32},{1,33},{2,34},{3,35},{4,36},{5,37},{6,38},{7,39},{8,40},{9,... | collective-permute-start | bytes 1572872 | tf_op jit(solution)/shard_map/ppermute | solution.py:288
  90.6 15.1 %all-to-all-start.4 = ((bf16[16,4,32,128]{3,2,1,0:T(8,128)(2,1)}), bf16[16,4,32,128]{3,2,1,0:T(8,128)(2,1)S(1)}, u32[]{:S(2)}, u32[]{:S(2)}) async-start(bf16[16,4,32,128]{3,2,1,0:T(8,128)(2,1)} %get-tuple-element.309), calls=%async_computation.4 | async-start | bytes 1048576 | tf_op jit(solution)/shard_map/all_to_all | solution.py:347
  105.7 2.5 %collective-permute-start.18 = (bf16[64,32,128]{2,1,0:T(8,128)(2,1)S(1)}, bf16[64,32,128]{2,1,0:T(8,128)(2,1)S(1)}, u32[]{:S(2)}, u32[]{:S(2)}) collective-permute-start(bf16[64,32,128]{2,1,0:T(8,128)(2,1)S(1)} %bitcast.100), channel_id=1, source_target_pairs={{0,1},{1,0},{2,3},{3,2},{4,5},{5,4},{6,7},{7,6},{8,9},{9,8},{10,11... | collective-permute-start | bytes 1572872 | tf_op jit(solution)/shard_map/ppermute | solution.py:288
  106.7 14.7 %collective-permute-start.19 = (bf16[64,32,128]{2,1,0:T(8,128)(2,1)S(1)}, bf16[64,32,128]{2,1,0:T(8,128)(2,1)S(1)}, u32[]{:S(2)}, u32[]{:S(2)}) collective-permute-start(bf16[64,32,128]{2,1,0:T(8,128)(2,1)S(1)} %bitcast.101), channel_id=1, source_target_pairs={{0,32},{1,33},{2,34},{3,35},{4,36},{5,37},{6,38},{7,39},{8,40},{9,... | collective-permute-start | bytes 1572872 | tf_op jit(solution)/shard_map/ppermute | solution.py:288
  110.3 14.3 %all-to-all-start.5 = ((bf16[16,4,32,128]{3,2,1,0:T(8,128)(2,1)}), bf16[16,4,32,128]{3,2,1,0:T(8,128)(2,1)S(1)}, u32[]{:S(2)}, u32[]{:S(2)}) async-start(bf16[16,4,32,128]{3,2,1,0:T(8,128)(2,1)} %get-tuple-element.315), calls=%async_computation.5 | async-start | bytes 1048576 | tf_op jit(solution)/shard_map/all_to_all | solution.py:347
  124.6 3.3 %collective-permute-start.20 = (bf16[64,32,128]{2,1,0:T(8,128)(2,1)S(1)}, bf16[64,32,128]{2,1,0:T(8,128)(2,1)S(1)}, u32[]{:S(2)}, u32[]{:S(2)}) collective-permute-start(bf16[64,32,128]{2,1,0:T(8,128)(2,1)S(1)} %bitcast.84), channel_id=1, source_target_pairs={{0,1},{1,0},{2,3},{3,2},{4,5},{5,4},{6,7},{7,6},{8,9},{9,8},{10,11... | collective-permute-start | bytes 1572872 | tf_op jit(solution)/shard_map/ppermute | solution.py:288
  126.3 14.8 %collective-permute-start.21 = (bf16[64,32,128]{2,1,0:T(8,128)(2,1)S(1)}, bf16[64,32,128]{2,1,0:T(8,128)(2,1)S(1)}, u32[]{:S(2)}, u32[]{:S(2)}) collective-permute-start(bf16[64,32,128]{2,1,0:T(8,128)(2,1)S(1)} %bitcast.85), channel_id=1, source_target_pairs={{0,32},{1,33},{2,34},{3,35},{4,36},{5,37},{6,38},{7,39},{8,40},{9,... | collective-permute-start | bytes 1572872 | tf_op jit(solution)/shard_map/ppermute | solution.py:288
  129.3 14.3 %all-to-all-start.6 = ((bf16[16,4,32,128]{3,2,1,0:T(8,128)(2,1)}), bf16[16,4,32,128]{3,2,1,0:T(8,128)(2,1)S(1)}, u32[]{:S(2)}, u32[]{:S(2)}) async-start(bf16[16,4,32,128]{3,2,1,0:T(8,128)(2,1)} %get-tuple-element.321), calls=%async_computation.6 | async-start | bytes 1048576 | tf_op jit(solution)/shard_map/all_to_all | solution.py:347
  143.6 3.3 %collective-permute-start.22 = (bf16[64,32,128]{2,1,0:T(8,128)(2,1)S(1)}, bf16[64,32,128]{2,1,0:T(8,128)(2,1)S(1)}, u32[]{:S(2)}, u32[]{:S(2)}) collective-permute-start(bf16[64,32,128]{2,1,0:T(8,128)(2,1)S(1)} %bitcast.88), channel_id=1, source_target_pairs={{0,1},{1,0},{2,3},{3,2},{4,5},{5,4},{6,7},{7,6},{8,9},{9,8},{10,11... | collective-permute-start | bytes 1572872 | tf_op jit(solution)/shard_map/ppermute | solution.py:288
  145.4 14.8 %collective-permute-start.23 = (bf16[64,32,128]{2,1,0:T(8,128)(2,1)S(1)}, bf16[64,32,128]{2,1,0:T(8,128)(2,1)S(1)}, u32[]{:S(2)}, u32[]{:S(2)}) collective-permute-start(bf16[64,32,128]{2,1,0:T(8,128)(2,1)S(1)} %bitcast.89), channel_id=1, source_target_pairs={{0,32},{1,33},{2,34},{3,35},{4,36},{5,37},{6,38},{7,39},{8,40},{9,... | collective-permute-start | bytes 1572872 | tf_op jit(solution)/shard_map/ppermute | solution.py:288
  148.3 14.5 %all-to-all-start.7 = ((bf16[16,4,32,128]{3,2,1,0:T(8,128)(2,1)}), bf16[16,4,32,128]{3,2,1,0:T(8,128)(2,1)S(1)}, u32[]{:S(2)}, u32[]{:S(2)}) async-start(bf16[16,4,32,128]{3,2,1,0:T(8,128)(2,1)} %get-tuple-element.327), calls=%async_computation.7 | async-start | bytes 1048576 | tf_op jit(solution)/shard_map/all_to_all | solution.py:347
  162.8 3.3 %collective-permute-start.24 = (bf16[64,32,128]{2,1,0:T(8,128)(2,1)S(1)}, bf16[64,32,128]{2,1,0:T(8,128)(2,1)S(1)}, u32[]{:S(2)}, u32[]{:S(2)}) collective-permute-start(bf16[64,32,128]{2,1,0:T(8,128)(2,1)S(1)} %bitcast.92), channel_id=1, source_target_pairs={{0,1},{1,0},{2,3},{3,2},{4,5},{5,4},{6,7},{7,6},{8,9},{9,8},{10,11... | collective-permute-start | bytes 1572872 | tf_op jit(solution)/shard_map/ppermute | solution.py:288
  164.6 14.8 %collective-permute-start.25 = (bf16[64,32,128]{2,1,0:T(8,128)(2,1)S(1)}, bf16[64,32,128]{2,1,0:T(8,128)(2,1)S(1)}, u32[]{:S(2)}, u32[]{:S(2)}) collective-permute-start(bf16[64,32,128]{2,1,0:T(8,128)(2,1)S(1)} %bitcast.93), channel_id=1, source_target_pairs={{0,32},{1,33},{2,34},{3,35},{4,36},{5,37},{6,38},{7,39},{8,40},{9,... | collective-permute-start | bytes 1572872 | tf_op jit(solution)/shard_map/ppermute | solution.py:288
  167.6 14.3 %all-to-all-start.8 = ((bf16[16,4,32,128]{3,2,1,0:T(8,128)(2,1)}), bf16[16,4,32,128]{3,2,1,0:T(8,128)(2,1)S(1)}, u32[]{:S(2)}, u32[]{:S(2)}) async-start(bf16[16,4,32,128]{3,2,1,0:T(8,128)(2,1)} %get-tuple-element.333), calls=%async_computation.8 | async-start | bytes 1048576 | tf_op jit(solution)/shard_map/all_to_all | solution.py:347
  181.8 3.3 %collective-permute-start.26 = (bf16[64,32,128]{2,1,0:T(8,128)(2,1)S(1)}, bf16[64,32,128]{2,1,0:T(8,128)(2,1)S(1)}, u32[]{:S(2)}, u32[]{:S(2)}) collective-permute-start(bf16[64,32,128]{2,1,0:T(8,128)(2,1)S(1)} %bitcast.77), channel_id=1, source_target_pairs={{0,1},{1,0},{2,3},{3,2},{4,5},{5,4},{6,7},{7,6},{8,9},{9,8},{10,11... | collective-permute-start | bytes 1572872 | tf_op jit(solution)/shard_map/ppermute | solution.py:288
  183.6 15.4 %collective-permute-start.27 = (bf16[64,32,128]{2,1,0:T(8,128)(2,1)S(1)}, bf16[64,32,128]{2,1,0:T(8,128)(2,1)S(1)}, u32[]{:S(2)}, u32[]{:S(2)}) collective-permute-start(bf16[64,32,128]{2,1,0:T(8,128)(2,1)S(1)} %bitcast.78), channel_id=1, source_target_pairs={{0,32},{1,33},{2,34},{3,35},{4,36},{5,37},{6,38},{7,39},{8,40},{9,... | collective-permute-start | bytes 1572872 | tf_op jit(solution)/shard_map/ppermute | solution.py:288
  187.2 15.0 %all-to-all-start.9 = ((bf16[16,4,32,128]{3,2,1,0:T(8,128)(2,1)}), bf16[16,4,32,128]{3,2,1,0:T(8,128)(2,1)S(1)}, u32[]{:S(2)}, u32[]{:S(2)}) async-start(bf16[16,4,32,128]{3,2,1,0:T(8,128)(2,1)} %get-tuple-element.339), calls=%async_computation.9 | async-start | bytes 1048576 | tf_op jit(solution)/shard_map/all_to_all | solution.py:347
  202.2 2.6 %collective-permute-start.28 = (bf16[64,32,128]{2,1,0:T(8,128)(2,1)S(1)}, bf16[64,32,128]{2,1,0:T(8,128)(2,1)S(1)}, u32[]{:S(2)}, u32[]{:S(2)}) collective-permute-start(bf16[64,32,128]{2,1,0:T(8,128)(2,1)S(1)} %bitcast.73), channel_id=1, source_target_pairs={{0,1},{1,0},{2,3},{3,2},{4,5},{5,4},{6,7},{7,6},{8,9},{9,8},{10,11... | collective-permute-start | bytes 1572872 | tf_op jit(solution)/shard_map/ppermute | solution.py:288
  203.3 16.0 %collective-permute-start.29 = (bf16[64,32,128]{2,1,0:T(8,128)(2,1)S(1)}, bf16[64,32,128]{2,1,0:T(8,128)(2,1)S(1)}, u32[]{:S(2)}, u32[]{:S(2)}) collective-permute-start(bf16[64,32,128]{2,1,0:T(8,128)(2,1)S(1)} %bitcast.74), channel_id=1, source_target_pairs={{0,32},{1,33},{2,34},{3,35},{4,36},{5,37},{6,38},{7,39},{8,40},{9,... | collective-permute-start | bytes 1572872 | tf_op jit(solution)/shard_map/ppermute | solution.py:288
  206.2 14.3 %all-to-all-start.10 = ((bf16[16,4,32,128]{3,2,1,0:T(8,128)(2,1)}), bf16[16,4,32,128]{3,2,1,0:T(8,128)(2,1)S(1)}, u32[]{:S(2)}, u32[]{:S(2)}) async-start(bf16[16,4,32,128]{3,2,1,0:T(8,128)(2,1)} %get-tuple-element.345), calls=%async_computation.10 | async-start | bytes 1048576 | tf_op jit(solution)/shard_map/all_to_all | solution.py:347
  220.5 3.3 %collective-permute-start.30 = (bf16[64,32,128]{2,1,0:T(8,128)(2,1)S(1)}, bf16[64,32,128]{2,1,0:T(8,128)(2,1)S(1)}, u32[]{:S(2)}, u32[]{:S(2)}) collective-permute-start(bf16[64,32,128]{2,1,0:T(8,128)(2,1)S(1)} %bitcast.81), channel_id=1, source_target_pairs={{0,1},{1,0},{2,3},{3,2},{4,5},{5,4},{6,7},{7,6},{8,9},{9,8},{10,11... | collective-permute-start | bytes 1572872 | tf_op jit(solution)/shard_map/ppermute | solution.py:288
  (13 other events, 44.4 us)

commit v5 on v4

--- a/solution.py
+++ b/solution.py
@@ -73,7 +73,11 @@
 def row_sums(pick, index_ref, w_ref, row):
     blocks = w_ref.shape[1]
     edge = w_ref.shape[2]
-    picked = jnp.concatenate([pick(index_ref[row * blocks + k]) for k in range(blocks)], axis=1)
+    if len(index_ref.shape) == 1:
+        index = [index_ref[row * blocks + k] for k in range(blocks)]
+    else:
+        index = [index_ref[row // 4, row % 4, k] for k in range(blocks)]
+    picked = jnp.concatenate([pick(i) for i in index], axis=1)
     return jnp.dot(picked, w_ref[row].reshape(blocks * edge, edge), preferred_element_type=F32)
 
 
@@ -191,20 +195,23 @@
     )
 
 
-def first_kernel(layer_ref, index_ref, inputs_ref, w_hbm, bias_ref, cell_out, rows_out, send_out, fresh_ref, w_out, arrived, loaded, spread_ref, sent):
+def first_kernel(layer_ref, index_ref, inputs_ref, w_hbm, bias_hbm, cell_out, rows_out, send_out, bias_ref, told, fresh_ref, w_out, arrived, loaded, spread_ref, sent):
     per_device, row_count, edge = cell_out.shape
 
     @pl.when(layer_ref[0] == 0)
     def _():
         fresh = pltpu.make_async_copy(inputs_ref.at[0], fresh_ref, arrived)
+        bias = pltpu.make_async_copy(bias_hbm, bias_ref, told)
+        bias.start()
         fresh.start()
         copies = stream(w_hbm, w_out, loaded)
+        bias.wait()
         fresh.wait()
         sender = Sender(send_out, spread_ref, sent)
         pick = from_rows(fresh_ref, edge)
         for j, copy in enumerate(copies):
             copy.wait()
-            sums = [row_sums(pick, index_ref, w_out, 4 * j + g) + bias_ref[4 * j + g] for g in range(4)]
+            sums = [row_sums(pick, index_ref, w_out, 4 * j + g) + bias_ref[g:g + 1, j * edge:(j + 1) * edge] for g in range(4)]
             cell_out[j], output = gates_to_state(sums, jnp.zeros((row_count, edge), F32))
             rows_out[:, j * edge:(j + 1) * edge] = output
             sender.put(j, output)
@@ -226,18 +233,25 @@
     return pl.pallas_call(
         first_kernel,
         out_shape=state_out((per_device, row_count, edge), peers),
-        in_specs=[smem(), smem(), hbm(), hbm(), vmem()],
+        in_specs=[smem(), smem(), hbm(), hbm(), hbm()],
         out_specs=(vmem(), vmem(), hbm()),
-        scratch_shapes=fresh_scratch(inputs, w, per_device) + send_scratch((per_device, row_count, edge), peers),
+        scratch_shapes=[pltpu.VMEM(bias.shape, F32), pltpu.SemaphoreType.DMA] + fresh_scratch(inputs, w, per_device) + send_scratch((per_device, row_count, edge), peers),
         compiler_params=pltpu.CompilerParams(vmem_limit_bytes=12 * MIB),
         name="first_step",
-    )(layer, index, unmoved(inputs), unmoved(w), held(bias))
+    )(layer, index, unmoved(inputs), unmoved(w), unmoved(bias))
 
 
 def state_kernel(tick, step_count, layer_ref, index_ref, mine_ref, other_ref, w_ref, partial_ref, cell_ref, token_ref, cell_out, rows_out, send_out, spread_ref, sent):
     step = tick - LAG * layer_ref[0]
     active = (step >= 0) & (step < step_count)
     per_device, _, edge = cell_ref.shape
+    last = len(cell_out.shape) == 2
+
+    def put_cell(j, cell):
+        if last:
+            cell_out[:, j * edge:(j + 1) * edge] = cell
+        else:
+            cell_out[j] = cell
 
     @pl.when(active)
     def _():
@@ -245,25 +259,31 @@
         sender = Sender(send_out, spread_ref, sent)
         for j in range(per_device):
             sums = [partial_ref[4 * j + g] + row_sums(pick, index_ref, w_ref, 4 * j + g) for g in range(4)]
-            cell_out[j], output = gates_to_state(sums, cell_ref[j])
+            cell, output = gates_to_state(sums, cell_ref[j])
+            put_cell(j, cell)
             rows_out[:, j * edge:(j + 1) * edge] = output
-            sender.put(j, output)
+            if not last:
+                sender.put(j, output)
         sender.finish()
 
     @pl.when(jnp.logical_not(active))
     def _():
         idle = Sender(send_out, spread_ref, sent)
         for j in range(per_device):
-            idle.put(j, jnp.zeros(cell_ref.shape[1:], BF16))
-        cell_out[...] = cell_ref[...]
+            if not last:
+                idle.put(j, jnp.zeros(cell_ref.shape[1:], BF16))
+            put_cell(j, cell_ref[j])
         rows_out[...] = jnp.zeros_like(rows_out)
         idle.finish()
 
 
-def state_step(tick, layer, index, state, w, partial, cell, step_count, peers, token):
+def state_step(tick, layer, index, state, w, partial, cell, step_count, peers, token, last):
+    outs = state_out(cell.shape, peers)
+    if last:
+        outs = (jax.ShapeDtypeStruct(outs[1].shape, F32), *outs[1:])
     return pl.pallas_call(
         functools.partial(state_kernel, tick, step_count),
-        out_shape=state_out(cell.shape, peers),
+        out_shape=outs,
         in_specs=[smem(), smem()] + [vmem()] * 6,
         out_specs=(vmem(), vmem(), hbm()),
         scratch_shapes=send_scratch(cell.shape, peers),
@@ -339,8 +359,8 @@
     tick_count = step_count + LAG * (layers - 1)
     steps = [tick - LAG * layer for tick in range(tick_count)]
     fed = [(layer > 0) & (step >= 0) & (step < step_count) for step in steps]
-    layer_ref, fed, in_index, rec_index = lax.optimization_barrier((layer_ref, fed, in_index, rec_index))
-    cell, out_rows, send = first_step(layer_ref, in_index, inputs, w_in, offsets, per_device, chips)
+    layer_ref, fed = lax.optimization_barrier((layer_ref, fed))
+    cell, out_rows, send = first_step(layer_ref, in_cols[0], inputs, w_in, bias[0], per_device, chips)
     arrived = {}
     outputs = [out_rows]
     for tick in range(1, tick_count):
@@ -356,11 +376,14 @@
         if tick <= tick_count - LAG:
             arrived[tick - 1] = upward(mine)
         state = (mine, other)
-        cell, out_rows, send = state_step(tick, layer_ref, rec_index, state, w_rec, partial, cell, step_count, chips, mark(mine, 1024 * w_rec.size))
+        token = mark(mine, 1024 * w_rec.size)
+        last = tick == tick_count - 1
+        cell, out_rows, send = state_step(
+            tick, layer_ref, rec_index, state, w_rec, partial, cell, step_count, chips, token, last
+        )
         outputs.append(out_rows)
     sequence = lax.dynamic_slice_in_dim(jnp.stack(outputs), LAG * layer, step_count, 0)
-    cells = cell.transpose(1, 0, 2).reshape(row_count, per_device * edge)
-    return sequence[None], cells[None]
+    return sequence[None], cell[None]
 
 
 def solution(mesh):

time: 229 us -> 228 us (level)
  transfers between devices with their start and end apart: 32 -> 32, of which waited for: 28 -> 29; matrix products, arithmetic and copies ran while one was open for 0% -> 0% of each run, Pallas kernels for 17% -> 17%
where the time goes in v5:
time: 228 us; the launch traced here: 225 us
  waiting for transfers between devices  117 us (51%)
  starting transfers between devices  60.4 us (26%)
  Pallas kernels  43.3 us (19%)
  local copies, waits for them, and re-layouts  3.18 us (1%)
    ppermute x21, waiting for transfers between devices, exchange(): return lax.ppermute(x, ('pipe',) + WIDTH, route)  94.7 us
    all_to_all x11, starting transfers between devices, body(): mine = lax.all_to_all(send, ('y', 'x'), 0, 0).reshape(half, row_count, edge)  43.7 us
    all_to_all x11, waiting for transfers between devices, body(): mine = lax.all_to_all(send, ('y', 'x'), 0, 0).reshape(half, row_count, edge)  21.9 us
    pallas_call x5, Pallas kernels, fresh_sums(): pl.pallas_call(functools.partial(fresh_kernel, tick), out_shape=pltpu.VME...  19.7 us
    pallas_call x11, Pallas kernels, state_step(): pl.pallas_call(functools.partial(state_kernel, tick, step_count), out_sha...  18.8 us
    ppermute x21, starting transfers between devices, exchange(): return lax.ppermute(x, ('pipe',) + WIDTH, route)  16.7 us
    pallas_call x1, Pallas kernels, first_step(): pl.pallas_call(first_kernel, out_shape=state_out((per_device, row_count,...  4.84 us
  transfers between devices with their start and end apart: 32, of which 29 were waited for; matrix products, arithmetic and copies ran while one was open for 0% of the time, Pallas kernels for 17%

profile of v5, /device:TPU:1, one launch (start us, length us, event | category | flops | bytes accessed | tf_op | source)
XLA Modules:
  0.0 225.0 jit_solution(14922660643959056631)
XLA Ops:
  1.4 4.8 %first_step.1 = (f32[4,32,128]{2,1,0:T(8,128)S(1)}, bf16[32,512]{1,0:T(8,128)(2,1)S(1)}, bf16[16,4,32,128]{3,2,1,0:T(8,128)(2,1)}) custom-call(s32[1]{0:T(128)} %bitcast.layer_ref, s32[4,4,8]{2,1,0:T(4,128)S(1)} %bitcast.118, bf16[6,32,16384]{2,1,0:T(8,128)(2,1)} %inputs_ref.3, bf16[16,8,128,128]{3,2,1,0:T(8,128)(2,1)} %bitcast.119, f32[4,512]{1,0:T(4,128)} %bitcast.102), custom_call_target="tpu_custom_call" | custom-call | tf_op jit(solution)/shard_map/first_step/pallas_call | solution.py:233
  6.2 7.6 %all-to-all-start = ((bf16[16,4,32,128]{3,2,1,0:T(8,128)(2,1)}), bf16[16,4,32,128]{3,2,1,0:T(8,128)(2,1)S(1)}, u32[]{:S(2)}, u32[]{:S(2)}) async-start(bf16[16,4,32,128]{3,2,1,0:T(8,128)(2,1)} %get-tuple-element.282), calls=%async_computation | async-start | bytes 1048576 | tf_op jit(solution)/shard_map/all_to_all | solution.py:367
  14.0 3.9 %fresh_sums.9.partial_ref = f32[16,32,128]{2,1,0:T(8,128)S(1)} custom-call(s32[1]{0:T(128)} %bitcast.layer_ref, s32[128]{0:T(128)S(1)} %broadcast_select_fusion.index_ref, bf16[6,32,16384]{2,1,0:T(8,128)(2,1)} %inputs_ref.3, bf16[16,8,128,128]{3,2,1,0:T(8,128)(2,1)} %bitcast.120, f32[16,1,128]{2,1,0:T(1,128)S(1)} %bitcast.103), custom_call_target="tpu_custom_call" | custom-call | flops 134217728 | bytes 4194304 | tf_op jit(solution)/shard_map/fresh_sums/pallas_call | solution.py:145
  17.9 6.4 %all-to-all-done = bf16[16,4,32,128]{3,2,1,0:T(8,128)(2,1)S(1)} async-done(((bf16[16,4,32,128]{3,2,1,0:T(8,128)(2,1)}), bf16[16,4,32,128]{3,2,1,0:T(8,128)(2,1)S(1)}, u32[]{:S(2)}, u32[]{:S(2)}) %all-to-all-start) | async-done | bytes 524320 | tf_op jit(solution)/shard_map/all_to_all | solution.py:367
  30.7 3.6 %all-to-all-start.1 = ((bf16[16,4,32,128]{3,2,1,0:T(8,128)(2,1)}), bf16[16,4,32,128]{3,2,1,0:T(8,128)(2,1)S(1)}, u32[]{:S(2)}, u32[]{:S(2)}) async-start(bf16[16,4,32,128]{3,2,1,0:T(8,128)(2,1)} %get-tuple-element.287), calls=%async_computation.1 | async-start | bytes 1048576 | tf_op jit(solution)/shard_map/all_to_all | solution.py:367
  34.3 7.0 %collective-permute-done.11 = bf16[64,32,128]{2,1,0:T(8,128)(2,1)S(1)} collective-permute-done((bf16[64,32,128]{2,1,0:T(8,128)(2,1)S(1)}, bf16[64,32,128]{2,1,0:T(8,128)(2,1)S(1)}, u32[]{:S(2)}, u32[]{:S(2)}) %collective-permute-start.11) | collective-permute-done | bytes 524320 | tf_op jit(solution)/shard_map/ppermute | solution.py:308
  41.3 4.0 %conditional.10 = (f32[16,32,128]{2,1,0:T(8,128)S(1)}) conditional(s32[]{:T(128)} %convert_element_type.30, (s32[1]{0:T(128)}, s32[128]{0:T(128)S(1)}, bf16[6,32,16384]{2,1,0:T(8,128)(2,1)}, bf16[16,8,128,128]{3,2,1,0:T(8,128)(2,1)}, f32[16,1,128]{2,1,0:T(1,128)S(1)}) %tuple.145, (bf16[64,32,128]{2,1,0:T(8,128)(2,1)S(1)}, ...), branch_computations={%region_0.1_spmd, %region_1.2_spmd} | conditional | flops 134217728 | bytes 8388656 | solution.py:373
  41.3 4.0 %fresh_sums.5 = f32[16,32,128]{2,1,0:T(8,128)S(1)} custom-call(s32[1]{0:T(128)} %get-tuple-element.139.layer_ref, s32[128]{0:T(128)S(1)} %get-tuple-element.140.index_ref, bf16[6,32,16384]{2,1,0:T(8,128)(2,1)} %get-tuple-element.141.inputs_ref, bf16[16,8,128,128]{3,2,1,0:T(8,128)(2,1)} %get-tuple-element.142.w_hbm, f32[16,1,128]{2,1,0:T(1,128)S(1)} %get-tuple-element.148.bias_ref), custom_call_target="tpu_custom_call" | custom-call | flops 134217728 | bytes 4194304 | tf_op jit(solution)/shard_map/cond/branch_0_fun/fresh_sums/pallas_call | solution.py:145
  50.4 3.6 %all-to-all-start.2 = ((bf16[16,4,32,128]{3,2,1,0:T(8,128)(2,1)}), bf16[16,4,32,128]{3,2,1,0:T(8,128)(2,1)S(1)}, u32[]{:S(2)}, u32[]{:S(2)}) async-start(bf16[16,4,32,128]{3,2,1,0:T(8,128)(2,1)} %get-tuple-element.293), calls=%async_computation.2 | async-start | bytes 1048576 | tf_op jit(solution)/shard_map/all_to_all | solution.py:367
  54.0 7.5 %collective-permute-done.13 = bf16[64,32,128]{2,1,0:T(8,128)(2,1)S(1)} collective-permute-done((bf16[64,32,128]{2,1,0:T(8,128)(2,1)S(1)}, bf16[64,32,128]{2,1,0:T(8,128)(2,1)S(1)}, u32[]{:S(2)}, u32[]{:S(2)}) %collective-permute-start.13) | collective-permute-done | bytes 524320 | tf_op jit(solution)/shard_map/ppermute | solution.py:308
  61.6 3.9 %conditional.11 = (f32[16,32,128]{2,1,0:T(8,128)S(1)}) conditional(s32[]{:T(128)} %convert_element_type.31, (s32[1]{0:T(128)}, s32[128]{0:T(128)S(1)}, bf16[6,32,16384]{2,1,0:T(8,128)(2,1)}, bf16[16,8,128,128]{3,2,1,0:T(8,128)(2,1)}, f32[16,1,128]{2,1,0:T(1,128)S(1)}) %tuple.147, (bf16[64,32,128]{2,1,0:T(8,128)(2,1)S(1)}, ...), branch_computations={%region_2.3_spmd, %region_3.4_spmd} | conditional | flops 134217728 | bytes 8388656 | solution.py:373
  61.6 3.9 %fresh_sums.6 = f32[16,32,128]{2,1,0:T(8,128)S(1)} custom-call(s32[1]{0:T(128)} %get-tuple-element.154.layer_ref, s32[128]{0:T(128)S(1)} %get-tuple-element.160.index_ref, bf16[6,32,16384]{2,1,0:T(8,128)(2,1)} %get-tuple-element.161.inputs_ref, bf16[16,8,128,128]{3,2,1,0:T(8,128)(2,1)} %get-tuple-element.162.w_hbm, f32[16,1,128]{2,1,0:T(1,128)S(1)} %get-tuple-element.163.bias_ref), custom_call_target="tpu_custom_call" | custom-call | flops 134217728 | bytes 4194304 | tf_op jit(solution)/shard_map/cond/branch_0_fun/fresh_sums/pallas_call | solution.py:145
  70.1 3.6 %all-to-all-start.3 = ((bf16[16,4,32,128]{3,2,1,0:T(8,128)(2,1)}), bf16[16,4,32,128]{3,2,1,0:T(8,128)(2,1)S(1)}, u32[]{:S(2)}, u32[]{:S(2)}) async-start(bf16[16,4,32,128]{3,2,1,0:T(8,128)(2,1)} %get-tuple-element.299), calls=%async_computation.3 | async-start | bytes 1048576 | tf_op jit(solution)/shard_map/all_to_all | solution.py:367
  73.7 7.5 %collective-permute-done.15 = bf16[64,32,128]{2,1,0:T(8,128)(2,1)S(1)} collective-permute-done((bf16[64,32,128]{2,1,0:T(8,128)(2,1)S(1)}, bf16[64,32,128]{2,1,0:T(8,128)(2,1)S(1)}, u32[]{:S(2)}, u32[]{:S(2)}) %collective-permute-start.15) | collective-permute-done | bytes 524320 | tf_op jit(solution)/shard_map/ppermute | solution.py:308
  81.2 4.1 %conditional.12 = (f32[16,32,128]{2,1,0:T(8,128)S(1)}) conditional(s32[]{:T(128)} %convert_element_type.32, (s32[1]{0:T(128)}, s32[128]{0:T(128)S(1)}, bf16[6,32,16384]{2,1,0:T(8,128)(2,1)}, bf16[16,8,128,128]{3,2,1,0:T(8,128)(2,1)}, f32[16,1,128]{2,1,0:T(1,128)S(1)}) %tuple.149, (bf16[64,32,128]{2,1,0:T(8,128)(2,1)S(1)}, ...), branch_computations={%region_4.5_spmd, %region_5.6_spmd} | conditional | flops 134217728 | bytes 8388656 | solution.py:373
  81.2 3.9 %fresh_sums.7 = f32[16,32,128]{2,1,0:T(8,128)S(1)} custom-call(s32[1]{0:T(128)} %get-tuple-element.168.layer_ref, s32[128]{0:T(128)S(1)} %get-tuple-element.169.index_ref, bf16[6,32,16384]{2,1,0:T(8,128)(2,1)} %get-tuple-element.170.inputs_ref, bf16[16,8,128,128]{3,2,1,0:T(8,128)(2,1)} %get-tuple-element.171.w_hbm, f32[16,1,128]{2,1,0:T(1,128)S(1)} %get-tuple-element.172.bias_ref), custom_call_target="tpu_custom_call" | custom-call | flops 134217728 | bytes 4194304 | tf_op jit(solution)/shard_map/cond/branch_0_fun/fresh_sums/pallas_call | solution.py:145
  89.9 3.6 %all-to-all-start.4 = ((bf16[16,4,32,128]{3,2,1,0:T(8,128)(2,1)}), bf16[16,4,32,128]{3,2,1,0:T(8,128)(2,1)S(1)}, u32[]{:S(2)}, u32[]{:S(2)}) async-start(bf16[16,4,32,128]{3,2,1,0:T(8,128)(2,1)} %get-tuple-element.305), calls=%async_computation.4 | async-start | bytes 1048576 | tf_op jit(solution)/shard_map/all_to_all | solution.py:367
  93.5 7.5 %collective-permute-done.17 = bf16[64,32,128]{2,1,0:T(8,128)(2,1)S(1)} collective-permute-done((bf16[64,32,128]{2,1,0:T(8,128)(2,1)S(1)}, bf16[64,32,128]{2,1,0:T(8,128)(2,1)S(1)}, u32[]{:S(2)}, u32[]{:S(2)}) %collective-permute-start.17) | collective-permute-done | bytes 524320 | tf_op jit(solution)/shard_map/ppermute | solution.py:308
  101.0 3.9 %conditional.13 = (f32[16,32,128]{2,1,0:T(8,128)S(1)}) conditional(s32[]{:T(128)} %convert_element_type.33, (s32[1]{0:T(128)}, s32[128]{0:T(128)S(1)}, bf16[6,32,16384]{2,1,0:T(8,128)(2,1)}, bf16[16,8,128,128]{3,2,1,0:T(8,128)(2,1)}, f32[16,1,128]{2,1,0:T(1,128)S(1)}) %tuple.151, (bf16[64,32,128]{2,1,0:T(8,128)(2,1)S(1)}, ...), branch_computations={%region_6.7_spmd, %region_7.8_spmd} | conditional | flops 134217728 | bytes 8388656 | solution.py:373
  101.0 3.9 %fresh_sums.8 = f32[16,32,128]{2,1,0:T(8,128)S(1)} custom-call(s32[1]{0:T(128)} %get-tuple-element.177.layer_ref, s32[128]{0:T(128)S(1)} %get-tuple-element.178.index_ref, bf16[6,32,16384]{2,1,0:T(8,128)(2,1)} %get-tuple-element.179.inputs_ref, bf16[16,8,128,128]{3,2,1,0:T(8,128)(2,1)} %get-tuple-element.180.w_hbm, f32[16,1,128]{2,1,0:T(1,128)S(1)} %get-tuple-element.181.bias_ref), custom_call_target="tpu_custom_call" | custom-call | flops 134217728 | bytes 4194304 | tf_op jit(solution)/shard_map/cond/branch_0_fun/fresh_sums/pallas_call | solution.py:145
  109.6 3.6 %all-to-all-start.5 = ((bf16[16,4,32,128]{3,2,1,0:T(8,128)(2,1)}), bf16[16,4,32,128]{3,2,1,0:T(8,128)(2,1)S(1)}, u32[]{:S(2)}, u32[]{:S(2)}) async-start(bf16[16,4,32,128]{3,2,1,0:T(8,128)(2,1)} %get-tuple-element.311), calls=%async_computation.5 | async-start | bytes 1048576 | tf_op jit(solution)/shard_map/all_to_all | solution.py:367
  113.2 7.5 %collective-permute-done.19 = bf16[64,32,128]{2,1,0:T(8,128)(2,1)S(1)} collective-permute-done((bf16[64,32,128]{2,1,0:T(8,128)(2,1)S(1)}, bf16[64,32,128]{2,1,0:T(8,128)(2,1)S(1)}, u32[]{:S(2)}, u32[]{:S(2)}) %collective-permute-start.19) | collective-permute-done | bytes 524320 | tf_op jit(solution)/shard_map/ppermute | solution.py:308
  128.6 3.6 %all-to-all-start.6 = ((bf16[16,4,32,128]{3,2,1,0:T(8,128)(2,1)}), bf16[16,4,32,128]{3,2,1,0:T(8,128)(2,1)S(1)}, u32[]{:S(2)}, u32[]{:S(2)}) async-start(bf16[16,4,32,128]{3,2,1,0:T(8,128)(2,1)} %get-tuple-element.317), calls=%async_computation.6 | async-start | bytes 1048576 | tf_op jit(solution)/shard_map/all_to_all | solution.py:367
  132.2 8.2 %collective-permute-done.21 = bf16[64,32,128]{2,1,0:T(8,128)(2,1)S(1)} collective-permute-done((bf16[64,32,128]{2,1,0:T(8,128)(2,1)S(1)}, bf16[64,32,128]{2,1,0:T(8,128)(2,1)S(1)}, u32[]{:S(2)}, u32[]{:S(2)}) %collective-permute-start.21) | collective-permute-done | bytes 524320 | tf_op jit(solution)/shard_map/ppermute | solution.py:308
  147.6 3.8 %all-to-all-start.7 = ((bf16[16,4,32,128]{3,2,1,0:T(8,128)(2,1)}), bf16[16,4,32,128]{3,2,1,0:T(8,128)(2,1)S(1)}, u32[]{:S(2)}, u32[]{:S(2)}) async-start(bf16[16,4,32,128]{3,2,1,0:T(8,128)(2,1)} %get-tuple-element.323), calls=%async_computation.7 | async-start | bytes 1048576 | tf_op jit(solution)/shard_map/all_to_all | solution.py:367
  151.4 8.0 %collective-permute-done.23 = bf16[64,32,128]{2,1,0:T(8,128)(2,1)S(1)} collective-permute-done((bf16[64,32,128]{2,1,0:T(8,128)(2,1)S(1)}, bf16[64,32,128]{2,1,0:T(8,128)(2,1)S(1)}, u32[]{:S(2)}, u32[]{:S(2)}) %collective-permute-start.23) | collective-permute-done | bytes 524320 | tf_op jit(solution)/shard_map/ppermute | solution.py:308
  166.8 3.6 %all-to-all-start.8 = ((bf16[16,4,32,128]{3,2,1,0:T(8,128)(2,1)}), bf16[16,4,32,128]{3,2,1,0:T(8,128)(2,1)S(1)}, u32[]{:S(2)}, u32[]{:S(2)}) async-start(bf16[16,4,32,128]{3,2,1,0:T(8,128)(2,1)} %get-tuple-element.329), calls=%async_computation.8 | async-start | bytes 1048576 | tf_op jit(solution)/shard_map/all_to_all | solution.py:367
  170.4 8.2 %collective-permute-done.25 = bf16[64,32,128]{2,1,0:T(8,128)(2,1)S(1)} collective-permute-done((bf16[64,32,128]{2,1,0:T(8,128)(2,1)S(1)}, bf16[64,32,128]{2,1,0:T(8,128)(2,1)S(1)}, u32[]{:S(2)}, u32[]{:S(2)}) %collective-permute-start.25) | collective-permute-done | bytes 524320 | tf_op jit(solution)/shard_map/ppermute | solution.py:308
  186.5 3.6 %all-to-all-start.9 = ((bf16[16,4,32,128]{3,2,1,0:T(8,128)(2,1)}), bf16[16,4,32,128]{3,2,1,0:T(8,128)(2,1)S(1)}, u32[]{:S(2)}, u32[]{:S(2)}) async-start(bf16[16,4,32,128]{3,2,1,0:T(8,128)(2,1)} %get-tuple-element.335), calls=%async_computation.9 | async-start | bytes 1048576 | tf_op jit(solution)/shard_map/all_to_all | solution.py:367
  190.1 8.1 %collective-permute-done.27 = bf16[64,32,128]{2,1,0:T(8,128)(2,1)S(1)} collective-permute-done((bf16[64,32,128]{2,1,0:T(8,128)(2,1)S(1)}, bf16[64,32,128]{2,1,0:T(8,128)(2,1)S(1)}, u32[]{:S(2)}, u32[]{:S(2)}) %collective-permute-start.27) | collective-permute-done | bytes 524320 | tf_op jit(solution)/shard_map/ppermute | solution.py:308
  205.5 3.6 %all-to-all-start.10 = ((bf16[16,4,32,128]{3,2,1,0:T(8,128)(2,1)}), bf16[16,4,32,128]{3,2,1,0:T(8,128)(2,1)S(1)}, u32[]{:S(2)}, u32[]{:S(2)}) async-start(bf16[16,4,32,128]{3,2,1,0:T(8,128)(2,1)} %get-tuple-element.341), calls=%async_computation.10 | async-start | bytes 1048576 | tf_op jit(solution)/shard_map/all_to_all | solution.py:367
  209.1 9.5 %collective-permute-done.29 = bf16[64,32,128]{2,1,0:T(8,128)(2,1)S(1)} collective-permute-done((bf16[64,32,128]{2,1,0:T(8,128)(2,1)S(1)}, bf16[64,32,128]{2,1,0:T(8,128)(2,1)S(1)}, u32[]{:S(2)}, u32[]{:S(2)}) %collective-permute-start.29) | collective-permute-done | bytes 524320 | tf_op jit(solution)/shard_map/ppermute | solution.py:308
  (121 shorter events, 70.1 us)
Async XLA Ops:
  6.2 18.1 %all-to-all-start = ((bf16[16,4,32,128]{3,2,1,0:T(8,128)(2,1)}), bf16[16,4,32,128]{3,2,1,0:T(8,128)(2,1)S(1)}, u32[]{:S(2)}, u32[]{:S(2)}) async-start(bf16[16,4,32,128]{3,2,1,0:T(8,128)(2,1)} %get-tuple-element.282), calls=%async_computation | async-start | bytes 1048576 | tf_op jit(solution)/shard_map/all_to_all | solution.py:367
  24.4 3.5 %collective-permute-start.10 = (bf16[64,32,128]{2,1,0:T(8,128)(2,1)S(1)}, bf16[64,32,128]{2,1,0:T(8,128)(2,1)S(1)}, u32[]{:S(2)}, u32[]{:S(2)}) collective-permute-start(bf16[64,32,128]{2,1,0:T(8,128)(2,1)S(1)} %bitcast.98), channel_id=1, source_target_pairs={{0,1},{1,0},{2,3},{3,2},{4,5},{5,4},{6,7},{7,6},{8,9},{9,8},{10,11... | collective-permute-start | bytes 1572872 | tf_op jit(solution)/shard_map/ppermute | solution.py:308
  26.5 14.8 %collective-permute-start.11 = (bf16[64,32,128]{2,1,0:T(8,128)(2,1)S(1)}, bf16[64,32,128]{2,1,0:T(8,128)(2,1)S(1)}, u32[]{:S(2)}, u32[]{:S(2)}) collective-permute-start(bf16[64,32,128]{2,1,0:T(8,128)(2,1)S(1)} %bitcast.99), channel_id=1, source_target_pairs={{0,32},{1,33},{2,34},{3,35},{4,36},{5,37},{6,38},{7,39},{8,40},{9,... | collective-permute-start | bytes 1572872 | tf_op jit(solution)/shard_map/ppermute | solution.py:308
  30.7 15.0 %all-to-all-start.1 = ((bf16[16,4,32,128]{3,2,1,0:T(8,128)(2,1)}), bf16[16,4,32,128]{3,2,1,0:T(8,128)(2,1)S(1)}, u32[]{:S(2)}, u32[]{:S(2)}) async-start(bf16[16,4,32,128]{3,2,1,0:T(8,128)(2,1)} %get-tuple-element.287), calls=%async_computation.1 | async-start | bytes 1048576 | tf_op jit(solution)/shard_map/all_to_all | solution.py:367
  45.7 2.6 %collective-permute-start.12 = (bf16[64,32,128]{2,1,0:T(8,128)(2,1)S(1)}, bf16[64,32,128]{2,1,0:T(8,128)(2,1)S(1)}, u32[]{:S(2)}, u32[]{:S(2)}) collective-permute-start(bf16[64,32,128]{2,1,0:T(8,128)(2,1)S(1)} %bitcast.82), channel_id=1, source_target_pairs={{0,1},{1,0},{2,3},{3,2},{4,5},{5,4},{6,7},{7,6},{8,9},{9,8},{10,11... | collective-permute-start | bytes 1572872 | tf_op jit(solution)/shard_map/ppermute | solution.py:308
  46.8 14.8 %collective-permute-start.13 = (bf16[64,32,128]{2,1,0:T(8,128)(2,1)S(1)}, bf16[64,32,128]{2,1,0:T(8,128)(2,1)S(1)}, u32[]{:S(2)}, u32[]{:S(2)}) collective-permute-start(bf16[64,32,128]{2,1,0:T(8,128)(2,1)S(1)} %bitcast.83), channel_id=1, source_target_pairs={{0,32},{1,33},{2,34},{3,35},{4,36},{5,37},{6,38},{7,39},{8,40},{9,... | collective-permute-start | bytes 1572872 | tf_op jit(solution)/shard_map/ppermute | solution.py:308
  50.4 15.1 %all-to-all-start.2 = ((bf16[16,4,32,128]{3,2,1,0:T(8,128)(2,1)}), bf16[16,4,32,128]{3,2,1,0:T(8,128)(2,1)S(1)}, u32[]{:S(2)}, u32[]{:S(2)}) async-start(bf16[16,4,32,128]{3,2,1,0:T(8,128)(2,1)} %get-tuple-element.293), calls=%async_computation.2 | async-start | bytes 1048576 | tf_op jit(solution)/shard_map/all_to_all | solution.py:367
  65.5 2.5 %collective-permute-start.14 = (bf16[64,32,128]{2,1,0:T(8,128)(2,1)S(1)}, bf16[64,32,128]{2,1,0:T(8,128)(2,1)S(1)}, u32[]{:S(2)}, u32[]{:S(2)}) collective-permute-start(bf16[64,32,128]{2,1,0:T(8,128)(2,1)S(1)} %bitcast.90), channel_id=1, source_target_pairs={{0,1},{1,0},{2,3},{3,2},{4,5},{5,4},{6,7},{7,6},{8,9},{9,8},{10,11... | collective-permute-start | bytes 1572872 | tf_op jit(solution)/shard_map/ppermute | solution.py:308
  66.5 14.8 %collective-permute-start.15 = (bf16[64,32,128]{2,1,0:T(8,128)(2,1)S(1)}, bf16[64,32,128]{2,1,0:T(8,128)(2,1)S(1)}, u32[]{:S(2)}, u32[]{:S(2)}) collective-permute-start(bf16[64,32,128]{2,1,0:T(8,128)(2,1)S(1)} %bitcast.91), channel_id=1, source_target_pairs={{0,32},{1,33},{2,34},{3,35},{4,36},{5,37},{6,38},{7,39},{8,40},{9,... | collective-permute-start | bytes 1572872 | tf_op jit(solution)/shard_map/ppermute | solution.py:308
  70.1 15.3 %all-to-all-start.3 = ((bf16[16,4,32,128]{3,2,1,0:T(8,128)(2,1)}), bf16[16,4,32,128]{3,2,1,0:T(8,128)(2,1)S(1)}, u32[]{:S(2)}, u32[]{:S(2)}) async-start(bf16[16,4,32,128]{3,2,1,0:T(8,128)(2,1)} %get-tuple-element.299), calls=%async_computation.3 | async-start | bytes 1048576 | tf_op jit(solution)/shard_map/all_to_all | solution.py:367
  85.4 2.4 %collective-permute-start.16 = (bf16[64,32,128]{2,1,0:T(8,128)(2,1)S(1)}, bf16[64,32,128]{2,1,0:T(8,128)(2,1)S(1)}, u32[]{:S(2)}, u32[]{:S(2)}) collective-permute-start(bf16[64,32,128]{2,1,0:T(8,128)(2,1)S(1)} %bitcast.94), channel_id=1, source_target_pairs={{0,1},{1,0},{2,3},{3,2},{4,5},{5,4},{6,7},{7,6},{8,9},{9,8},{10,11... | collective-permute-start | bytes 1572872 | tf_op jit(solution)/shard_map/ppermute | solution.py:308
  86.3 14.7 %collective-permute-start.17 = (bf16[64,32,128]{2,1,0:T(8,128)(2,1)S(1)}, bf16[64,32,128]{2,1,0:T(8,128)(2,1)S(1)}, u32[]{:S(2)}, u32[]{:S(2)}) collective-permute-start(bf16[64,32,128]{2,1,0:T(8,128)(2,1)S(1)} %bitcast.95), channel_id=1, source_target_pairs={{0,32},{1,33},{2,34},{3,35},{4,36},{5,37},{6,38},{7,39},{8,40},{9,... | collective-permute-start | bytes 1572872 | tf_op jit(solution)/shard_map/ppermute | solution.py:308
  89.9 15.0 %all-to-all-start.4 = ((bf16[16,4,32,128]{3,2,1,0:T(8,128)(2,1)}), bf16[16,4,32,128]{3,2,1,0:T(8,128)(2,1)S(1)}, u32[]{:S(2)}, u32[]{:S(2)}) async-start(bf16[16,4,32,128]{3,2,1,0:T(8,128)(2,1)} %get-tuple-element.305), calls=%async_computation.4 | async-start | bytes 1048576 | tf_op jit(solution)/shard_map/all_to_all | solution.py:367
  104.9 2.5 %collective-permute-start.18 = (bf16[64,32,128]{2,1,0:T(8,128)(2,1)S(1)}, bf16[64,32,128]{2,1,0:T(8,128)(2,1)S(1)}, u32[]{:S(2)}, u32[]{:S(2)}) collective-permute-start(bf16[64,32,128]{2,1,0:T(8,128)(2,1)S(1)} %bitcast.86), channel_id=1, source_target_pairs={{0,1},{1,0},{2,3},{3,2},{4,5},{5,4},{6,7},{7,6},{8,9},{9,8},{10,11... | collective-permute-start | bytes 1572872 | tf_op jit(solution)/shard_map/ppermute | solution.py:308
  105.9 14.7 %collective-permute-start.19 = (bf16[64,32,128]{2,1,0:T(8,128)(2,1)S(1)}, bf16[64,32,128]{2,1,0:T(8,128)(2,1)S(1)}, u32[]{:S(2)}, u32[]{:S(2)}) collective-permute-start(bf16[64,32,128]{2,1,0:T(8,128)(2,1)S(1)} %bitcast.87), channel_id=1, source_target_pairs={{0,32},{1,33},{2,34},{3,35},{4,36},{5,37},{6,38},{7,39},{8,40},{9,... | collective-permute-start | bytes 1572872 | tf_op jit(solution)/shard_map/ppermute | solution.py:308
  109.6 14.3 %all-to-all-start.5 = ((bf16[16,4,32,128]{3,2,1,0:T(8,128)(2,1)}), bf16[16,4,32,128]{3,2,1,0:T(8,128)(2,1)S(1)}, u32[]{:S(2)}, u32[]{:S(2)}) async-start(bf16[16,4,32,128]{3,2,1,0:T(8,128)(2,1)} %get-tuple-element.311), calls=%async_computation.5 | async-start | bytes 1048576 | tf_op jit(solution)/shard_map/all_to_all | solution.py:367
  123.9 3.3 %collective-permute-start.20 = (bf16[64,32,128]{2,1,0:T(8,128)(2,1)S(1)}, bf16[64,32,128]{2,1,0:T(8,128)(2,1)S(1)}, u32[]{:S(2)}, u32[]{:S(2)}) collective-permute-start(bf16[64,32,128]{2,1,0:T(8,128)(2,1)S(1)} %bitcast.70), channel_id=1, source_target_pairs={{0,1},{1,0},{2,3},{3,2},{4,5},{5,4},{6,7},{7,6},{8,9},{9,8},{10,11... | collective-permute-start | bytes 1572872 | tf_op jit(solution)/shard_map/ppermute | solution.py:308
  125.6 14.8 %collective-permute-start.21 = (bf16[64,32,128]{2,1,0:T(8,128)(2,1)S(1)}, bf16[64,32,128]{2,1,0:T(8,128)(2,1)S(1)}, u32[]{:S(2)}, u32[]{:S(2)}) collective-permute-start(bf16[64,32,128]{2,1,0:T(8,128)(2,1)S(1)} %bitcast.71), channel_id=1, source_target_pairs={{0,32},{1,33},{2,34},{3,35},{4,36},{5,37},{6,38},{7,39},{8,40},{9,... | collective-permute-start | bytes 1572872 | tf_op jit(solution)/shard_map/ppermute | solution.py:308
  128.6 14.3 %all-to-all-start.6 = ((bf16[16,4,32,128]{3,2,1,0:T(8,128)(2,1)}), bf16[16,4,32,128]{3,2,1,0:T(8,128)(2,1)S(1)}, u32[]{:S(2)}, u32[]{:S(2)}) async-start(bf16[16,4,32,128]{3,2,1,0:T(8,128)(2,1)} %get-tuple-element.317), calls=%async_computation.6 | async-start | bytes 1048576 | tf_op jit(solution)/shard_map/all_to_all | solution.py:367
  142.9 3.3 %collective-permute-start.22 = (bf16[64,32,128]{2,1,0:T(8,128)(2,1)S(1)}, bf16[64,32,128]{2,1,0:T(8,128)(2,1)S(1)}, u32[]{:S(2)}, u32[]{:S(2)}) collective-permute-start(bf16[64,32,128]{2,1,0:T(8,128)(2,1)S(1)} %bitcast.74), channel_id=1, source_target_pairs={{0,1},{1,0},{2,3},{3,2},{4,5},{5,4},{6,7},{7,6},{8,9},{9,8},{10,11... | collective-permute-start | bytes 1572872 | tf_op jit(solution)/shard_map/ppermute | solution.py:308
  144.6 14.8 %collective-permute-start.23 = (bf16[64,32,128]{2,1,0:T(8,128)(2,1)S(1)}, bf16[64,32,128]{2,1,0:T(8,128)(2,1)S(1)}, u32[]{:S(2)}, u32[]{:S(2)}) collective-permute-start(bf16[64,32,128]{2,1,0:T(8,128)(2,1)S(1)} %bitcast.75), channel_id=1, source_target_pairs={{0,32},{1,33},{2,34},{3,35},{4,36},{5,37},{6,38},{7,39},{8,40},{9,... | collective-permute-start | bytes 1572872 | tf_op jit(solution)/shard_map/ppermute | solution.py:308
  147.6 14.5 %all-to-all-start.7 = ((bf16[16,4,32,128]{3,2,1,0:T(8,128)(2,1)}), bf16[16,4,32,128]{3,2,1,0:T(8,128)(2,1)S(1)}, u32[]{:S(2)}, u32[]{:S(2)}) async-start(bf16[16,4,32,128]{3,2,1,0:T(8,128)(2,1)} %get-tuple-element.323), calls=%async_computation.7 | async-start | bytes 1048576 | tf_op jit(solution)/shard_map/all_to_all | solution.py:367
  162.1 3.3 %collective-permute-start.24 = (bf16[64,32,128]{2,1,0:T(8,128)(2,1)S(1)}, bf16[64,32,128]{2,1,0:T(8,128)(2,1)S(1)}, u32[]{:S(2)}, u32[]{:S(2)}) collective-permute-start(bf16[64,32,128]{2,1,0:T(8,128)(2,1)S(1)} %bitcast.78), channel_id=1, source_target_pairs={{0,1},{1,0},{2,3},{3,2},{4,5},{5,4},{6,7},{7,6},{8,9},{9,8},{10,11... | collective-permute-start | bytes 1572872 | tf_op jit(solution)/shard_map/ppermute | solution.py:308
  163.9 14.8 %collective-permute-start.25 = (bf16[64,32,128]{2,1,0:T(8,128)(2,1)S(1)}, bf16[64,32,128]{2,1,0:T(8,128)(2,1)S(1)}, u32[]{:S(2)}, u32[]{:S(2)}) collective-permute-start(bf16[64,32,128]{2,1,0:T(8,128)(2,1)S(1)} %bitcast.79), channel_id=1, source_target_pairs={{0,32},{1,33},{2,34},{3,35},{4,36},{5,37},{6,38},{7,39},{8,40},{9,... | collective-permute-start | bytes 1572872 | tf_op jit(solution)/shard_map/ppermute | solution.py:308
  166.8 14.3 %all-to-all-start.8 = ((bf16[16,4,32,128]{3,2,1,0:T(8,128)(2,1)}), bf16[16,4,32,128]{3,2,1,0:T(8,128)(2,1)S(1)}, u32[]{:S(2)}, u32[]{:S(2)}) async-start(bf16[16,4,32,128]{3,2,1,0:T(8,128)(2,1)} %get-tuple-element.329), calls=%async_computation.8 | async-start | bytes 1048576 | tf_op jit(solution)/shard_map/all_to_all | solution.py:367
  181.1 3.3 %collective-permute-start.26 = (bf16[64,32,128]{2,1,0:T(8,128)(2,1)S(1)}, bf16[64,32,128]{2,1,0:T(8,128)(2,1)S(1)}, u32[]{:S(2)}, u32[]{:S(2)}) collective-permute-start(bf16[64,32,128]{2,1,0:T(8,128)(2,1)S(1)} %bitcast.63), channel_id=1, source_target_pairs={{0,1},{1,0},{2,3},{3,2},{4,5},{5,4},{6,7},{7,6},{8,9},{9,8},{10,11... | collective-permute-start | bytes 1572872 | tf_op jit(solution)/shard_map/ppermute | solution.py:308
  182.9 15.4 %collective-permute-start.27 = (bf16[64,32,128]{2,1,0:T(8,128)(2,1)S(1)}, bf16[64,32,128]{2,1,0:T(8,128)(2,1)S(1)}, u32[]{:S(2)}, u32[]{:S(2)}) collective-permute-start(bf16[64,32,128]{2,1,0:T(8,128)(2,1)S(1)} %bitcast.64), channel_id=1, source_target_pairs={{0,32},{1,33},{2,34},{3,35},{4,36},{5,37},{6,38},{7,39},{8,40},{9,... | collective-permute-start | bytes 1572872 | tf_op jit(solution)/shard_map/ppermute | solution.py:308
  186.5 15.0 %all-to-all-start.9 = ((bf16[16,4,32,128]{3,2,1,0:T(8,128)(2,1)}), bf16[16,4,32,128]{3,2,1,0:T(8,128)(2,1)S(1)}, u32[]{:S(2)}, u32[]{:S(2)}) async-start(bf16[16,4,32,128]{3,2,1,0:T(8,128)(2,1)} %get-tuple-element.335), calls=%async_computation.9 | async-start | bytes 1048576 | tf_op jit(solution)/shard_map/all_to_all | solution.py:367
  201.5 2.6 %collective-permute-start.28 = (bf16[64,32,128]{2,1,0:T(8,128)(2,1)S(1)}, bf16[64,32,128]{2,1,0:T(8,128)(2,1)S(1)}, u32[]{:S(2)}, u32[]{:S(2)}) collective-permute-start(bf16[64,32,128]{2,1,0:T(8,128)(2,1)S(1)} %bitcast.59), channel_id=1, source_target_pairs={{0,1},{1,0},{2,3},{3,2},{4,5},{5,4},{6,7},{7,6},{8,9},{9,8},{10,11... | collective-permute-start | bytes 1572872 | tf_op jit(solution)/shard_map/ppermute | solution.py:308
  202.5 16.0 %collective-permute-start.29 = (bf16[64,32,128]{2,1,0:T(8,128)(2,1)S(1)}, bf16[64,32,128]{2,1,0:T(8,128)(2,1)S(1)}, u32[]{:S(2)}, u32[]{:S(2)}) collective-permute-start(bf16[64,32,128]{2,1,0:T(8,128)(2,1)S(1)} %bitcast.60), channel_id=1, source_target_pairs={{0,32},{1,33},{2,34},{3,35},{4,36},{5,37},{6,38},{7,39},{8,40},{9,... | collective-permute-start | bytes 1572872 | tf_op jit(solution)/shard_map/ppermute | solution.py:308
  205.5 14.3 %all-to-all-start.10 = ((bf16[16,4,32,128]{3,2,1,0:T(8,128)(2,1)}), bf16[16,4,32,128]{3,2,1,0:T(8,128)(2,1)S(1)}, u32[]{:S(2)}, u32[]{:S(2)}) async-start(bf16[16,4,32,128]{3,2,1,0:T(8,128)(2,1)} %get-tuple-element.341), calls=%async_computation.10 | async-start | bytes 1048576 | tf_op jit(solution)/shard_map/all_to_all | solution.py:367
  219.8 3.3 %collective-permute-start.30 = (bf16[64,32,128]{2,1,0:T(8,128)(2,1)S(1)}, bf16[64,32,128]{2,1,0:T(8,128)(2,1)S(1)}, u32[]{:S(2)}, u32[]{:S(2)}) collective-permute-start(bf16[64,32,128]{2,1,0:T(8,128)(2,1)S(1)} %bitcast.67), channel_id=1, source_target_pairs={{0,1},{1,0},{2,3},{3,2},{4,5},{5,4},{6,7},{7,6},{8,9},{9,8},{10,11... | collective-permute-start | bytes 1572872 | tf_op jit(solution)/shard_map/ppermute | solution.py:308
  (14 other events, 56.0 us)

commit v6 on v5

--- a/solution.py
+++ b/solution.py
@@ -241,8 +241,9 @@
     )(layer, index, unmoved(inputs), unmoved(w), unmoved(bias))
 
 
-def state_kernel(tick, step_count, layer_ref, index_ref, mine_ref, other_ref, w_ref, partial_ref, cell_ref, token_ref, cell_out, rows_out, send_out, spread_ref, sent):
-    step = tick - LAG * layer_ref[0]
+def state_kernel(tick, step_count, index_ref, mine_ref, other_ref, w_ref, partial_ref, cell_ref, token_ref, cell_out, rows_out, send_out, spread_ref, sent):
+    total = 2 * mine_ref.shape[0]
+    step = tick - LAG * (index_ref[0] // total)
     active = (step >= 0) & (step < step_count)
     per_device, _, edge = cell_ref.shape
     last = len(cell_out.shape) == 2
@@ -255,7 +256,8 @@
 
     @pl.when(active)
     def _():
-        pick = from_halves(mine_ref, other_ref)
+        block = from_halves(mine_ref, other_ref)
+        pick = lambda i: block(i & (total - 1))
         sender = Sender(send_out, spread_ref, sent)
         for j in range(per_device):
             sums = [partial_ref[4 * j + g] + row_sums(pick, index_ref, w_ref, 4 * j + g) for g in range(4)]
@@ -277,20 +279,20 @@
         idle.finish()
 
 
-def state_step(tick, layer, index, state, w, partial, cell, step_count, peers, token, last):
+def state_step(tick, index, state, w, partial, cell, step_count, peers, token, last):
     outs = state_out(cell.shape, peers)
     if last:
         outs = (jax.ShapeDtypeStruct(outs[1].shape, F32), *outs[1:])
     return pl.pallas_call(
         functools.partial(state_kernel, tick, step_count),
         out_shape=outs,
-        in_specs=[smem(), smem()] + [vmem()] * 6,
+        in_specs=[smem()] + [vmem()] * 6,
         out_specs=(vmem(), vmem(), hbm()),
         scratch_shapes=send_scratch(cell.shape, peers),
         compiler_params=pltpu.CompilerParams(vmem_limit_bytes=8 * MIB),
         cost_estimate=pl.CostEstimate(flops=2 * w.size * 32, bytes_accessed=w.size, transcendentals=0),
         name="state_step",
-    )(layer, index, *[held(part) for part in state], held(w), partial, cell, token)
+    )(index, *[held(part) for part in state], held(w), partial, cell, token)
 
 
 def exchange(x, target):
@@ -350,7 +352,7 @@
 
     in_flat = in_cols.reshape(-1)
     in_index = jnp.where(layer == 0, in_flat, place(in_flat))
-    rec_index = place(rec_cols.reshape(-1))
+    rec_index = place(rec_cols.reshape(-1)) + total * layer.astype(jnp.int32)
     offsets = bias[0].reshape(gates, per_device, edge).transpose(1, 0, 2).reshape(rows, 1, edge)
     layer_ref = layer.astype(jnp.int32).reshape(1)
     w_in = in_blocks.reshape(rows, kept, edge, edge)
@@ -379,7 +381,7 @@
         token = mark(mine, 1024 * w_rec.size)
         last = tick == tick_count - 1
         cell, out_rows, send = state_step(
-            tick, layer_ref, rec_index, state, w_rec, partial, cell, step_count, chips, token, last
+            tick, rec_index, state, w_rec, partial, cell, step_count, chips, token, last
         )
         outputs.append(out_rows)
     sequence = lax.dynamic_slice_in_dim(jnp.stack(outputs), LAG * layer, step_count, 0)

time: 228 us -> 228 us (level)
  no operation moved by 1% of the time
where the time goes in v6:
time: 228 us; the launch traced here: 225 us
  waiting for transfers between devices  117 us (51%)
  starting transfers between devices  59.9 us (26%)
  Pallas kernels  43.9 us (19%)
  local copies, waits for them, and re-layouts  3.18 us (1%)
    ppermute x21, waiting for transfers between devices, exchange(): return lax.ppermute(x, ('pipe',) + WIDTH, route)  94.7 us
    all_to_all x11, starting transfers between devices, body(): mine = lax.all_to_all(send, ('y', 'x'), 0, 0).reshape(half, row_count, edge)  43.4 us
    all_to_all x11, waiting for transfers between devices, body(): mine = lax.all_to_all(send, ('y', 'x'), 0, 0).reshape(half, row_count, edge)  22 us
    pallas_call x5, Pallas kernels, fresh_sums(): pl.pallas_call(functools.partial(fresh_kernel, tick), out_shape=pltpu.VME...  19.8 us
    pallas_call x11, Pallas kernels, state_step(): pl.pallas_call(functools.partial(state_kernel, tick, step_count), out_sha...  19.2 us
    ppermute x21, starting transfers between devices, exchange(): return lax.ppermute(x, ('pipe',) + WIDTH, route)  16.4 us
    pallas_call x1, Pallas kernels, first_step(): pl.pallas_call(first_kernel, out_shape=state_out((per_device, row_count,...  4.84 us
  transfers between devices with their start and end apart: 32, of which 29 were waited for; matrix products, arithmetic and copies ran while one was open for 0% of the time, Pallas kernels for 17%

profile of v6, /device:TPU:1, one launch (start us, length us, event | category | flops | bytes accessed | tf_op | source)
XLA Modules:
  0.0 225.2 jit_solution(16948350038294779276)
XLA Ops:
  1.4 4.8 %first_step.1 = (f32[4,32,128]{2,1,0:T(8,128)S(1)}, bf16[32,512]{1,0:T(8,128)(2,1)S(1)}, bf16[16,4,32,128]{3,2,1,0:T(8,128)(2,1)}) custom-call(s32[1]{0:T(128)} %bitcast.layer_ref, s32[4,4,8]{2,1,0:T(4,128)S(1)} %bitcast.118, bf16[6,32,16384]{2,1,0:T(8,128)(2,1)} %inputs_ref.3, bf16[16,8,128,128]{3,2,1,0:T(8,128)(2,1)} %bitcast.119, f32[4,512]{1,0:T(4,128)} %bitcast.102), custom_call_target="tpu_custom_call" | custom-call | tf_op jit(solution)/shard_map/first_step/pallas_call | solution.py:233
  6.2 7.6 %all-to-all-start = ((bf16[16,4,32,128]{3,2,1,0:T(8,128)(2,1)}), bf16[16,4,32,128]{3,2,1,0:T(8,128)(2,1)S(1)}, u32[]{:S(2)}, u32[]{:S(2)}) async-start(bf16[16,4,32,128]{3,2,1,0:T(8,128)(2,1)} %get-tuple-element.282), calls=%async_computation | async-start | bytes 1048576 | tf_op jit(solution)/shard_map/all_to_all | solution.py:369
  14.0 3.9 %fresh_sums.9.partial_ref = f32[16,32,128]{2,1,0:T(8,128)S(1)} custom-call(s32[1]{0:T(128)} %bitcast.layer_ref, s32[128]{0:T(128)S(1)} %broadcast_select_fusion.index_ref, bf16[6,32,16384]{2,1,0:T(8,128)(2,1)} %inputs_ref.3, bf16[16,8,128,128]{3,2,1,0:T(8,128)(2,1)} %bitcast.120, f32[16,1,128]{2,1,0:T(1,128)S(1)} %bitcast.103), custom_call_target="tpu_custom_call" | custom-call | flops 134217728 | bytes 4194304 | tf_op jit(solution)/shard_map/fresh_sums/pallas_call | solution.py:145
  17.9 6.4 %all-to-all-done = bf16[16,4,32,128]{3,2,1,0:T(8,128)(2,1)S(1)} async-done(((bf16[16,4,32,128]{3,2,1,0:T(8,128)(2,1)}), bf16[16,4,32,128]{3,2,1,0:T(8,128)(2,1)S(1)}, u32[]{:S(2)}, u32[]{:S(2)}) %all-to-all-start) | async-done | bytes 524320 | tf_op jit(solution)/shard_map/all_to_all | solution.py:369
  30.7 3.6 %all-to-all-start.1 = ((bf16[16,4,32,128]{3,2,1,0:T(8,128)(2,1)}), bf16[16,4,32,128]{3,2,1,0:T(8,128)(2,1)S(1)}, u32[]{:S(2)}, u32[]{:S(2)}) async-start(bf16[16,4,32,128]{3,2,1,0:T(8,128)(2,1)} %get-tuple-element.287), calls=%async_computation.1 | async-start | bytes 1048576 | tf_op jit(solution)/shard_map/all_to_all | solution.py:369
  34.3 7.0 %collective-permute-done.11 = bf16[64,32,128]{2,1,0:T(8,128)(2,1)S(1)} collective-permute-done((bf16[64,32,128]{2,1,0:T(8,128)(2,1)S(1)}, bf16[64,32,128]{2,1,0:T(8,128)(2,1)S(1)}, u32[]{:S(2)}, u32[]{:S(2)}) %collective-permute-start.11) | collective-permute-done | bytes 524320 | tf_op jit(solution)/shard_map/ppermute | solution.py:310
  41.3 4.0 %conditional.10 = (f32[16,32,128]{2,1,0:T(8,128)S(1)}) conditional(s32[]{:T(128)} %convert_element_type.30, (s32[1]{0:T(128)}, s32[128]{0:T(128)S(1)}, bf16[6,32,16384]{2,1,0:T(8,128)(2,1)}, bf16[16,8,128,128]{3,2,1,0:T(8,128)(2,1)}, f32[16,1,128]{2,1,0:T(1,128)S(1)}) %tuple.145, (bf16[64,32,128]{2,1,0:T(8,128)(2,1)S(1)}, ...), branch_computations={%region_0.1_spmd, %region_1.2_spmd} | conditional | flops 134217728 | bytes 8388656 | solution.py:375
  41.3 4.0 %fresh_sums.5 = f32[16,32,128]{2,1,0:T(8,128)S(1)} custom-call(s32[1]{0:T(128)} %get-tuple-element.139.layer_ref, s32[128]{0:T(128)S(1)} %get-tuple-element.140.index_ref, bf16[6,32,16384]{2,1,0:T(8,128)(2,1)} %get-tuple-element.141.inputs_ref, bf16[16,8,128,128]{3,2,1,0:T(8,128)(2,1)} %get-tuple-element.142.w_hbm, f32[16,1,128]{2,1,0:T(1,128)S(1)} %get-tuple-element.148.bias_ref), custom_call_target="tpu_custom_call" | custom-call | flops 134217728 | bytes 4194304 | tf_op jit(solution)/shard_map/cond/branch_0_fun/fresh_sums/pallas_call | solution.py:145
  50.5 3.6 %all-to-all-start.2 = ((bf16[16,4,32,128]{3,2,1,0:T(8,128)(2,1)}), bf16[16,4,32,128]{3,2,1,0:T(8,128)(2,1)S(1)}, u32[]{:S(2)}, u32[]{:S(2)}) async-start(bf16[16,4,32,128]{3,2,1,0:T(8,128)(2,1)} %get-tuple-element.293), calls=%async_computation.2 | async-start | bytes 1048576 | tf_op jit(solution)/shard_map/all_to_all | solution.py:369
  54.1 7.5 %collective-permute-done.13 = bf16[64,32,128]{2,1,0:T(8,128)(2,1)S(1)} collective-permute-done((bf16[64,32,128]{2,1,0:T(8,128)(2,1)S(1)}, bf16[64,32,128]{2,1,0:T(8,128)(2,1)S(1)}, u32[]{:S(2)}, u32[]{:S(2)}) %collective-permute-start.13) | collective-permute-done | bytes 524320 | tf_op jit(solution)/shard_map/ppermute | solution.py:310
  61.5 4.0 %conditional.11 = (f32[16,32,128]{2,1,0:T(8,128)S(1)}) conditional(s32[]{:T(128)} %convert_element_type.31, (s32[1]{0:T(128)}, s32[128]{0:T(128)S(1)}, bf16[6,32,16384]{2,1,0:T(8,128)(2,1)}, bf16[16,8,128,128]{3,2,1,0:T(8,128)(2,1)}, f32[16,1,128]{2,1,0:T(1,128)S(1)}) %tuple.147, (bf16[64,32,128]{2,1,0:T(8,128)(2,1)S(1)}, ...), branch_computations={%region_2.3_spmd, %region_3.4_spmd} | conditional | flops 134217728 | bytes 8388656 | solution.py:375
  61.5 3.9 %fresh_sums.6 = f32[16,32,128]{2,1,0:T(8,128)S(1)} custom-call(s32[1]{0:T(128)} %get-tuple-element.154.layer_ref, s32[128]{0:T(128)S(1)} %get-tuple-element.160.index_ref, bf16[6,32,16384]{2,1,0:T(8,128)(2,1)} %get-tuple-element.161.inputs_ref, bf16[16,8,128,128]{3,2,1,0:T(8,128)(2,1)} %get-tuple-element.162.w_hbm, f32[16,1,128]{2,1,0:T(1,128)S(1)} %get-tuple-element.163.bias_ref), custom_call_target="tpu_custom_call" | custom-call | flops 134217728 | bytes 4194304 | tf_op jit(solution)/shard_map/cond/branch_0_fun/fresh_sums/pallas_call | solution.py:145
  70.2 3.6 %all-to-all-start.3 = ((bf16[16,4,32,128]{3,2,1,0:T(8,128)(2,1)}), bf16[16,4,32,128]{3,2,1,0:T(8,128)(2,1)S(1)}, u32[]{:S(2)}, u32[]{:S(2)}) async-start(bf16[16,4,32,128]{3,2,1,0:T(8,128)(2,1)} %get-tuple-element.299), calls=%async_computation.3 | async-start | bytes 1048576 | tf_op jit(solution)/shard_map/all_to_all | solution.py:369
  73.8 7.5 %collective-permute-done.15 = bf16[64,32,128]{2,1,0:T(8,128)(2,1)S(1)} collective-permute-done((bf16[64,32,128]{2,1,0:T(8,128)(2,1)S(1)}, bf16[64,32,128]{2,1,0:T(8,128)(2,1)S(1)}, u32[]{:S(2)}, u32[]{:S(2)}) %collective-permute-start.15) | collective-permute-done | bytes 524320 | tf_op jit(solution)/shard_map/ppermute | solution.py:310
  81.3 4.1 %conditional.12 = (f32[16,32,128]{2,1,0:T(8,128)S(1)}) conditional(s32[]{:T(128)} %convert_element_type.32, (s32[1]{0:T(128)}, s32[128]{0:T(128)S(1)}, bf16[6,32,16384]{2,1,0:T(8,128)(2,1)}, bf16[16,8,128,128]{3,2,1,0:T(8,128)(2,1)}, f32[16,1,128]{2,1,0:T(1,128)S(1)}) %tuple.149, (bf16[64,32,128]{2,1,0:T(8,128)(2,1)S(1)}, ...), branch_computations={%region_4.5_spmd, %region_5.6_spmd} | conditional | flops 134217728 | bytes 8388656 | solution.py:375
  81.3 3.9 %fresh_sums.7 = f32[16,32,128]{2,1,0:T(8,128)S(1)} custom-call(s32[1]{0:T(128)} %get-tuple-element.168.layer_ref, s32[128]{0:T(128)S(1)} %get-tuple-element.169.index_ref, bf16[6,32,16384]{2,1,0:T(8,128)(2,1)} %get-tuple-element.170.inputs_ref, bf16[16,8,128,128]{3,2,1,0:T(8,128)(2,1)} %get-tuple-element.171.w_hbm, f32[16,1,128]{2,1,0:T(1,128)S(1)} %get-tuple-element.172.bias_ref), custom_call_target="tpu_custom_call" | custom-call | flops 134217728 | bytes 4194304 | tf_op jit(solution)/shard_map/cond/branch_0_fun/fresh_sums/pallas_call | solution.py:145
  90.0 3.6 %all-to-all-start.4 = ((bf16[16,4,32,128]{3,2,1,0:T(8,128)(2,1)}), bf16[16,4,32,128]{3,2,1,0:T(8,128)(2,1)S(1)}, u32[]{:S(2)}, u32[]{:S(2)}) async-start(bf16[16,4,32,128]{3,2,1,0:T(8,128)(2,1)} %get-tuple-element.305), calls=%async_computation.4 | async-start | bytes 1048576 | tf_op jit(solution)/shard_map/all_to_all | solution.py:369
  93.6 7.4 %collective-permute-done.17 = bf16[64,32,128]{2,1,0:T(8,128)(2,1)S(1)} collective-permute-done((bf16[64,32,128]{2,1,0:T(8,128)(2,1)S(1)}, bf16[64,32,128]{2,1,0:T(8,128)(2,1)S(1)}, u32[]{:S(2)}, u32[]{:S(2)}) %collective-permute-start.17) | collective-permute-done | bytes 524320 | tf_op jit(solution)/shard_map/ppermute | solution.py:310
  101.0 4.0 %conditional.13 = (f32[16,32,128]{2,1,0:T(8,128)S(1)}) conditional(s32[]{:T(128)} %convert_element_type.33, (s32[1]{0:T(128)}, s32[128]{0:T(128)S(1)}, bf16[6,32,16384]{2,1,0:T(8,128)(2,1)}, bf16[16,8,128,128]{3,2,1,0:T(8,128)(2,1)}, f32[16,1,128]{2,1,0:T(1,128)S(1)}) %tuple.151, (bf16[64,32,128]{2,1,0:T(8,128)(2,1)S(1)}, ...), branch_computations={%region_6.7_spmd, %region_7.8_spmd} | conditional | flops 134217728 | bytes 8388656 | solution.py:375
  101.0 3.9 %fresh_sums.8 = f32[16,32,128]{2,1,0:T(8,128)S(1)} custom-call(s32[1]{0:T(128)} %get-tuple-element.177.layer_ref, s32[128]{0:T(128)S(1)} %get-tuple-element.178.index_ref, bf16[6,32,16384]{2,1,0:T(8,128)(2,1)} %get-tuple-element.179.inputs_ref, bf16[16,8,128,128]{3,2,1,0:T(8,128)(2,1)} %get-tuple-element.180.w_hbm, f32[16,1,128]{2,1,0:T(1,128)S(1)} %get-tuple-element.181.bias_ref), custom_call_target="tpu_custom_call" | custom-call | flops 134217728 | bytes 4194304 | tf_op jit(solution)/shard_map/cond/branch_0_fun/fresh_sums/pallas_call | solution.py:145
  109.7 3.6 %all-to-all-start.5 = ((bf16[16,4,32,128]{3,2,1,0:T(8,128)(2,1)}), bf16[16,4,32,128]{3,2,1,0:T(8,128)(2,1)S(1)}, u32[]{:S(2)}, u32[]{:S(2)}) async-start(bf16[16,4,32,128]{3,2,1,0:T(8,128)(2,1)} %get-tuple-element.311), calls=%async_computation.5 | async-start | bytes 1048576 | tf_op jit(solution)/shard_map/all_to_all | solution.py:369
  113.3 7.5 %collective-permute-done.19 = bf16[64,32,128]{2,1,0:T(8,128)(2,1)S(1)} collective-permute-done((bf16[64,32,128]{2,1,0:T(8,128)(2,1)S(1)}, bf16[64,32,128]{2,1,0:T(8,128)(2,1)S(1)}, u32[]{:S(2)}, u32[]{:S(2)}) %collective-permute-start.19) | collective-permute-done | bytes 524320 | tf_op jit(solution)/shard_map/ppermute | solution.py:310
  128.7 3.6 %all-to-all-start.6 = ((bf16[16,4,32,128]{3,2,1,0:T(8,128)(2,1)}), bf16[16,4,32,128]{3,2,1,0:T(8,128)(2,1)S(1)}, u32[]{:S(2)}, u32[]{:S(2)}) async-start(bf16[16,4,32,128]{3,2,1,0:T(8,128)(2,1)} %get-tuple-element.317), calls=%async_computation.6 | async-start | bytes 1048576 | tf_op jit(solution)/shard_map/all_to_all | solution.py:369
  132.3 8.2 %collective-permute-done.21 = bf16[64,32,128]{2,1,0:T(8,128)(2,1)S(1)} collective-permute-done((bf16[64,32,128]{2,1,0:T(8,128)(2,1)S(1)}, bf16[64,32,128]{2,1,0:T(8,128)(2,1)S(1)}, u32[]{:S(2)}, u32[]{:S(2)}) %collective-permute-start.21) | collective-permute-done | bytes 524320 | tf_op jit(solution)/shard_map/ppermute | solution.py:310
  148.0 3.6 %all-to-all-start.7 = ((bf16[16,4,32,128]{3,2,1,0:T(8,128)(2,1)}), bf16[16,4,32,128]{3,2,1,0:T(8,128)(2,1)S(1)}, u32[]{:S(2)}, u32[]{:S(2)}) async-start(bf16[16,4,32,128]{3,2,1,0:T(8,128)(2,1)} %get-tuple-element.323), calls=%async_computation.7 | async-start | bytes 1048576 | tf_op jit(solution)/shard_map/all_to_all | solution.py:369
  151.6 8.0 %collective-permute-done.23 = bf16[64,32,128]{2,1,0:T(8,128)(2,1)S(1)} collective-permute-done((bf16[64,32,128]{2,1,0:T(8,128)(2,1)S(1)}, bf16[64,32,128]{2,1,0:T(8,128)(2,1)S(1)}, u32[]{:S(2)}, u32[]{:S(2)}) %collective-permute-start.23) | collective-permute-done | bytes 524320 | tf_op jit(solution)/shard_map/ppermute | solution.py:310
  167.0 3.6 %all-to-all-start.8 = ((bf16[16,4,32,128]{3,2,1,0:T(8,128)(2,1)}), bf16[16,4,32,128]{3,2,1,0:T(8,128)(2,1)S(1)}, u32[]{:S(2)}, u32[]{:S(2)}) async-start(bf16[16,4,32,128]{3,2,1,0:T(8,128)(2,1)} %get-tuple-element.329), calls=%async_computation.8 | async-start | bytes 1048576 | tf_op jit(solution)/shard_map/all_to_all | solution.py:369
  170.6 8.2 %collective-permute-done.25 = bf16[64,32,128]{2,1,0:T(8,128)(2,1)S(1)} collective-permute-done((bf16[64,32,128]{2,1,0:T(8,128)(2,1)S(1)}, bf16[64,32,128]{2,1,0:T(8,128)(2,1)S(1)}, u32[]{:S(2)}, u32[]{:S(2)}) %collective-permute-start.25) | collective-permute-done | bytes 524320 | tf_op jit(solution)/shard_map/ppermute | solution.py:310
  186.7 3.6 %all-to-all-start.9 = ((bf16[16,4,32,128]{3,2,1,0:T(8,128)(2,1)}), bf16[16,4,32,128]{3,2,1,0:T(8,128)(2,1)S(1)}, u32[]{:S(2)}, u32[]{:S(2)}) async-start(bf16[16,4,32,128]{3,2,1,0:T(8,128)(2,1)} %get-tuple-element.335), calls=%async_computation.9 | async-start | bytes 1048576 | tf_op jit(solution)/shard_map/all_to_all | solution.py:369
  190.3 8.1 %collective-permute-done.27 = bf16[64,32,128]{2,1,0:T(8,128)(2,1)S(1)} collective-permute-done((bf16[64,32,128]{2,1,0:T(8,128)(2,1)S(1)}, bf16[64,32,128]{2,1,0:T(8,128)(2,1)S(1)}, u32[]{:S(2)}, u32[]{:S(2)}) %collective-permute-start.27) | collective-permute-done | bytes 524320 | tf_op jit(solution)/shard_map/ppermute | solution.py:310
  205.7 3.6 %all-to-all-start.10 = ((bf16[16,4,32,128]{3,2,1,0:T(8,128)(2,1)}), bf16[16,4,32,128]{3,2,1,0:T(8,128)(2,1)S(1)}, u32[]{:S(2)}, u32[]{:S(2)}) async-start(bf16[16,4,32,128]{3,2,1,0:T(8,128)(2,1)} %get-tuple-element.341), calls=%async_computation.10 | async-start | bytes 1048576 | tf_op jit(solution)/shard_map/all_to_all | solution.py:369
  209.3 9.4 %collective-permute-done.29 = bf16[64,32,128]{2,1,0:T(8,128)(2,1)S(1)} collective-permute-done((bf16[64,32,128]{2,1,0:T(8,128)(2,1)S(1)}, bf16[64,32,128]{2,1,0:T(8,128)(2,1)S(1)}, u32[]{:S(2)}, u32[]{:S(2)}) %collective-permute-start.29) | collective-permute-done | bytes 524320 | tf_op jit(solution)/shard_map/ppermute | solution.py:310
  (121 shorter events, 70.8 us)
Async XLA Ops:
  6.2 18.1 %all-to-all-start = ((bf16[16,4,32,128]{3,2,1,0:T(8,128)(2,1)}), bf16[16,4,32,128]{3,2,1,0:T(8,128)(2,1)S(1)}, u32[]{:S(2)}, u32[]{:S(2)}) async-start(bf16[16,4,32,128]{3,2,1,0:T(8,128)(2,1)} %get-tuple-element.282), calls=%async_computation | async-start | bytes 1048576 | tf_op jit(solution)/shard_map/all_to_all | solution.py:369
  24.3 3.5 %collective-permute-start.10 = (bf16[64,32,128]{2,1,0:T(8,128)(2,1)S(1)}, bf16[64,32,128]{2,1,0:T(8,128)(2,1)S(1)}, u32[]{:S(2)}, u32[]{:S(2)}) collective-permute-start(bf16[64,32,128]{2,1,0:T(8,128)(2,1)S(1)} %bitcast.98), channel_id=1, source_target_pairs={{0,1},{1,0},{2,3},{3,2},{4,5},{5,4},{6,7},{7,6},{8,9},{9,8},{10,11... | collective-permute-start | bytes 1572872 | tf_op jit(solution)/shard_map/ppermute | solution.py:310
  26.5 14.8 %collective-permute-start.11 = (bf16[64,32,128]{2,1,0:T(8,128)(2,1)S(1)}, bf16[64,32,128]{2,1,0:T(8,128)(2,1)S(1)}, u32[]{:S(2)}, u32[]{:S(2)}) collective-permute-start(bf16[64,32,128]{2,1,0:T(8,128)(2,1)S(1)} %bitcast.99), channel_id=1, source_target_pairs={{0,32},{1,33},{2,34},{3,35},{4,36},{5,37},{6,38},{7,39},{8,40},{9,... | collective-permute-start | bytes 1572872 | tf_op jit(solution)/shard_map/ppermute | solution.py:310
  30.7 15.0 %all-to-all-start.1 = ((bf16[16,4,32,128]{3,2,1,0:T(8,128)(2,1)}), bf16[16,4,32,128]{3,2,1,0:T(8,128)(2,1)S(1)}, u32[]{:S(2)}, u32[]{:S(2)}) async-start(bf16[16,4,32,128]{3,2,1,0:T(8,128)(2,1)} %get-tuple-element.287), calls=%async_computation.1 | async-start | bytes 1048576 | tf_op jit(solution)/shard_map/all_to_all | solution.py:369
  45.7 2.6 %collective-permute-start.12 = (bf16[64,32,128]{2,1,0:T(8,128)(2,1)S(1)}, bf16[64,32,128]{2,1,0:T(8,128)(2,1)S(1)}, u32[]{:S(2)}, u32[]{:S(2)}) collective-permute-start(bf16[64,32,128]{2,1,0:T(8,128)(2,1)S(1)} %bitcast.86), channel_id=1, source_target_pairs={{0,1},{1,0},{2,3},{3,2},{4,5},{5,4},{6,7},{7,6},{8,9},{9,8},{10,11... | collective-permute-start | bytes 1572872 | tf_op jit(solution)/shard_map/ppermute | solution.py:310
  46.8 14.8 %collective-permute-start.13 = (bf16[64,32,128]{2,1,0:T(8,128)(2,1)S(1)}, bf16[64,32,128]{2,1,0:T(8,128)(2,1)S(1)}, u32[]{:S(2)}, u32[]{:S(2)}) collective-permute-start(bf16[64,32,128]{2,1,0:T(8,128)(2,1)S(1)} %bitcast.87), channel_id=1, source_target_pairs={{0,32},{1,33},{2,34},{3,35},{4,36},{5,37},{6,38},{7,39},{8,40},{9,... | collective-permute-start | bytes 1572872 | tf_op jit(solution)/shard_map/ppermute | solution.py:310
  50.5 15.0 %all-to-all-start.2 = ((bf16[16,4,32,128]{3,2,1,0:T(8,128)(2,1)}), bf16[16,4,32,128]{3,2,1,0:T(8,128)(2,1)S(1)}, u32[]{:S(2)}, u32[]{:S(2)}) async-start(bf16[16,4,32,128]{3,2,1,0:T(8,128)(2,1)} %get-tuple-element.293), calls=%async_computation.2 | async-start | bytes 1048576 | tf_op jit(solution)/shard_map/all_to_all | solution.py:369
  65.5 2.5 %collective-permute-start.14 = (bf16[64,32,128]{2,1,0:T(8,128)(2,1)S(1)}, bf16[64,32,128]{2,1,0:T(8,128)(2,1)S(1)}, u32[]{:S(2)}, u32[]{:S(2)}) collective-permute-start(bf16[64,32,128]{2,1,0:T(8,128)(2,1)S(1)} %bitcast.90), channel_id=1, source_target_pairs={{0,1},{1,0},{2,3},{3,2},{4,5},{5,4},{6,7},{7,6},{8,9},{9,8},{10,11... | collective-permute-start | bytes 1572872 | tf_op jit(solution)/shard_map/ppermute | solution.py:310
  66.5 14.8 %collective-permute-start.15 = (bf16[64,32,128]{2,1,0:T(8,128)(2,1)S(1)}, bf16[64,32,128]{2,1,0:T(8,128)(2,1)S(1)}, u32[]{:S(2)}, u32[]{:S(2)}) collective-permute-start(bf16[64,32,128]{2,1,0:T(8,128)(2,1)S(1)} %bitcast.91), channel_id=1, source_target_pairs={{0,32},{1,33},{2,34},{3,35},{4,36},{5,37},{6,38},{7,39},{8,40},{9,... | collective-permute-start | bytes 1572872 | tf_op jit(solution)/shard_map/ppermute | solution.py:310
  70.2 15.2 %all-to-all-start.3 = ((bf16[16,4,32,128]{3,2,1,0:T(8,128)(2,1)}), bf16[16,4,32,128]{3,2,1,0:T(8,128)(2,1)S(1)}, u32[]{:S(2)}, u32[]{:S(2)}) async-start(bf16[16,4,32,128]{3,2,1,0:T(8,128)(2,1)} %get-tuple-element.299), calls=%async_computation.3 | async-start | bytes 1048576 | tf_op jit(solution)/shard_map/all_to_all | solution.py:369
  85.4 2.4 %collective-permute-start.16 = (bf16[64,32,128]{2,1,0:T(8,128)(2,1)S(1)}, bf16[64,32,128]{2,1,0:T(8,128)(2,1)S(1)}, u32[]{:S(2)}, u32[]{:S(2)}) collective-permute-start(bf16[64,32,128]{2,1,0:T(8,128)(2,1)S(1)} %bitcast.94), channel_id=1, source_target_pairs={{0,1},{1,0},{2,3},{3,2},{4,5},{5,4},{6,7},{7,6},{8,9},{9,8},{10,11... | collective-permute-start | bytes 1572872 | tf_op jit(solution)/shard_map/ppermute | solution.py:310
  86.3 14.7 %collective-permute-start.17 = (bf16[64,32,128]{2,1,0:T(8,128)(2,1)S(1)}, bf16[64,32,128]{2,1,0:T(8,128)(2,1)S(1)}, u32[]{:S(2)}, u32[]{:S(2)}) collective-permute-start(bf16[64,32,128]{2,1,0:T(8,128)(2,1)S(1)} %bitcast.95), channel_id=1, source_target_pairs={{0,32},{1,33},{2,34},{3,35},{4,36},{5,37},{6,38},{7,39},{8,40},{9,... | collective-permute-start | bytes 1572872 | tf_op jit(solution)/shard_map/ppermute | solution.py:310
  90.0 15.0 %all-to-all-start.4 = ((bf16[16,4,32,128]{3,2,1,0:T(8,128)(2,1)}), bf16[16,4,32,128]{3,2,1,0:T(8,128)(2,1)S(1)}, u32[]{:S(2)}, u32[]{:S(2)}) async-start(bf16[16,4,32,128]{3,2,1,0:T(8,128)(2,1)} %get-tuple-element.305), calls=%async_computation.4 | async-start | bytes 1048576 | tf_op jit(solution)/shard_map/all_to_all | solution.py:369
  105.0 2.6 %collective-permute-start.18 = (bf16[64,32,128]{2,1,0:T(8,128)(2,1)S(1)}, bf16[64,32,128]{2,1,0:T(8,128)(2,1)S(1)}, u32[]{:S(2)}, u32[]{:S(2)}) collective-permute-start(bf16[64,32,128]{2,1,0:T(8,128)(2,1)S(1)} %bitcast.70), channel_id=1, source_target_pairs={{0,1},{1,0},{2,3},{3,2},{4,5},{5,4},{6,7},{7,6},{8,9},{9,8},{10,11... | collective-permute-start | bytes 1572872 | tf_op jit(solution)/shard_map/ppermute | solution.py:310
  106.0 14.8 %collective-permute-start.19 = (bf16[64,32,128]{2,1,0:T(8,128)(2,1)S(1)}, bf16[64,32,128]{2,1,0:T(8,128)(2,1)S(1)}, u32[]{:S(2)}, u32[]{:S(2)}) collective-permute-start(bf16[64,32,128]{2,1,0:T(8,128)(2,1)S(1)} %bitcast.71), channel_id=1, source_target_pairs={{0,32},{1,33},{2,34},{3,35},{4,36},{5,37},{6,38},{7,39},{8,40},{9,... | collective-permute-start | bytes 1572872 | tf_op jit(solution)/shard_map/ppermute | solution.py:310
  109.7 14.3 %all-to-all-start.5 = ((bf16[16,4,32,128]{3,2,1,0:T(8,128)(2,1)}), bf16[16,4,32,128]{3,2,1,0:T(8,128)(2,1)S(1)}, u32[]{:S(2)}, u32[]{:S(2)}) async-start(bf16[16,4,32,128]{3,2,1,0:T(8,128)(2,1)} %get-tuple-element.311), calls=%async_computation.5 | async-start | bytes 1048576 | tf_op jit(solution)/shard_map/all_to_all | solution.py:369
  124.0 3.3 %collective-permute-start.20 = (bf16[64,32,128]{2,1,0:T(8,128)(2,1)S(1)}, bf16[64,32,128]{2,1,0:T(8,128)(2,1)S(1)}, u32[]{:S(2)}, u32[]{:S(2)}) collective-permute-start(bf16[64,32,128]{2,1,0:T(8,128)(2,1)S(1)} %bitcast.74), channel_id=1, source_target_pairs={{0,1},{1,0},{2,3},{3,2},{4,5},{5,4},{6,7},{7,6},{8,9},{9,8},{10,11... | collective-permute-start | bytes 1572872 | tf_op jit(solution)/shard_map/ppermute | solution.py:310
  125.7 14.8 %collective-permute-start.21 = (bf16[64,32,128]{2,1,0:T(8,128)(2,1)S(1)}, bf16[64,32,128]{2,1,0:T(8,128)(2,1)S(1)}, u32[]{:S(2)}, u32[]{:S(2)}) collective-permute-start(bf16[64,32,128]{2,1,0:T(8,128)(2,1)S(1)} %bitcast.75), channel_id=1, source_target_pairs={{0,32},{1,33},{2,34},{3,35},{4,36},{5,37},{6,38},{7,39},{8,40},{9,... | collective-permute-start | bytes 1572872 | tf_op jit(solution)/shard_map/ppermute | solution.py:310
  128.7 14.3 %all-to-all-start.6 = ((bf16[16,4,32,128]{3,2,1,0:T(8,128)(2,1)}), bf16[16,4,32,128]{3,2,1,0:T(8,128)(2,1)S(1)}, u32[]{:S(2)}, u32[]{:S(2)}) async-start(bf16[16,4,32,128]{3,2,1,0:T(8,128)(2,1)} %get-tuple-element.317), calls=%async_computation.6 | async-start | bytes 1048576 | tf_op jit(solution)/shard_map/all_to_all | solution.py:369
  143.0 3.3 %collective-permute-start.22 = (bf16[64,32,128]{2,1,0:T(8,128)(2,1)S(1)}, bf16[64,32,128]{2,1,0:T(8,128)(2,1)S(1)}, u32[]{:S(2)}, u32[]{:S(2)}) collective-permute-start(bf16[64,32,128]{2,1,0:T(8,128)(2,1)S(1)} %bitcast.78), channel_id=1, source_target_pairs={{0,1},{1,0},{2,3},{3,2},{4,5},{5,4},{6,7},{7,6},{8,9},{9,8},{10,11... | collective-permute-start | bytes 1572872 | tf_op jit(solution)/shard_map/ppermute | solution.py:310
  144.8 14.8 %collective-permute-start.23 = (bf16[64,32,128]{2,1,0:T(8,128)(2,1)S(1)}, bf16[64,32,128]{2,1,0:T(8,128)(2,1)S(1)}, u32[]{:S(2)}, u32[]{:S(2)}) collective-permute-start(bf16[64,32,128]{2,1,0:T(8,128)(2,1)S(1)} %bitcast.79), channel_id=1, source_target_pairs={{0,32},{1,33},{2,34},{3,35},{4,36},{5,37},{6,38},{7,39},{8,40},{9,... | collective-permute-start | bytes 1572872 | tf_op jit(solution)/shard_map/ppermute | solution.py:310
  148.0 14.3 %all-to-all-start.7 = ((bf16[16,4,32,128]{3,2,1,0:T(8,128)(2,1)}), bf16[16,4,32,128]{3,2,1,0:T(8,128)(2,1)S(1)}, u32[]{:S(2)}, u32[]{:S(2)}) async-start(bf16[16,4,32,128]{3,2,1,0:T(8,128)(2,1)} %get-tuple-element.323), calls=%async_computation.7 | async-start | bytes 1048576 | tf_op jit(solution)/shard_map/all_to_all | solution.py:369
  162.2 3.3 %collective-permute-start.24 = (bf16[64,32,128]{2,1,0:T(8,128)(2,1)S(1)}, bf16[64,32,128]{2,1,0:T(8,128)(2,1)S(1)}, u32[]{:S(2)}, u32[]{:S(2)}) collective-permute-start(bf16[64,32,128]{2,1,0:T(8,128)(2,1)S(1)} %bitcast.82), channel_id=1, source_target_pairs={{0,1},{1,0},{2,3},{3,2},{4,5},{5,4},{6,7},{7,6},{8,9},{9,8},{10,11... | collective-permute-start | bytes 1572872 | tf_op jit(solution)/shard_map/ppermute | solution.py:310
  164.0 14.8 %collective-permute-start.25 = (bf16[64,32,128]{2,1,0:T(8,128)(2,1)S(1)}, bf16[64,32,128]{2,1,0:T(8,128)(2,1)S(1)}, u32[]{:S(2)}, u32[]{:S(2)}) collective-permute-start(bf16[64,32,128]{2,1,0:T(8,128)(2,1)S(1)} %bitcast.83), channel_id=1, source_target_pairs={{0,32},{1,33},{2,34},{3,35},{4,36},{5,37},{6,38},{7,39},{8,40},{9,... | collective-permute-start | bytes 1572872 | tf_op jit(solution)/shard_map/ppermute | solution.py:310
  167.0 14.3 %all-to-all-start.8 = ((bf16[16,4,32,128]{3,2,1,0:T(8,128)(2,1)}), bf16[16,4,32,128]{3,2,1,0:T(8,128)(2,1)S(1)}, u32[]{:S(2)}, u32[]{:S(2)}) async-start(bf16[16,4,32,128]{3,2,1,0:T(8,128)(2,1)} %get-tuple-element.329), calls=%async_computation.8 | async-start | bytes 1048576 | tf_op jit(solution)/shard_map/all_to_all | solution.py:369
  181.3 3.3 %collective-permute-start.26 = (bf16[64,32,128]{2,1,0:T(8,128)(2,1)S(1)}, bf16[64,32,128]{2,1,0:T(8,128)(2,1)S(1)}, u32[]{:S(2)}, u32[]{:S(2)}) collective-permute-start(bf16[64,32,128]{2,1,0:T(8,128)(2,1)S(1)} %bitcast.63), channel_id=1, source_target_pairs={{0,1},{1,0},{2,3},{3,2},{4,5},{5,4},{6,7},{7,6},{8,9},{9,8},{10,11... | collective-permute-start | bytes 1572872 | tf_op jit(solution)/shard_map/ppermute | solution.py:310
  183.0 15.3 %collective-permute-start.27 = (bf16[64,32,128]{2,1,0:T(8,128)(2,1)S(1)}, bf16[64,32,128]{2,1,0:T(8,128)(2,1)S(1)}, u32[]{:S(2)}, u32[]{:S(2)}) collective-permute-start(bf16[64,32,128]{2,1,0:T(8,128)(2,1)S(1)} %bitcast.64), channel_id=1, source_target_pairs={{0,32},{1,33},{2,34},{3,35},{4,36},{5,37},{6,38},{7,39},{8,40},{9,... | collective-permute-start | bytes 1572872 | tf_op jit(solution)/shard_map/ppermute | solution.py:310
  186.7 15.0 %all-to-all-start.9 = ((bf16[16,4,32,128]{3,2,1,0:T(8,128)(2,1)}), bf16[16,4,32,128]{3,2,1,0:T(8,128)(2,1)S(1)}, u32[]{:S(2)}, u32[]{:S(2)}) async-start(bf16[16,4,32,128]{3,2,1,0:T(8,128)(2,1)} %get-tuple-element.335), calls=%async_computation.9 | async-start | bytes 1048576 | tf_op jit(solution)/shard_map/all_to_all | solution.py:369
  201.6 2.6 %collective-permute-start.28 = (bf16[64,32,128]{2,1,0:T(8,128)(2,1)S(1)}, bf16[64,32,128]{2,1,0:T(8,128)(2,1)S(1)}, u32[]{:S(2)}, u32[]{:S(2)}) collective-permute-start(bf16[64,32,128]{2,1,0:T(8,128)(2,1)S(1)} %bitcast.59), channel_id=1, source_target_pairs={{0,1},{1,0},{2,3},{3,2},{4,5},{5,4},{6,7},{7,6},{8,9},{9,8},{10,11... | collective-permute-start | bytes 1572872 | tf_op jit(solution)/shard_map/ppermute | solution.py:310
  202.7 16.0 %collective-permute-start.29 = (bf16[64,32,128]{2,1,0:T(8,128)(2,1)S(1)}, bf16[64,32,128]{2,1,0:T(8,128)(2,1)S(1)}, u32[]{:S(2)}, u32[]{:S(2)}) collective-permute-start(bf16[64,32,128]{2,1,0:T(8,128)(2,1)S(1)} %bitcast.60), channel_id=1, source_target_pairs={{0,32},{1,33},{2,34},{3,35},{4,36},{5,37},{6,38},{7,39},{8,40},{9,... | collective-permute-start | bytes 1572872 | tf_op jit(solution)/shard_map/ppermute | solution.py:310
  205.7 14.3 %all-to-all-start.10 = ((bf16[16,4,32,128]{3,2,1,0:T(8,128)(2,1)}), bf16[16,4,32,128]{3,2,1,0:T(8,128)(2,1)S(1)}, u32[]{:S(2)}, u32[]{:S(2)}) async-start(bf16[16,4,32,128]{3,2,1,0:T(8,128)(2,1)} %get-tuple-element.341), calls=%async_computation.10 | async-start | bytes 1048576 | tf_op jit(solution)/shard_map/all_to_all | solution.py:369
  220.0 3.3 %collective-permute-start.30 = (bf16[64,32,128]{2,1,0:T(8,128)(2,1)S(1)}, bf16[64,32,128]{2,1,0:T(8,128)(2,1)S(1)}, u32[]{:S(2)}, u32[]{:S(2)}) collective-permute-start(bf16[64,32,128]{2,1,0:T(8,128)(2,1)S(1)} %bitcast.67), channel_id=1, source_target_pairs={{0,1},{1,0},{2,3},{3,2},{4,5},{5,4},{6,7},{7,6},{8,9},{9,8},{10,11... | collective-permute-start | bytes 1572872 | tf_op jit(solution)/shard_map/ppermute | solution.py:310
  (14 other events, 56.0 us)
